TPU v7x, 256 devices: a whole 4x4x8 slice. The times are simulated.
256 devices in a mesh: dp: 8 (over z), segment: 4 (over y), tm: 8 (over x, core).
Axes of the slice: x: 4, y: 4, z: 8, core: 2. Of those that a mesh axis runs over, the one named last changes fastest.
Arguments:
- latents: bfloat16 [16, 16, 4, 64], P('dp', 'tm'), may hold values from -6 to 6
- timesteps: int32 [16], P('dp'), may hold values from 0 to 999
- seeds: int32 [16], P('dp'), may hold values from 0 to 1073741823
- in_weight: bfloat16 [4, 320], replicated, may hold values from -3 to 3
- out_weight: bfloat16 [320, 4], replicated, may hold values from -0.3125 to 0.3125
- down_weight: bfloat16 [4, 3, 320, 320], P('segment'), may hold values from -0.1875 to 0.1875
- up_weight: bfloat16 [4, 3, 640, 320], P('segment'), may hold values from -0.125 to 0.125
- skip_weight: bfloat16 [4, 640, 320], P('segment'), may hold values from -0.25 to 0.25
Outputs:
- grad_down: float32 [4, 3, 320, 320], P('segment', None, ('dp', 'tm'))
- grad_up: float32 [4, 3, 640, 320], P('segment', None, ('dp', 'tm'))
- grad_skip: float32 [4, 640, 320], P('segment', ('dp', 'tm'))
All inputs are finite; a program needn't handle non-finite values.
Results may differ from a plain program's by a relative error of at most 0.0035.
Values may be sent and summed in bfloat16 or wider, within the bound.
No kernel may reach another device: no remote copies, remote signals or barrier semaphores. Data moves between devices by JAX's collectives and lax.ppermute only.
A program may use at most 128 MiB of HBM per device.

v0:
```python
import math

import jax
import jax.numpy as jnp
from jax import lax
from jax.sharding import PartitionSpec as P

GROUPS = 32


def extended(array, sides, width):
    for axis, dim in sides:
        count, length = (lax.axis_size(axis), array.shape[dim])
        up = [(i, (i + 1) % count) for i in range(count - 1)]
        down = [(j, i) for i, j in up]
        last = lax.slice_in_dim(array, length - width, length, axis=dim)
        first = lax.slice_in_dim(array, 0, width, axis=dim)
        before = lax.ppermute(last, axis, up)
        after = lax.ppermute(first, axis, down)
        array = jnp.concatenate([before, array, after], axis=dim)
    return array


def from_behind(value, axis, steps):
    count = lax.axis_size(axis)
    first, last = (max(0, -steps), min(count, count - steps))
    return lax.ppermute(value, axis, [(source, source + steps) for source in range(first, last)])


def mix_bits(value):
    value = value ^ lax.shift_right_logical(value, jnp.int32(16))
    value = value * -2048144789
    value = value ^ lax.shift_right_logical(value, jnp.int32(13))
    value = value * -1028477387
    value = value ^ lax.shift_right_logical(value, jnp.int32(16))
    return value


def noise_field(seed_value, frame_start, frame_count, lat_dim, pix_dim):
    frame_ids = frame_start + jnp.arange(frame_count, dtype=jnp.int32)
    lat_ids = jnp.arange(lat_dim, dtype=jnp.int32)
    pix_ids = jnp.arange(pix_dim, dtype=jnp.int32)
    index = (frame_ids[:, None, None] * lat_dim + lat_ids[None, :, None]) * pix_dim + pix_ids[
        None, None, :
    ]
    salted = seed_value * -1640531535
    first = mix_bits(index * 2 + salted)
    second = mix_bits(index * 2 + 1 + salted)
    unit_a = (lax.shift_right_logical(first, jnp.int32(8)).astype(jnp.float32) + 0.5) / 16777216.0
    unit_b = (lax.shift_right_logical(second, jnp.int32(8)).astype(jnp.float32) + 0.5) / 16777216.0
    return jnp.sqrt(-2.0 * jnp.log(unit_a)) * jnp.cos(2.0 * math.pi * unit_b)


def plan(step_value):
    theta = step_value.astype(jnp.float32) * (0.5 * math.pi / 1000.0)
    return (jnp.cos(theta), jnp.sin(theta))


def time_embedding(step_value, channels):
    half = channels // 2
    frequency = jnp.exp(-math.log(10000.0) * jnp.arange(half, dtype=jnp.float32) / half)
    phase = step_value.astype(jnp.float32) * frequency
    return jnp.concatenate([jnp.sin(phase), jnp.cos(phase)])


def project_in(noisy, in_weight):
    frames, lat_dim, pix_dim = noisy.shape
    flat = jnp.transpose(noisy, (0, 2, 1)).reshape(frames * pix_dim, lat_dim)
    result = jnp.dot(flat, in_weight, preferred_element_type=jnp.float32)
    return result.reshape(frames, pix_dim, -1).astype(jnp.bfloat16)


def group_norm(values, groups):
    frames, pixels, channels = values.shape
    grouped = values.reshape(frames, pixels, groups, channels // groups)
    center = jnp.mean(grouped, axis=(1, 3), keepdims=True)
    spread = jnp.mean((grouped - center) ** 2, axis=(1, 3), keepdims=True)
    return ((grouped - center) * lax.rsqrt(spread + 1e-05)).reshape(frames, pixels, channels)


def act_down(values, embedding):
    return jax.nn.silu(group_norm(values, GROUPS) + embedding)


def act_up(values):
    return jax.nn.silu(group_norm(values, GROUPS))


def stack_taps(padded):
    frames = padded.shape[0] - 2
    stacked = jnp.concatenate([padded[tap : tap + frames] for tap in range(3)], axis=-1)
    return stacked.reshape(frames * padded.shape[1], 3 * padded.shape[2])


def conv_fwd(padded, weight):
    frames = padded.shape[0] - 2
    result = jnp.dot(
        stack_taps(padded),
        weight.reshape(3 * weight.shape[1], weight.shape[2]),
        preferred_element_type=jnp.float32,
    )
    return result.reshape(frames, padded.shape[1], weight.shape[2])


def conv_back(grad_out, weight):
    frames, pixels, cout = grad_out.shape
    cin = weight.shape[1]
    parts = lax.dot_general(
        grad_out.reshape(frames * pixels, cout),
        weight.reshape(3 * cin, cout),
        (((1,), (1,)), ((), ())),
        preferred_element_type=jnp.float32,
    )
    parts = parts.reshape(frames, pixels, 3, cin)
    result = jnp.zeros((frames + 2, pixels, cin), jnp.float32)
    for tap in range(3):
        result = result.at[tap : tap + frames].add(parts[:, :, tap])
    return result


def conv_wgrad(padded, grad_out):
    cout = grad_out.shape[2]
    result = lax.dot_general(
        stack_taps(padded),
        grad_out.reshape(-1, cout),
        (((0,), (0,)), ((), ())),
        preferred_element_type=jnp.float32,
    )
    return result.reshape(3, padded.shape[2], cout)


def flat_wgrad(joined, grad_out):
    return lax.dot_general(
        joined.reshape(-1, joined.shape[2]),
        grad_out.reshape(-1, grad_out.shape[2]),
        (((0,), (0,)), ((), ())),
        preferred_element_type=jnp.float32,
    )


def pick_row(store, slot):
    return lax.dynamic_index_in_dim(store, slot, 0, keepdims=False)


def store_row(store, slot, value, active):
    previous = pick_row(store, slot)
    return lax.dynamic_update_index_in_dim(store, jnp.where(active, value, previous), slot, 0)


def local(latents, timesteps, seeds, in_weight, out_weight, down_weight, up_weight, skip_weight):
    segments = lax.axis_size("segment")
    segment_index = lax.axis_index("segment")
    batch_local, frames, lat_dim, pix_dim = latents.shape
    channels = in_weight.shape[1]
    w_down = down_weight[0]
    w_up = up_weight[0]
    w_skip = skip_weight[0]
    elements = batch_local * lax.axis_size("dp") * frames * lax.axis_size("tm") * lat_dim * pix_dim
    loss_scale = 64.0 / math.sqrt(elements)
    frame_start = lax.axis_index("tm") * frames
    noise = jax.vmap(
        lambda seed_value: noise_field(seed_value, frame_start, frames, lat_dim, pix_dim)
    )(seeds)
    coef_a, coef_s = plan(timesteps)
    noisy = (
        coef_a[:, None, None, None] * latents.astype(jnp.float32)
        + coef_s[:, None, None, None] * noise
    ).astype(jnp.bfloat16)
    fresh = jax.vmap(lambda clip: project_in(clip, in_weight))(noisy)
    embeds = jax.vmap(lambda step_value: time_embedding(step_value, channels))(timesteps)
    target = jnp.transpose(noise, (0, 1, 3, 2))
    out_wide = out_weight.astype(jnp.float32).T
    last = batch_local + segments - 1
    feature = jnp.zeros((frames, pix_dim, channels), jnp.bfloat16)
    state = {
        "down_mail": feature,
        "up_mail": feature,
        "upc_mail": feature,
        "downc_mail": feature,
        "inputs": jnp.zeros((batch_local, frames, pix_dim, channels), jnp.bfloat16),
        "down_pad": jnp.zeros((batch_local, frames + 2, pix_dim, channels), jnp.bfloat16),
        "skips": jnp.zeros((batch_local, frames, pix_dim, channels), jnp.bfloat16),
        "joined": jnp.zeros((batch_local, frames, pix_dim, 2 * channels), jnp.bfloat16),
        "up_pad": jnp.zeros((batch_local, frames + 2, pix_dim, 2 * channels), jnp.bfloat16),
        "grad_top": jnp.zeros((batch_local, frames, pix_dim, channels), jnp.bfloat16),
        "grad_skips": jnp.zeros((batch_local, frames, pix_dim, channels), jnp.bfloat16),
        "grad_bottom": jnp.zeros((batch_local, frames, pix_dim, channels), jnp.bfloat16),
        "acc_down": jnp.zeros((3, channels, channels), jnp.float32),
        "acc_up": jnp.zeros((3, 2 * channels, channels), jnp.float32),
        "acc_skip": jnp.zeros((2 * channels, channels), jnp.float32),
    }

    def slot_of(micro):
        active = (micro >= 0) & (micro < batch_local)
        return (active, jnp.clip(micro, 0, batch_local - 1))

    def down_forward(moment):
        active, slot = slot_of(moment - segment_index)
        inputs = jnp.where(segment_index == 0, pick_row(fresh, slot), state["down_mail"])
        activated = act_down(inputs.astype(jnp.float32), pick_row(embeds, slot)).astype(
            jnp.bfloat16
        )
        padded = extended(activated, (("tm", 0),), 1)
        result = lax.cond(
            active,
            lambda: (inputs.astype(jnp.float32) + conv_fwd(padded, w_down)).astype(jnp.bfloat16),
            lambda: jnp.zeros_like(inputs),
        )
        state["inputs"] = store_row(state["inputs"], slot, inputs, active)
        state["down_pad"] = store_row(state["down_pad"], slot, padded, active)
        state["skips"] = store_row(state["skips"], slot, result, active)
        return result

    def up_forward(moment):
        active, slot = slot_of(moment - (segments - 1 - segment_index))
        skip_value = pick_row(state["skips"], slot)
        below = jnp.where(segment_index == segments - 1, skip_value, state["up_mail"])
        joined = jnp.concatenate([below, skip_value], axis=-1)
        activated = act_up(joined.astype(jnp.float32)).astype(jnp.bfloat16)
        padded = extended(activated, (("tm", 0),), 1)

        def compute():
            shortcut = jnp.dot(
                joined.reshape(-1, 2 * channels), w_skip, preferred_element_type=jnp.float32
            ).reshape(frames, pix_dim, channels)
            return (conv_fwd(padded, w_up) + shortcut).astype(jnp.bfloat16)

        result = lax.cond(active, compute, lambda: jnp.zeros_like(below))
        state["joined"] = store_row(state["joined"], slot, joined, active)
        state["up_pad"] = store_row(state["up_pad"], slot, padded, active)
        predicted = jnp.dot(
            result.reshape(-1, channels), out_weight, preferred_element_type=jnp.float32
        ).reshape(frames, pix_dim, lat_dim)
        errors = predicted - pick_row(target, slot)
        at_top = active & (segment_index == 0)
        cotangent = jnp.dot(
            (errors * loss_scale).reshape(-1, lat_dim),
            out_wide,
            preferred_element_type=jnp.float32,
            precision=lax.Precision.HIGHEST,
        )
        cotangent = cotangent.reshape(frames, pix_dim, channels).astype(jnp.bfloat16)
        state["grad_top"] = store_row(state["grad_top"], slot, cotangent, at_top)
        return result

    def add_rims(grad_padded, neighbours):
        interior = grad_padded[1:-1]
        interior = interior.at[0].add(neighbours[0])
        return interior.at[-1].add(neighbours[-1])

    def up_backward(moment):
        active, slot = slot_of(moment - segment_index)
        grad_out = jnp.where(
            segment_index == 0, pick_row(state["grad_top"], slot), state["upc_mail"]
        )
        padded = pick_row(state["up_pad"], slot)
        joined = pick_row(state["joined"], slot)
        acc_up = state["acc_up"]
        acc_skip = state["acc_skip"]

        def compute():
            through = lax.dot_general(
                grad_out.reshape(-1, channels),
                w_skip,
                (((1,), (1,)), ((), ())),
                preferred_element_type=jnp.float32,
            )
            return (
                conv_back(grad_out, w_up),
                acc_up + conv_wgrad(padded, grad_out),
                acc_skip + flat_wgrad(joined, grad_out),
                through.reshape(frames, pix_dim, 2 * channels),
            )

        def resting():
            return (
                jnp.zeros((frames + 2, pix_dim, 2 * channels), jnp.float32),
                acc_up,
                acc_skip,
                jnp.zeros((frames, pix_dim, 2 * channels), jnp.float32),
            )

        grad_padded, state["acc_up"], state["acc_skip"], through = lax.cond(
            active, compute, resting
        )
        boundary = jnp.stack([grad_padded[0], grad_padded[-1]])
        neighbours = extended(boundary.astype(jnp.bfloat16), (("tm", 0),), 1).astype(boundary.dtype)
        interior = add_rims(grad_padded, neighbours)
        norm_grad = jax.vjp(act_up, joined.astype(jnp.float32))[1](interior)[0]
        grad_joined = (norm_grad + through).astype(jnp.bfloat16)
        lower = grad_joined[..., :channels]
        state["grad_skips"] = store_row(
            state["grad_skips"], slot, grad_joined[..., channels:], active
        )
        state["grad_bottom"] = store_row(
            state["grad_bottom"], slot, lower, active & (segment_index == segments - 1)
        )
        return lower

    def down_backward(moment):
        active, slot = slot_of(moment - (segments - 1 - segment_index))
        arriving = jnp.where(
            segment_index == segments - 1, pick_row(state["grad_bottom"], slot), state["downc_mail"]
        )
        grad_out = (
            pick_row(state["grad_skips"], slot).astype(jnp.float32) + arriving.astype(jnp.float32)
        ).astype(jnp.bfloat16)
        padded = pick_row(state["down_pad"], slot)
        inputs = pick_row(state["inputs"], slot)
        embedding = pick_row(embeds, slot)
        acc_down = state["acc_down"]
        grad_padded, state["acc_down"] = lax.cond(
            active,
            lambda: (conv_back(grad_out, w_down), acc_down + conv_wgrad(padded, grad_out)),
            lambda: (jnp.zeros((frames + 2, pix_dim, channels), jnp.float32), acc_down),
        )
        boundary = jnp.stack([grad_padded[0], grad_padded[-1]])
        neighbours = extended(boundary.astype(jnp.bfloat16), (("tm", 0),), 1).astype(boundary.dtype)
        interior = add_rims(grad_padded, neighbours)
        norm_grad = jax.vjp(lambda values: act_down(values, embedding), inputs.astype(jnp.float32))[
            1
        ](interior)[0]
        return (grad_out.astype(jnp.float32) + norm_grad).astype(jnp.bfloat16)

    timeline = [(moment, None) for moment in range(last)] + [
        (None, moment) for moment in range(last)
    ]
    for first_tick, second_tick in timeline:
        if first_tick is not None:
            sent_down = down_forward(first_tick)
        if second_tick is not None:
            sent_up = up_forward(second_tick)
        if first_tick is not None:
            state["down_mail"] = from_behind(sent_down, "segment", 1)
        if second_tick is not None:
            state["up_mail"] = from_behind(sent_up, "segment", -1)
    for first_tick, second_tick in timeline:
        if first_tick is not None:
            sent_back_up = up_backward(first_tick)
        if second_tick is not None:
            sent_back_down = down_backward(second_tick)
        if first_tick is not None:
            state["upc_mail"] = from_behind(sent_back_up, "segment", 1)
        if second_tick is not None:
            state["downc_mail"] = from_behind(sent_back_down, "segment", -1)
    total_down, total_up, total_skip = (
        lax.psum_scatter(state["acc_down"], ("dp", "tm"), scatter_dimension=1, tiled=True),
        lax.psum_scatter(state["acc_up"], ("dp", "tm"), scatter_dimension=1, tiled=True),
        lax.psum_scatter(state["acc_skip"], ("dp", "tm"), scatter_dimension=0, tiled=True),
    )
    return (total_down[None], total_up[None], total_skip[None])


def solution(mesh):
    return jax.shard_map(
        local,
        mesh=mesh,
        in_specs=(
            P("dp", "tm", None, None),
            P("dp"),
            P("dp"),
            P(),
            P(),
            P("segment", None, None, None),
            P("segment", None, None, None),
            P("segment", None, None),
        ),
        out_specs=(
            P("segment", None, ("dp", "tm"), None),
            P("segment", None, ("dp", "tm"), None),
            P("segment", ("dp", "tm"), None),
        ),
        check_vma=False,
    )
```

profile of v0, /device:TPU:1, one launch (start us, length us, event | category | flops | bytes accessed | tf_op | source)
XLA Modules:
  0.0 825.6 jit_solution(6932792046711864825)
XLA Ops:
  12.6 4.5 collective-permute-start
  28.6 3.1 collective-permute-start.3
  33.7 3.4 collective-permute-done.4
  37.5 4.1 collective-permute-start.5
  49.1 3.4 collective-permute-done.7
  52.6 4.4 collective-permute-start.8
  64.6 3.4 collective-permute-done.10
  68.1 4.0 collective-permute-start.11
  87.2 3.4 collective-permute-start.14
  92.9 3.5 collective-permute-done.15
  157.6 4.4 collective-permute-start.20
  175.5 16.0 %collective-permute-done.22 = bf16[2,64,320]{2,1,0:T(8,128)(2,1)S(1)} collective-permute-done((bf16[2,64,320]{2,1,0:T(8,128)(2,1)S(1)}, bf16[2,64,320]{2,1,0:T(8,128)(2,1)S(1)}, u32[]{:S(2)}, u32[]{:S(2)}) %collective-permute-start.22) | collective-permute-done | bytes 81952 | tf_op jit(solution)/shard_map/ppermute | solution.py:27
  209.6 5.3 collective-permute-start.23
  223.4 6.2 conditional.28
  258.0 4.5 collective-permute-start.26
  297.6 6.2 conditional.29
  307.1 13.3 %conditional.30 = (f32[4,64,640]{2,1,0:T(8,128)}, f32[3,640,320]{1,2,0:T(8,128)}, f32[640,320]{0,1:T(8,128)}, f32[2,64,640]{2,1,0:T(8,128)}) conditional(s32[]{:T(128)} %convert_element_type.567, () %tuple.368, (bf16[2,2,64,320]{3,2,1,0:T(8,128)(2,1)S(1)}, s32[]{:T(128)}, pred[2,64,320]{2,1,0:T(8,128)(4,1)S(1)}, ...), branch_computations={%region_50.51_spmd, %region_51.52_spmd} | conditional | flops 421109760 | bytes 15360160 | solution.py:283
  321.6 3.8 collective-permute-start.28
  351.6 15.9 %conditional.31 = (f32[4,64,640]{2,1,0:T(8,128)}, f32[3,640,320]{1,2,0:T(8,128)}, f32[640,320]{0,1:T(8,128)}, f32[2,64,640]{2,1,0:T(8,128)}) conditional(s32[]{:T(128)} %convert_element_type.577, (f32[3,640,320]{1,2,0:T(8,128)}, f32[640,320]{0,1:T(8,128)}) %tuple.390, (bf16[2,2,64,320]{3,2,1,0:T(8,128)(2,1)}, s32[]{:T(128)}, ...), branch_computations={%region_62.63_spmd, %region_63.64_spmd} | conditional | flops 421928960 | bytes 17981544 | solution.py:283
  360.3 3.9 convolution_add_fusion.10
  368.7 4.3 collective-permute-start.31
  391.3 4.0 collective-permute-start.33
  400.4 3.6 collective-permute-start.34
  422.2 18.2 %collective-permute-start.36 = (bf16[2,64,320]{2,1,0:T(8,128)(2,1)S(1)}, bf16[2,64,320]{2,1,0:T(8,128)(2,1)S(1)}, u32[]{:S(2)}, u32[]{:S(2)}) collective-permute-start(bf16[2,64,320]{2,1,0:T(8,128)(2,1)S(1)} %slice.1841), channel_id=1, source_target_pairs={{0,8},{8,16},{16,24},{1,9},{9,17},{17,25},{2,10},{10,18},{18,26},{... | collective-permute-start | bytes 245768 | tf_op jit(solution)/shard_map/ppermute | solution.py:27
  466.7 3.9 collective-permute-start.39
  499.9 16.5 %collective-permute-done.44 = bf16[2,64,320]{2,1,0:T(8,128)(2,1)S(1)} collective-permute-done((bf16[2,64,320]{2,1,0:T(8,128)(2,1)S(1)}, bf16[2,64,320]{2,1,0:T(8,128)(2,1)S(1)}, u32[]{:S(2)}, u32[]{:S(2)}) %collective-permute-start.44) | collective-permute-done | bytes 81952 | tf_op jit(solution)/shard_map/ppermute | solution.py:27
  518.3 3.2 collective-permute-start.45
  532.3 4.4 collective-permute-done.47
  552.2 31.4 %collective-permute-done.50 = bf16[2,64,320]{2,1,0:T(8,128)(2,1)S(1)} collective-permute-done((bf16[2,64,320]{2,1,0:T(8,128)(2,1)S(1)}, bf16[2,64,320]{2,1,0:T(8,128)(2,1)S(1)}, u32[]{:S(2)}, u32[]{:S(2)}) %collective-permute-start.50) | collective-permute-done | bytes 81952 | tf_op jit(solution)/shard_map/ppermute | solution.py:27
  583.6 5.2 conditional.38
  601.6 5.5 copy.378
  615.2 198.9 %all-reduce.15.cloned.1.call-done = (f32[3,320,320]{2,0,1:T(4,128)}, f32[3,640,320]{2,0,1:T(4,128)}, f32[640,320]{1,0:T(8,128)}) async-done(((f32[3,320,320]{2,0,1:T(4,128)}, f32[3,640,320]{2,0,1:T(4,128)}, f32[640,320]{1,0:T(8,128)}), (f32[3,320,320]{2,0,1:T(4,128)}, f32[3,640,320]{2,0,1:T(4,128)}, f32[640,320]{1,0:T(8,128)})) %all-reduce.15.cloned.1.call-update) | async-done | bytes 4505616
  (883 shorter events, 445.2 us)
Async XLA Ops:
  7.2 806.8 %all-reduce.15.cloned.1.call-start = ((), (), s32[]{:S(2)}) async-start(), calls=%async_computation | async-start | bytes 13762560
  12.6 7.5 collective-permute-start
  52.6 6.1 collective-permute-start.8
  74.9 7.9 collective-permute-start.12
  97.3 6.2 collective-permute-start.16
  121.5 9.7 %collective-permute-start.17 = (bf16[1,64,640]{2,1,0:T(8,128)(2,1)}, bf16[1,64,640]{2,1,0:T(8,128)(2,1)}, u32[]{:S(2)}, u32[]{:S(2)}) collective-permute-start(bf16[1,64,640]{2,1,0:T(8,128)(2,1)} %get-tuple-element.1636), channel_id=1, source_target_pairs={{0,1},{1,2},{2,3},{3,4},{4,5},{5,6},{6,7},{8,9},{9,10},{10,11},{11... | collective-permute-start | bytes 245768 | tf_op jit(solution)/shard_map/ppermute | solution.py:18
  124.2 7.0 collective-permute-start.18
  133.1 6.5 collective-permute-start.19
  157.6 11.1 %collective-permute-start.20 = (bf16[1,64,640]{2,1,0:T(8,128)(2,1)}, bf16[1,64,640]{2,1,0:T(8,128)(2,1)}, u32[]{:S(2)}, u32[]{:S(2)}) collective-permute-start(bf16[1,64,640]{2,1,0:T(8,128)(2,1)} %get-tuple-element.1634), channel_id=1, source_target_pairs={{0,1},{1,2},{2,3},{3,4},{4,5},{5,6},{6,7},{8,9},{9,10},{10,11},{11... | collective-permute-start | bytes 245768 | tf_op jit(solution)/shard_map/ppermute | solution.py:18
  162.0 6.7 collective-permute-start.21
  170.5 21.0 %collective-permute-start.22 = (bf16[2,64,320]{2,1,0:T(8,128)(2,1)S(1)}, bf16[2,64,320]{2,1,0:T(8,128)(2,1)S(1)}, u32[]{:S(2)}, u32[]{:S(2)}) collective-permute-start(bf16[2,64,320]{2,1,0:T(8,128)(2,1)S(1)} %get-tuple-element.1724), channel_id=1, source_target_pairs={{8,0},{16,8},{24,16},{9,1},{17,9},{25,17},{10,2},{18,10},{26,18},{... | collective-permute-start | bytes 245768 | tf_op jit(solution)/shard_map/ppermute | solution.py:27
  209.6 12.0 %collective-permute-start.23 = (bf16[1,64,640]{2,1,0:T(8,128)(2,1)}, bf16[1,64,640]{2,1,0:T(8,128)(2,1)}, u32[]{:S(2)}, u32[]{:S(2)}) collective-permute-start(bf16[1,64,640]{2,1,0:T(8,128)(2,1)} %get-tuple-element.1632), channel_id=1, source_target_pairs={{0,1},{1,2},{2,3},{3,4},{4,5},{5,6},{6,7},{8,9},{9,10},{10,11},{11... | collective-permute-start | bytes 245768 | tf_op jit(solution)/shard_map/ppermute | solution.py:18
  214.9 6.7 collective-permute-start.24
  229.6 5.8 collective-permute-start.25
  258.0 37.8 %collective-permute-start.26 = (bf16[1,64,640]{2,1,0:T(8,128)(2,1)}, bf16[1,64,640]{2,1,0:T(8,128)(2,1)}, u32[]{:S(2)}, u32[]{:S(2)}) collective-permute-start(bf16[1,64,640]{2,1,0:T(8,128)(2,1)} %get-tuple-element.1630), channel_id=1, source_target_pairs={{0,1},{1,2},{2,3},{3,4},{4,5},{5,6},{6,7},{8,9},{9,10},{10,11},{11... | collective-permute-start | bytes 245768 | tf_op jit(solution)/shard_map/ppermute | solution.py:18
  262.6 33.3 %collective-permute-start.27 = (bf16[1,64,640]{2,1,0:T(8,128)(2,1)}, bf16[1,64,640]{2,1,0:T(8,128)(2,1)}, u32[]{:S(2)}, u32[]{:S(2)}) collective-permute-start(bf16[1,64,640]{2,1,0:T(8,128)(2,1)} %get-tuple-element.1631), channel_id=1, source_target_pairs={{1,0},{2,1},{3,2},{4,3},{5,4},{6,5},{7,6},{9,8},{10,9},{11,10},{12... | collective-permute-start | bytes 245768 | tf_op jit(solution)/shard_map/ppermute | solution.py:19
  321.6 21.4 %collective-permute-start.28 = (bf16[1,64,640]{2,1,0:T(8,128)(2,1)S(1)}, bf16[1,64,640]{2,1,0:T(8,128)(2,1)}, u32[]{:S(2)}, u32[]{:S(2)}) collective-permute-start(bf16[1,64,640]{2,1,0:T(8,128)(2,1)S(1)} %get-tuple-element.1612), channel_id=1, source_target_pairs={{0,1},{1,2},{2,3},{3,4},{4,5},{5,6},{6,7},{8,9},{9,10},{10,11},{11... | collective-permute-start | bytes 245768 | tf_op jit(solution)/shard_map/ppermute | solution.py:18
  325.3 17.6 %collective-permute-start.29 = (bf16[1,64,640]{2,1,0:T(8,128)(2,1)S(1)}, bf16[1,64,640]{2,1,0:T(8,128)(2,1)}, u32[]{:S(2)}, u32[]{:S(2)}) collective-permute-start(bf16[1,64,640]{2,1,0:T(8,128)(2,1)S(1)} %get-tuple-element.1613), channel_id=1, source_target_pairs={{1,0},{2,1},{3,2},{4,3},{5,4},{6,5},{7,6},{9,8},{10,9},{11,10},{12... | collective-permute-start | bytes 245768 | tf_op jit(solution)/shard_map/ppermute | solution.py:19
  368.7 8.8 %collective-permute-start.31 = (bf16[1,64,640]{2,1,0:T(8,128)(2,1)S(1)}, bf16[1,64,640]{2,1,0:T(8,128)(2,1)S(1)}, u32[]{:S(2)}, u32[]{:S(2)}) collective-permute-start(bf16[1,64,640]{2,1,0:T(8,128)(2,1)S(1)} %get-tuple-element.1610), channel_id=1, source_target_pairs={{0,1},{1,2},{2,3},{3,4},{4,5},{5,6},{6,7},{8,9},{9,10},{10,11},{11... | collective-permute-start | bytes 245768 | tf_op jit(solution)/shard_map/ppermute | solution.py:18
  391.3 6.3 collective-permute-start.33
  400.4 8.1 collective-permute-start.34
  422.2 20.5 %collective-permute-start.36 = (bf16[2,64,320]{2,1,0:T(8,128)(2,1)S(1)}, bf16[2,64,320]{2,1,0:T(8,128)(2,1)S(1)}, u32[]{:S(2)}, u32[]{:S(2)}) collective-permute-start(bf16[2,64,320]{2,1,0:T(8,128)(2,1)S(1)} %slice.1841), channel_id=1, source_target_pairs={{0,8},{8,16},{16,24},{1,9},{9,17},{17,25},{2,10},{10,18},{18,26},{... | collective-permute-start | bytes 245768 | tf_op jit(solution)/shard_map/ppermute | solution.py:27
  445.6 7.5 collective-permute-start.37
  466.7 6.2 collective-permute-start.39
  473.8 5.9 collective-permute-start.40
  498.4 18.0 %collective-permute-start.44 = (bf16[2,64,320]{2,1,0:T(8,128)(2,1)S(1)}, bf16[2,64,320]{2,1,0:T(8,128)(2,1)S(1)}, u32[]{:S(2)}, u32[]{:S(2)}) collective-permute-start(bf16[2,64,320]{2,1,0:T(8,128)(2,1)S(1)} %fusion.300), channel_id=1, source_target_pairs={{8,0},{16,8},{24,16},{9,1},{17,9},{25,17},{10,2},{18,10},{26,18},{... | collective-permute-start | bytes 245768 | tf_op jit(solution)/shard_map/ppermute | solution.py:27
  518.3 6.3 collective-permute-start.45
  530.8 5.9 collective-permute-start.47
  538.7 5.8 collective-permute-start.48
  550.7 32.9 %collective-permute-start.50 = (bf16[2,64,320]{2,1,0:T(8,128)(2,1)S(1)}, bf16[2,64,320]{2,1,0:T(8,128)(2,1)S(1)}, u32[]{:S(2)}, u32[]{:S(2)}) collective-permute-start(bf16[2,64,320]{2,1,0:T(8,128)(2,1)S(1)} %fusion.330), channel_id=1, source_target_pairs={{8,0},{16,8},{24,16},{9,1},{17,9},{25,17},{10,2},{18,10},{26,18},{... | collective-permute-start | bytes 245768 | tf_op jit(solution)/shard_map/ppermute | solution.py:27
  589.9 6.1 collective-permute-start.51
  600.3 9.2 %collective-permute-start.53 = (bf16[2,64,320]{2,1,0:T(8,128)(2,1)S(1)}, bf16[2,64,320]{2,1,0:T(8,128)(2,1)S(1)}, u32[]{:S(2)}, u32[]{:S(2)}) collective-permute-start(bf16[2,64,320]{2,1,0:T(8,128)(2,1)S(1)} %fusion.345), channel_id=1, source_target_pairs={{8,0},{16,8},{24,16},{9,1},{17,9},{25,17},{10,2},{18,10},{26,18},{... | collective-permute-start | bytes 245768 | tf_op jit(solution)/shard_map/ppermute | solution.py:27
  (99 other events, 1014.2 us)
Sparse Core Ops, SparseCore 0:
  612.8 201.2 all-reduce.14
where the time goes:
time: 841 us; the launch traced here: 826 us
  waiting for transfers between devices  311 us (37%)
  other arithmetic  161 us (19%)
  starting transfers between devices  156 us (19%)
  local copies, waits for them, and re-layouts  150 us (18%)
  matrix products  26.8 us (3%)
  between operations  18.8 us (2%)
    unnamed x2, waiting for transfers between devices  199 us
    ppermute x16, waiting for transfers between devices, from_behind(): lax.ppermute(value, axis, [(source, source + steps) for source in range(f...  81 us
    ppermute x19, starting transfers between devices, extended(): before = lax.ppermute(last, axis, up)  64.3 us
    ppermute x16, starting transfers between devices, from_behind(): lax.ppermute(value, axis, [(source, source + steps) for source in range(f...  54.2 us
    ppermute x19, starting transfers between devices, extended(): after = lax.ppermute(first, axis, down)  37.8 us
    ppermute x19, waiting for transfers between devices, extended(): after = lax.ppermute(first, axis, down)  31.5 us
    reduce_sum x45, other arithmetic, group_norm(): spread = jnp.mean((grouped - center) ** 2, axis=(1, 3), keepdims=True)  23.4 us
    convert_element_type x14, other arithmetic, up_forward(): activated = act_up(joined.astype(jnp.float32)).astype(jnp.bfloat16)  20.8 us
  transfers between devices with their start and end apart: 55, of which 27 were waited for; matrix products, arithmetic and copies ran while one was open for 13% of the time, Pallas kernels for 0%

commit v1 on v0

v1 whole, which is shorter than its diff:
```python
import functools
import math

import jax
import jax.numpy as jnp
import numpy as np
from jax import lax
from jax.experimental import pallas as pl
from jax.experimental.pallas import tpu as pltpu
from jax.sharding import Mesh
from jax.sharding import PartitionSpec as P

CH = 320
GROUPS = 32
SEGS = 4
TOK = 1024
FRAMES = 16
LANES = 128
TILES = TOK // LANES
ROWS = 32
BF = jnp.bfloat16
F32 = jnp.float32
DOWN_SEL = 80
UP_SEL = 160


def mix_bits(value):
    value = value ^ lax.shift_right_logical(value, jnp.int32(16))
    value = value * -2048144789
    value = value ^ lax.shift_right_logical(value, jnp.int32(13))
    value = value * -1028477387
    value = value ^ lax.shift_right_logical(value, jnp.int32(16))
    return value


def noise_field(seed_value, lat_dim, pix_dim):
    lat_ids = lax.broadcasted_iota(jnp.int32, (lat_dim, pix_dim * FRAMES), 0)
    tokens = lax.broadcasted_iota(jnp.int32, (lat_dim, pix_dim * FRAMES), 1)
    frame_ids = tokens % FRAMES
    pix_ids = tokens // FRAMES
    index = (frame_ids * lat_dim + lat_ids) * pix_dim + pix_ids
    salted = seed_value * -1640531535
    first = mix_bits(index * 2 + salted)
    second = mix_bits(index * 2 + 1 + salted)
    unit_a = (lax.shift_right_logical(first, jnp.int32(8)).astype(F32) + 0.5) / 16777216.0
    unit_b = (lax.shift_right_logical(second, jnp.int32(8)).astype(F32) + 0.5) / 16777216.0
    return jnp.sqrt(-2.0 * jnp.log(unit_a)) * jnp.cos(2.0 * math.pi * unit_b)


def time_embedding(step_value, channels):
    half = channels // 2
    frequency = jnp.exp(-math.log(10000.0) * jnp.arange(half, dtype=F32) / half)
    phase = step_value.astype(F32) * frequency
    return jnp.concatenate([jnp.sin(phase), jnp.cos(phase)])


def group_matrix(size):
    ids = np.arange(CH) // size
    return (ids[:, None] == ids[None, :]).astype(np.float32)


def dot(a, b):
    return jnp.dot(a, b, preferred_element_type=F32)


def dot_nt(a, b):
    return lax.dot_general(a, b, (((1,), (1,)), ((), ())), preferred_element_type=F32)


def tile(j):
    return slice(j * LANES, (j + 1) * LANES)


def row_block(r):
    return pl.ds(pl.multiple_of(r * ROWS, ROWS), ROWS)


def fold(value):
    for step in (16, 32, 64):
        value = value + pltpu.roll(value, step, 1)
    return value


def group_sums(group, values, parts):
    pieces = []
    for value in values:
        rest = value
        for _ in range(parts):
            piece = rest.astype(BF)
            pieces.append(piece)
            rest = rest - piece.astype(F32)
    sums = dot(group, jnp.concatenate(pieces, axis=1))
    out = []
    for i in range(len(values)):
        total = sums[:, tile(i * parts)]
        for q in range(1, parts):
            total = total + sums[:, tile(i * parts + q)]
        out.append(fold(total))
    return out


def gn_stats(x_at, group, size, m_scr, q_scr, mean_at, rstd_at):
    def body(r, carry):
        rows = row_block(r)
        parts = [x_at(rows, tile(j)) for j in range(TILES)]
        total = parts[0]
        for p in parts[1:]:
            total = total + p
        mid = total * (1.0 / TILES)
        square = None
        for p in parts:
            d = p - mid
            square = d * d if square is None else square + d * d
        m_scr[rows, :] = mid
        q_scr[rows, :] = square
        return carry

    lax.fori_loop(0, CH // ROWS, body, 0)
    mid = m_scr[...]
    (mean,) = group_sums(group, [mid], 3)
    mean = mean * (1.0 / (8 * size))
    away = mid - mean
    (spread,) = group_sums(group, [q_scr[...] + (TILES * 1.0) * away * away], 2)
    mean_at[...] = mean
    rstd_at[...] = lax.rsqrt(spread * (1.0 / (64 * size)) + 1e-05)


def frame_masks():
    lane = lax.broadcasted_iota(jnp.int32, (ROWS, LANES), 1) % FRAMES
    return lane != 0, lane != FRAMES - 1


def earlier(value, masks):
    return jnp.where(masks[0], pltpu.roll(value, 1, 1), 0.0).astype(BF)


def later(value, masks):
    return jnp.where(masks[1], pltpu.roll(value, LANES - 1, 1), 0.0).astype(BF)


def silu_parts(y):
    sig = 0.5 * jnp.tanh(0.5 * y) + 0.5
    return sig, y * sig


def norm_bwd(ga_ref, ga_off, x_at, group, size, mean_at, rstd_at, emb_ref, m_scr, q_scr, emit):
    def first(r, carry):
        rows = row_block(r)
        grows = pl.ds(pl.multiple_of(ga_off + r * ROWS, ROWS), ROWS)
        mean = mean_at[rows, :]
        rstd = rstd_at[rows, :]
        emb = None if emb_ref is None else emb_ref[rows, :]
        s1 = None
        s2 = None
        for j in range(TILES):
            xhat = (x_at(rows, tile(j)) - mean) * rstd
            y = xhat if emb is None else xhat + emb
            sig, act = silu_parts(y)
            dy = ga_ref[grows, tile(j)] * (sig + act * (1.0 - sig))
            ga_ref[grows, tile(j)] = dy
            s1 = dy if s1 is None else s1 + dy
            s2 = dy * xhat if s2 is None else s2 + dy * xhat
        m_scr[rows, :] = s1
        q_scr[rows, :] = s2
        return carry

    lax.fori_loop(0, CH // ROWS, first, 0)
    s1, s2 = group_sums(group, [m_scr[...], q_scr[...]], 2)
    scale = 1.0 / (64 * size)
    m_scr[...] = s1 * scale
    q_scr[...] = s2 * scale

    def second(r, carry):
        rows = row_block(r)
        grows = pl.ds(pl.multiple_of(ga_off + r * ROWS, ROWS), ROWS)
        mean = mean_at[rows, :]
        rstd = rstd_at[rows, :]
        m1 = m_scr[rows, :]
        m2 = q_scr[rows, :]
        for j in range(TILES):
            xhat = (x_at(rows, tile(j)) - mean) * rstd
            emit(rows, tile(j), rstd * (ga_ref[grows, tile(j)] - m1 - xhat * m2))
        return carry

    lax.fori_loop(0, CH // ROWS, second, 0)


def conv_cols(body):
    def step(n, carry):
        body(pl.ds(pl.multiple_of(n * 256, 256), 256))
        return carry

    lax.fori_loop(0, TOK // 256, step, 0)


def transpose_into(dst, src, rows):
    for start in range(0, rows, LANES):
        size = min(LANES, rows - start)
        dst[:, start : start + size] = src[start : start + size, :].astype(F32).T.astype(BF)


def segment_copies(ids, own, mine, other, dest, sems):
    seg = ids[0]
    core = ids[1]
    half = mine.shape[1]
    copies = [pltpu.make_async_copy(own, dest.at[seg], sems.at[0])]
    for slot, away in enumerate((1, 3, 2)):
        s = lax.rem(seg + away, SEGS)
        for which, source, place in ((0, mine, core), (1, other, 1 - core)):
            copies.append(
                pltpu.make_async_copy(
                    source.at[slot],
                    dest.at[s, pl.ds(pl.multiple_of(place * half, 32), half), :],
                    sems.at[1 + slot * 2 + which],
                )
            )
    return copies


def down_forward_kernel(
    ids, noisy, in_t, emb, group, pick, own, mine, other,
    xs, mean, rstd, asel, wnat_out,
    wt, stack, m_scr, q_scr, sems,
):
    copies = segment_copies(ids, own, mine, other, wnat_out, sems)
    for c in copies:
        c.start()
    conv_cols(lambda cols: xs.__setitem__((0, slice(None), cols), dot(in_t[...], noisy[:, cols]).astype(BF)))
    for c in copies:
        c.wait()
    masks = frame_masks()

    def stage(s, carry):
        transpose_into(wt, wnat_out.at[s], 3 * CH)
        x_at = lambda rows, cols: xs[s, rows, cols].astype(F32)
        gn_stats(x_at, group[...], 10, m_scr, q_scr, mean.at[s], rstd.at[s])

        def act(r, c2):
            rows = row_block(r)
            mu = mean[s, rows, :]
            rs = rstd[s, rows, :]
            e = emb[rows, :]
            for j in range(TILES):
                y = (x_at(rows, tile(j)) - mu) * rs + e
                _, a = silu_parts(y)
                stack[0, rows, tile(j)] = earlier(a, masks)
                stack[1, rows, tile(j)] = a.astype(BF)
                stack[2, rows, tile(j)] = later(a, masks)
            return c2

        lax.fori_loop(0, CH // ROWS, act, 0)

        @pl.when(s == ids[0])
        def _():
            asel[...] = dot(pick[...], stack[1]).astype(BF)

        def conv(cols):
            taps = stack[:, :, cols].reshape(3 * CH, 256)
            total = dot(wt[...], taps) + xs[s, :, cols].astype(F32)
            xs[s + 1, :, cols] = total.astype(BF)

        conv_cols(conv)
        return carry

    lax.fori_loop(0, SEGS, stage, 0)


def up_kernel(
    ids, xs, group, pick, out_t, out_wide, noise, own, mine, other,
    gu, gsk, kgrad, cgrad,
    wnat, wt, wb, stack, bsel, jsel, es, umean, urstd, ga, thru, gcur, gstack, m_scr, q_scr, sems, *, scale
):
    copies = segment_copies(ids, own, mine, other, wnat, sems)
    for c in copies:
        c.start()
    for c in copies:
        c.wait()
    masks = frame_masks()
    es[SEGS] = xs[SEGS]

    def forward(i, carry):
        s = SEGS - 1 - i
        transpose_into(wt, wnat.at[s], 8 * CH)
        for half, src in ((0, es), (1, xs)):
            x_at = lambda rows, cols: src[s + 1, rows, cols].astype(F32)
            gn_stats(x_at, group[...], 20, m_scr, q_scr, umean.at[s, half], urstd.at[s, half])

            def act(r, c2):
                rows = row_block(r)
                mu = umean[s, half, rows, :]
                rs = urstd[s, half, rows, :]
                for j in range(TILES):
                    raw = src[s + 1, rows, tile(j)]
                    y = (raw.astype(F32) - mu) * rs
                    _, a = silu_parts(y)
                    stack[0 + half, rows, tile(j)] = earlier(a, masks)
                    stack[2 + half, rows, tile(j)] = a.astype(BF)
                    stack[4 + half, rows, tile(j)] = later(a, masks)
                    stack[6 + half, rows, tile(j)] = raw
                return c2

            lax.fori_loop(0, CH // ROWS, act, 0)

        @pl.when(s == ids[0])
        def _():
            bsel[...] = dot(pick[...], stack[2:4].reshape(2 * CH, TOK)).astype(BF)
            jsel[...] = dot(pick[...], stack[6:8].reshape(2 * CH, TOK)).astype(BF)

        def conv(cols):
            es[s, :, cols] = dot(wt[...], stack[:, :, cols].reshape(8 * CH, 256)).astype(BF)

        conv_cols(conv)
        return carry

    lax.fori_loop(0, SEGS, forward, 0)

    def seed(cols):
        predicted = dot(out_t[...], es[0, :, cols])
        error = (predicted[:4] - noise[:, cols]) * scale
        total = out_wide[:, 0:1] * error[0:1, :]
        for l in range(1, 4):
            total = total + out_wide[:, l : l + 1] * error[l : l + 1, :]
        gcur[:, cols] = total.astype(BF)

    conv_cols(seed)

    def backward(s, carry):
        for k in range(3):
            wb[:, k * CH : (k + 1) * CH] = wnat[s, k * 2 * CH : (k + 1) * 2 * CH, :]

        def spread(r, c2):
            rows = row_block(r)
            for j in range(TILES):
                g = gcur[rows, tile(j)]
                g32 = g.astype(F32)
                gstack[0, rows, tile(j)] = later(g32, masks)
                gstack[1, rows, tile(j)] = g
                gstack[2, rows, tile(j)] = earlier(g32, masks)
            return c2

        lax.fori_loop(0, CH // ROWS, spread, 0)

        @pl.when(s == ids[0])
        def _():
            for k in range(3):
                gu[k] = dot_nt(bsel[...], gstack[k])
            gsk[...] = dot_nt(jsel[...], gcur[...])

        def conv(cols):
            ga[:, cols] = dot(wb[...], gstack[:, :, cols].reshape(3 * CH, 256))
            thru[:, cols] = dot(wnat[s, 6 * CH :, :], gcur[:, cols])

        conv_cols(conv)
        for half, src in ((0, es), (1, xs)):
            x_at = lambda rows, cols: src[s + 1, rows, cols].astype(F32)

            def emit(rows, cols, dx):
                if half == 0:
                    gcur[rows, cols] = (dx + thru[rows, cols]).astype(BF)
                else:
                    trows = pl.ds(pl.multiple_of(rows.start + CH, ROWS), ROWS)
                    kgrad[s, rows, cols] = (dx + thru[trows, cols]).astype(BF)

            norm_bwd(
                ga, half * CH, x_at, group[...], 20, umean.at[s, half], urstd.at[s, half], None, m_scr, q_scr, emit
            )
        return carry

    lax.fori_loop(0, SEGS, backward, 0)
    cgrad[...] = gcur[...]


def down_backward_kernel(
    ids, xs, mean, rstd, asel, wnat, emb, group, kgrad, cgrad,
    gd,
    wb, hstack, ga, ccur, m_scr, q_scr,
):
    masks = frame_masks()
    ccur[...] = cgrad[...]

    def take(s):
        def spread(r, c2):
            rows = row_block(r)
            for j in range(TILES):
                h = (kgrad[s, rows, tile(j)].astype(F32) + ccur[rows, tile(j)].astype(F32)).astype(BF)
                h32 = h.astype(F32)
                hstack[0, rows, tile(j)] = later(h32, masks)
                hstack[1, rows, tile(j)] = h
                hstack[2, rows, tile(j)] = earlier(h32, masks)
            return c2

        lax.fori_loop(0, CH // ROWS, spread, 0)

        @pl.when(s == ids[0])
        def _():
            for k in range(3):
                gd[k] = dot_nt(asel[...], hstack[k])

    def stage(i, carry):
        s = SEGS - 1 - i
        take(s)
        for k in range(3):
            wb[:, k * CH : (k + 1) * CH] = wnat[s, k * CH : (k + 1) * CH, :]

        def conv(cols):
            ga[:, cols] = dot(wb[...], hstack[:, :, cols].reshape(3 * CH, 256))

        conv_cols(conv)
        x_at = lambda rows, cols: xs[s, rows, cols].astype(F32)

        def emit(rows, cols, dx):
            ccur[rows, cols] = (hstack[1, rows, cols].astype(F32) + dx).astype(BF)

        norm_bwd(ga, 0, x_at, group[...], 10, mean.at[s], rstd.at[s], emb, m_scr, q_scr, emit)
        return carry

    lax.fori_loop(0, SEGS - 1, stage, 0)
    take(0)


VMEM = pl.BlockSpec(memory_space=pltpu.VMEM)
SMEM = pl.BlockSpec(memory_space=pltpu.SMEM)
ANY = pl.BlockSpec(memory_space=pl.ANY)
PARAMS = pltpu.CompilerParams(vmem_limit_bytes=60 * 1024 * 1024)


def shape(dims, dtype=BF):
    return jax.ShapeDtypeStruct(dims, dtype)


def run_down_forward(ids, noisy, in_t, emb, group, pick, own, mine, other):
    return pl.pallas_call(
        down_forward_kernel,
        name="down_forward",
        out_shape=(
            shape((SEGS + 1, CH, TOK)),
            shape((SEGS, CH, LANES), F32),
            shape((SEGS, CH, LANES), F32),
            shape((DOWN_SEL, TOK)),
            shape((SEGS, 3 * CH, CH)),
        ),
        in_specs=[SMEM] + [VMEM] * 5 + [ANY] * 3,
        out_specs=(VMEM,) * 5,
        scratch_shapes=[
            pltpu.VMEM((CH, 3 * CH), BF),
            pltpu.VMEM((3, CH, TOK), BF),
            pltpu.VMEM((CH, LANES), F32),
            pltpu.VMEM((CH, LANES), F32),
            pltpu.SemaphoreType.DMA((7,)),
        ],
        compiler_params=PARAMS,
    )(ids, noisy, in_t, emb, group, pick, own, mine, other)


def run_up(ids, xs, group, pick, out_t, out_wide, noise, own, mine, other, scale):
    return pl.pallas_call(
        functools.partial(up_kernel, scale=scale),
        name="up_both",
        out_shape=(
            shape((3, UP_SEL, CH), F32),
            shape((UP_SEL, CH), F32),
            shape((SEGS, CH, TOK)),
            shape((CH, TOK)),
        ),
        in_specs=[SMEM] + [VMEM] * 6 + [ANY] * 3,
        out_specs=(VMEM,) * 4,
        scratch_shapes=[
            pltpu.VMEM((SEGS, 8 * CH, CH), BF),
            pltpu.VMEM((CH, 8 * CH), BF),
            pltpu.VMEM((2 * CH, 3 * CH), BF),
            pltpu.VMEM((8, CH, TOK), BF),
            pltpu.VMEM((UP_SEL, TOK), BF),
            pltpu.VMEM((UP_SEL, TOK), BF),
            pltpu.VMEM((SEGS + 1, CH, TOK), BF),
            pltpu.VMEM((SEGS, 2, CH, LANES), F32),
            pltpu.VMEM((SEGS, 2, CH, LANES), F32),
            pltpu.VMEM((2 * CH, TOK), F32),
            pltpu.VMEM((2 * CH, TOK), F32),
            pltpu.VMEM((CH, TOK), BF),
            pltpu.VMEM((3, CH, TOK), BF),
            pltpu.VMEM((CH, LANES), F32),
            pltpu.VMEM((CH, LANES), F32),
            pltpu.SemaphoreType.DMA((7,)),
        ],
        compiler_params=PARAMS,
    )(ids, xs, group, pick, out_t, out_wide, noise, own, mine, other)


def run_down_backward(ids, xs, mean, rstd, asel, wnat, emb, group, kgrad, cgrad):
    return pl.pallas_call(
        down_backward_kernel,
        name="down_backward",
        out_shape=shape((3, DOWN_SEL, CH), F32),
        in_specs=[SMEM] + [VMEM] * 9,
        out_specs=VMEM,
        scratch_shapes=[
            pltpu.VMEM((CH, 3 * CH), BF),
            pltpu.VMEM((3, CH, TOK), BF),
            pltpu.VMEM((CH, TOK), F32),
            pltpu.VMEM((CH, TOK), BF),
            pltpu.VMEM((CH, LANES), F32),
            pltpu.VMEM((CH, LANES), F32),
        ],
        compiler_params=PARAMS,
    )(ids, xs, mean, rstd, asel, wnat, emb, group, kgrad, cgrad)


def pick_matrix(x_index, per_device, channels):
    row = lax.broadcasted_iota(jnp.int32, (16 * per_device, channels), 0)
    col = lax.broadcasted_iota(jnp.int32, (16 * per_device, channels), 1)
    core = row // (8 * per_device)
    dp = (row // per_device) % 8
    want = (dp * 8 + 2 * x_index + core) * per_device + row % per_device
    return (col == want).astype(BF)


def clip_inputs(clip, step_value, seed_value, in_weight, out_weight):
    lat_dim, pix_dim, frames = clip.shape
    noise = noise_field(seed_value, lat_dim, pix_dim)
    theta = step_value.astype(F32) * (0.5 * math.pi / 1000.0)
    noisy = (
        jnp.cos(theta) * clip.reshape(lat_dim, pix_dim * frames).astype(F32) + jnp.sin(theta) * noise
    ).astype(BF)
    noisy = jnp.pad(noisy, ((0, 16 - lat_dim), (0, 0)))
    in_t = jnp.pad(in_weight.T, ((0, 0), (0, 16 - lat_dim)))
    out_t = jnp.pad(out_weight.T, ((0, 16 - lat_dim), (0, 0)))
    emb = jnp.broadcast_to(time_embedding(step_value, CH)[:, None], (CH, LANES))
    return noise, noisy, in_t, out_t, emb


def swap_core(value):
    return lax.ppermute(value, "core", [(0, 1), (1, 0)])


def from_segment(value, away):
    return lax.ppermute(value, "segment", [((i + away) % SEGS, i) for i in range(SEGS)])


def gather_sections(half):
    mine = jnp.stack([from_segment(half, away) for away in (1, 3, 2)])
    return mine, swap_core(mine)


def share(total, core):
    keep = lax.dynamic_index_in_dim(total, core, 0, keepdims=False)
    give = lax.dynamic_index_in_dim(total, 1 - core, 0, keepdims=False)
    both = keep + swap_core(give)
    parts = lax.all_to_all(both, "dp", 0, 0, tiled=True)
    return jnp.sum(parts, axis=0)


def local(latents, timesteps, seeds, in_weight, out_weight, down_weight, up_weight, skip_weight):
    seg = lax.axis_index("segment")
    core = lax.axis_index("core")
    x_index = lax.axis_index("x")
    elements = 16 * FRAMES * 4 * 64
    scale = 64.0 / math.sqrt(elements)
    ids = jnp.stack([seg, core]).astype(jnp.int32)
    down_nat = down_weight[0].reshape(3 * CH, CH)
    up_nat = jnp.concatenate([up_weight[0].reshape(6 * CH, CH), skip_weight[0]], axis=0)
    d_half = lax.dynamic_slice_in_dim(down_nat, core * (3 * CH // 2), 3 * CH // 2, 0)
    u_half = lax.dynamic_slice_in_dim(up_nat, core * 4 * CH, 4 * CH, 0)
    d_mine, d_other = gather_sections(d_half)
    u_mine, u_other = gather_sections(u_half)

    clips = lax.all_gather(latents, ("x", "core"), axis=0)
    clip = lax.dynamic_index_in_dim(clips, core, 1, keepdims=False)
    clip = jnp.transpose(clip.reshape(FRAMES, 4, 64), (1, 2, 0))
    step_value = lax.dynamic_index_in_dim(timesteps, core, 0, keepdims=False)
    seed_value = lax.dynamic_index_in_dim(seeds, core, 0, keepdims=False)
    noise, noisy, in_t, out_t, emb = clip_inputs(clip, step_value, seed_value, in_weight, out_weight)
    g10 = jnp.asarray(group_matrix(10), BF)
    g20 = jnp.asarray(group_matrix(20), BF)

    xs, mean, rstd, asel, wnat = run_down_forward(
        ids, noisy, in_t, emb, g10, pick_matrix(x_index, 5, CH), down_nat, d_mine, d_other
    )
    gu, gsk, kgrad, cgrad = run_up(
        ids, xs, g20, pick_matrix(x_index, 10, 2 * CH), out_t, out_weight.astype(F32), noise,
        up_nat, u_mine, u_other, scale,
    )
    up_all = jnp.concatenate([gu, gsk[None]], axis=0).reshape(4, 2, 8, 10, CH)
    up_all = jnp.transpose(up_all, (1, 2, 0, 3, 4)).reshape(2, 8, 40 * CH)
    up_sum = share(up_all, core).reshape(4, 10, CH)
    gd = run_down_backward(ids, xs, mean, rstd, asel, wnat, emb, g10, kgrad, cgrad)
    down_all = jnp.transpose(gd.reshape(3, 2, 8, 5, CH), (1, 2, 0, 3, 4)).reshape(2, 8, 15 * CH)
    down_sum = share(down_all, core).reshape(3, 5, CH)
    return down_sum[None], up_sum[:3][None], up_sum[3][None]


def solution(mesh):
    devices = mesh.devices
    grid = Mesh(devices.reshape(devices.shape[0], devices.shape[1], 4, 2), ("dp", "segment", "x", "core"))
    tm = ("x", "core")
    return jax.shard_map(
        local,
        mesh=grid,
        in_specs=(
            P("dp", tm, None, None),
            P("dp"),
            P("dp"),
            P(),
            P(),
            P("segment", None, None, None),
            P("segment", None, None, None),
            P("segment", None, None),
        ),
        out_specs=(
            P("segment", None, ("dp",) + tm, None),
            P("segment", None, ("dp",) + tm, None),
            P("segment", ("dp",) + tm, None),
        ),
        check_vma=False,
    )
```

time: 841 us -> 241 us (0.29); the launches traced: 826 us -> 239 us
  waiting for transfers between devices: 311 us -> 33.2 us
  other arithmetic: 161 us -> 11 us
  starting transfers between devices: 156 us -> 23.6 us
  Pallas kernels: 0 us -> 119 us
  local copies, waits for them, and re-layouts: 150 us -> 34.7 us
  matrix products: 26.8 us -> 0 us
  between operations: 18.8 us -> 2.5 us
  blocking collectives: 0 us -> 14.8 us
    unnamed x2 -> x0, waiting for transfers between devices: 199 us -> none
    ppermute x54 -> x10, starting transfers between devices: 156 us -> 11.9 us  [the longest x6 9.69 us: from_segment(): lax.ppermute(value, 'segment', [((i + away) % SEGS, i) for i in range(SEG...]
    pallas_call x0 -> x3, Pallas kernels: none -> 119 us  [the longest x1 74.9 us: run_up(): pl.pallas_call(functools.partial(up_kernel, scale=scale), name='up_both',...]
    ppermute x54 -> x10, waiting for transfers between devices: 113 us -> 12.6 us  [the longest x6 12.6 us: from_segment(): lax.ppermute(value, 'segment', [((i + away) % SEGS, i) for i in range(SEG...]
    reduce_sum x98 -> x2, other arithmetic: 48.5 us -> 0.42 us  [share(): return jnp.sum(parts, axis=0)]
    convert_element_type x35 -> x3, other arithmetic: 31.5 us -> 2.53 us  [the longest x2 1.74 us: pick_matrix(): return (col == want).astype(BF)]
    dot_general x28 -> x0, matrix products: 26.8 us -> none  [the longest x4 7.66 us: conv_wgrad(): lax.dot_general(stack_taps(padded), grad_out.reshape(-1, cout), (((0,), (...]
    mul x56 -> x2, local copies, waits for them, and re-layouts: 22.7 us -> 0.21 us  [clip_inputs(): jnp.cos(theta) * clip.reshape(lat_dim, pix_dim * frames).astype(F32)]
  transfers between devices with their start and end apart: 55 -> 12, of which waited for: 27 -> 3; matrix products, arithmetic and copies ran while one was open for 13% -> 12% of each run, Pallas kernels for 0% -> 10%
where the time goes in v1:
time: 241 us; the launch traced here: 239 us
  Pallas kernels  119 us (49%)
  local copies, waits for them, and re-layouts  34.7 us (14%)
  waiting for transfers between devices  33.2 us (14%)
  starting transfers between devices  23.6 us (10%)
  blocking collectives  14.8 us (6%)
  other arithmetic  11 us (5%)
  between operations  2.5 us (1%)
    pallas_call x1, Pallas kernels, run_up(): pl.pallas_call(functools.partial(up_kernel, scale=scale), name='up_both',...  74.9 us
    pallas_call x1, Pallas kernels, run_down_forward(): pl.pallas_call(down_forward_kernel, name='down_forward', out_shape=(shape...  24.3 us
    all_to_all x2, waiting for transfers between devices, share(): parts = lax.all_to_all(both, 'dp', 0, 0, tiled=True)  20.6 us
    pallas_call x1, Pallas kernels, run_down_backward(): pl.pallas_call(down_backward_kernel, name='down_backward', out_shape=shap...  20.2 us
    all_gather x1, blocking collectives, local(): clips = lax.all_gather(latents, ('x', 'core'), axis=0)  14.8 us
    ppermute x6, waiting for transfers between devices, from_segment(): lax.ppermute(value, 'segment', [((i + away) % SEGS, i) for i in range(SEG...  12.6 us
    all_to_all x2, starting transfers between devices, share(): parts = lax.all_to_all(both, 'dp', 0, 0, tiled=True)  11.6 us
    ppermute x6, starting transfers between devices, from_segment(): lax.ppermute(value, 'segment', [((i + away) % SEGS, i) for i in range(SEG...  9.69 us
  transfers between devices with their start and end apart: 12, of which 3 were waited for; matrix products, arithmetic and copies ran while one was open for 12% of the time, Pallas kernels for 10%

profile of v1, /device:TPU:1, one launch (start us, length us, event | category | flops | bytes accessed | tf_op | source)
XLA Modules:
  0.0 239.0 jit_solution(4327938656637199071)
XLA Ops:
  0.6 1.3 copy.50
  1.9 2.5 %copy.49 = bf16[1,3,640,320]{3,2,1,0:T(8,128)(2,1)S(1)} copy(bf16[1,3,640,320]{2,3,1,0:T(8,128)(2,1)} %param.16) | data formatting | bytes 2457600 | tf_op args[6]
  4.5 1.5 fusion
  6.0 1.3 copy.51
  7.3 3.7 %collective-permute-start.6 = (bf16[1280,320]{0,1:T(8,128)(2,1)}, bf16[1280,320]{0,1:T(8,128)(2,1)S(1)}, u32[]{:S(2)}, u32[]{:S(2)}) collective-permute-start(bf16[1280,320]{0,1:T(8,128)(2,1)} %copy.51), channel_id=1, source_target_pairs={{16,0},{24,8},{0,16},{8,24},{17,1},{25,9},{1,17},{9,25},{18,2},{26... | collective-permute-start | bytes 2457608 | tf_op jit(solution)/shard_map/ppermute | solution.py:536
  11.5 2.3 collective-permute-start.4
  13.8 1.8 constant_dynamic-slice_fusion
  17.5 14.8 %all-gather = bf16[16,2,4,64]{3,2,1,0:T(4,128)(2,1)S(1)} all-gather(bf16[2,2,4,64]{3,2,1,0:T(4,128)(2,1)S(1)} %copy-done.7), channel_id=2, replica_groups=mesh['dp'=8,'segment'=4,'x'=4,'core'=2] {'x','core'}, dimensions={0}, use_global_device_ids=true | all-gather | bytes 18432 | tf_op jit(solution)/shard_map/all_gather | solution.py:566
  33.8 2.7 %collective-permute-start = (bf16[480,320]{1,0:T(8,128)(2,1)}, bf16[480,320]{1,0:T(8,128)(2,1)}, u32[]{:S(2)}, u32[]{:S(2)}) collective-permute-start(bf16[480,320]{1,0:T(8,128)(2,1)} %constant_dynamic-slice_fusion), channel_id=1, source_target_pairs={{8,0},{16,8},{24,16},{0,24},{9,1},{17,9},{25,17},{1,25},{10,2},{18... | collective-permute-start | bytes 921608 | tf_op jit(solution)/shard_map/ppermute | solution.py:536
  36.5 1.3 copy.56
  37.8 12.6 %collective-permute-done.5 = bf16[1280,320]{0,1:T(8,128)(2,1)S(1)} collective-permute-done((bf16[1280,320]{0,1:T(8,128)(2,1)}, bf16[1280,320]{0,1:T(8,128)(2,1)S(1)}, u32[]{:S(2)}, u32[]{:S(2)}) %collective-permute-start.5) | collective-permute-done | bytes 819232 | tf_op jit(solution)/shard_map/ppermute | solution.py:536
  50.4 1.3 copy.54
  51.7 1.3 copy.52
  53.0 2.4 %pad_maximum_fusion.mine = bf16[3,1280,320]{2,1,0:T(8,128)(2,1)S(1)} fusion(bf16[1,1280,320]{2,1,0:T(8,128)(2,1)} %bitcast.34, bf16[1,1280,320]{2,1,0:T(8,128)(2,1)} %bitcast.35, bf16[1,1280,320]{2,1,0:T(8,128)(2,1)} %bitcast.36), kind=kLoop, calls=%fused_computation | loop fusion | flops 2457600 | bytes 4915200 | tf_op jit(solution)/shard_map/stack | solution.py:540
  55.4 3.7 %copy.57 = bf16[3,1280,320]{1,2,0:T(8,128)(2,1)} copy(bf16[3,1280,320]{2,1,0:T(8,128)(2,1)S(1)} %pad_maximum_fusion.mine) | data formatting | bytes 4915200 | tf_op jit(solution)/shard_map/stack | solution.py:540
  59.9 0.8 add_convert_fusion
  63.8 1.6 pad_maximum_fusion.2.mine
  65.4 1.6 copy.47
  68.2 0.8 fusion.16.pick
  69.0 0.9 fusion.8.pick
  69.9 1.5 pad_maximum_fusion.1.own
  71.4 2.3 copy.48.other
  74.5 24.3 %down_forward.1 = (bf16[5,320,1024]{2,1,0:T(8,128)(2,1)}, f32[4,320,128]{2,1,0:T(8,128)}, f32[4,320,128]{2,1,0:T(8,128)}, bf16[80,1024]{1,0:T(8,128)(2,1)}, bf16[4,960,320]{2,1,0:T(8,128)(2,1)}) custom-call(s32[2]{0:T(128)} %pad_add_fusion.ids, bf16[16,1024]{1,0:T(8,128)(2,1)} %pad.12.noisy, bf16[320,16]{1,0:T(8,128)(2,1)} %pad.13.in_t, ...), custom_call_target="tpu_custom_call" | custom-call | tf_op jit(solution)/shard_map/down_forward/pallas_call | solution.py:432
  98.8 5.2 %copy.59.other = bf16[3,1280,320]{2,1,0:T(8,128)(2,1)} copy(bf16[3,1280,320]{1,2,0:T(8,128)(2,1)} %collective-permute-done.7) | data formatting | bytes 4915200 | tf_op jit(solution)/shard_map/ppermute | solution.py:532
  104.0 74.9 %up_both.1 = (f32[3,160,320]{2,1,0:T(8,128)}, f32[160,320]{1,0:T(8,128)}, bf16[4,320,1024]{2,1,0:T(8,128)(2,1)}, bf16[320,1024]{1,0:T(8,128)(2,1)}) custom-call(s32[2]{0:T(128)} %pad_add_fusion.ids, bf16[5,320,1024]{2,1,0:T(8,128)(2,1)} %get-tuple-element.12.xs, bf16[320,320]{1,0:T(8,128)(2,1)} %constant.189.clone.group, bf16[160,640]{1,0:T(8,128)(2,1)} %fusion.8.pick, ...), custom_call_target="tpu_custom_call" | custom-call | tf_op jit(solution)/shard_map/up_both/pallas_call | solution.py:456
  178.9 20.2 %down_backward.1 = f32[3,80,320]{2,1,0:T(8,128)} custom-call(s32[2]{0:T(128)} %pad_add_fusion.ids, bf16[5,320,1024]{2,1,0:T(8,128)(2,1)} %get-tuple-element.12.xs, f32[4,320,128]{2,1,0:T(8,128)} %get-tuple-element.13.mean, f32[4,320,128]{2,1,0:T(8,128)} %get-tuple-element.14.rstd, bf16[80,1024]{1,0:T(8,128)(2,1)} %get-tuple-element.15.asel, ...), custom_call_target="tpu_custom_call" | custom-call | tf_op jit(solution)/shard_map/down_backward/pallas_call | solution.py:490
  199.1 1.1 reshape.48
  203.1 8.2 %all-to-all-start = ((f32[8,1,4800]{2,1,0:T(1,128)}), f32[8,1,4800]{2,1,0:T(1,128)S(1)}, u32[]{:S(2)}, u32[]{:S(2)}) async-start(f32[8,1,4800]{2,1,0:T(1,128)} %all_to_all.12), calls=%async_computation | async-start | bytes 311296 | tf_op jit(solution)/shard_map/all_to_all | solution.py:548
  211.4 1.0 all_to_all.14
  212.4 7.9 %all-to-all-done = f32[8,1,4800]{2,1,0:T(1,128)S(1)} async-done(((f32[8,1,4800]{2,1,0:T(1,128)}), f32[8,1,4800]{2,1,0:T(1,128)S(1)}, u32[]{:S(2)}, u32[]{:S(2)}) %all-to-all-start) | async-done | bytes 153632 | tf_op jit(solution)/shard_map/all_to_all | solution.py:548
  220.4 3.5 %all-to-all-start.1 = ((f32[8,1,12800]{2,1,0:T(1,128)}), f32[8,1,12800]{2,1,0:T(1,128)S(1)}, u32[]{:S(2)}, u32[]{:S(2)}) async-start(f32[8,1,12800]{2,1,0:T(1,128)} %all_to_all.14), calls=%async_computation.1 | async-start | bytes 819200 | tf_op jit(solution)/shard_map/all_to_all | solution.py:548
  224.6 12.7 %all-to-all-done.1 = f32[8,1,12800]{2,1,0:T(1,128)S(1)} async-done(((f32[8,1,12800]{2,1,0:T(1,128)}), f32[8,1,12800]{2,1,0:T(1,128)S(1)}, u32[]{:S(2)}, u32[]{:S(2)}) %all-to-all-start.1) | async-done | bytes 409632 | tf_op jit(solution)/shard_map/all_to_all | solution.py:548
  (85 shorter events, 13.6 us)
Async XLA Ops:
  4.5 2.9 %copy-start.1 = (bf16[1,3,640,320]{3,2,1,0:T(8,128)(2,1)}, bf16[1,3,640,320]{3,2,1,0:T(8,128)(2,1)S(1)}, u32[]{:S(2)}) copy-start(bf16[1,3,640,320]{3,2,1,0:T(8,128)(2,1)S(1)} %copy.49) | copy-start | bytes 3686404
  6.0 10.1 %copy-start.9 = (s32[2]{0:T(128)S(1)}, s32[2]{0:T(128)}, u32[]{:S(2)}) copy-start(s32[2]{0:T(128)} %param.11) | copy-start | bytes 28
  6.0 11.5 %copy-start.7 = (bf16[2,2,4,64]{3,2,1,0:T(4,128)(2,1)S(1)}, bf16[2,2,4,64]{3,2,1,0:T(4,128)(2,1)}, u32[]{:S(2)}) copy-start(bf16[2,2,4,64]{3,2,1,0:T(4,128)(2,1)} %param.10) | copy-start | bytes 6148
  6.0 26.5 %copy-start.10 = (s32[2]{0:T(128)S(1)}, s32[2]{0:T(128)}, u32[]{:S(2)}) copy-start(s32[2]{0:T(128)} %param.12) | copy-start | bytes 28
  7.3 26.5 %collective-permute-start.6 = (bf16[1280,320]{0,1:T(8,128)(2,1)}, bf16[1280,320]{0,1:T(8,128)(2,1)S(1)}, u32[]{:S(2)}, u32[]{:S(2)}) collective-permute-start(bf16[1280,320]{0,1:T(8,128)(2,1)} %copy.51), channel_id=1, source_target_pairs={{16,0},{24,8},{0,16},{8,24},{17,1},{25,9},{1,17},{9,25},{18,2},{26... | collective-permute-start | bytes 2457608 | tf_op jit(solution)/shard_map/ppermute | solution.py:536
  11.1 39.3 %collective-permute-start.5 = (bf16[1280,320]{0,1:T(8,128)(2,1)}, bf16[1280,320]{0,1:T(8,128)(2,1)S(1)}, u32[]{:S(2)}, u32[]{:S(2)}) collective-permute-start(bf16[1280,320]{0,1:T(8,128)(2,1)} %copy.51), channel_id=1, source_target_pairs={{24,0},{0,8},{8,16},{16,24},{25,1},{1,9},{9,17},{17,25},{26,2},{2,... | collective-permute-start | bytes 2457608 | tf_op jit(solution)/shard_map/ppermute | solution.py:536
  11.5 40.2 %collective-permute-start.4 = (bf16[1280,320]{0,1:T(8,128)(2,1)}, bf16[1280,320]{0,1:T(8,128)(2,1)S(1)}, u32[]{:S(2)}, u32[]{:S(2)}) collective-permute-start(bf16[1280,320]{0,1:T(8,128)(2,1)} %copy.51), channel_id=1, source_target_pairs={{8,0},{16,8},{24,16},{0,24},{9,1},{17,9},{25,17},{1,25},{10,2},{18... | collective-permute-start | bytes 2457608 | tf_op jit(solution)/shard_map/ppermute | solution.py:536
  15.5 48.3 %collective-permute-start.2 = (bf16[480,320]{1,0:T(8,128)(2,1)}, bf16[480,320]{1,0:T(8,128)(2,1)}, u32[]{:S(2)}, u32[]{:S(2)}) collective-permute-start(bf16[480,320]{1,0:T(8,128)(2,1)} %constant_dynamic-slice_fusion), channel_id=1, source_target_pairs={{16,0},{24,8},{0,16},{8,24},{17,1},{25,9},{1,17},{9,25},{18,2},{26... | collective-permute-start | bytes 921608 | tf_op jit(solution)/shard_map/ppermute | solution.py:536
  15.5 48.3 %collective-permute-start.1 = (bf16[480,320]{1,0:T(8,128)(2,1)}, bf16[480,320]{1,0:T(8,128)(2,1)}, u32[]{:S(2)}, u32[]{:S(2)}) collective-permute-start(bf16[480,320]{1,0:T(8,128)(2,1)} %constant_dynamic-slice_fusion), channel_id=1, source_target_pairs={{24,0},{0,8},{8,16},{16,24},{25,1},{1,9},{9,17},{17,25},{26,2},{2,... | collective-permute-start | bytes 921608 | tf_op jit(solution)/shard_map/ppermute | solution.py:536
  33.8 30.0 %collective-permute-start = (bf16[480,320]{1,0:T(8,128)(2,1)}, bf16[480,320]{1,0:T(8,128)(2,1)}, u32[]{:S(2)}, u32[]{:S(2)}) collective-permute-start(bf16[480,320]{1,0:T(8,128)(2,1)} %constant_dynamic-slice_fusion), channel_id=1, source_target_pairs={{8,0},{16,8},{24,16},{0,24},{9,1},{17,9},{25,17},{1,25},{10,2},{18... | collective-permute-start | bytes 921608 | tf_op jit(solution)/shard_map/ppermute | solution.py:536
  55.4 3.8 %copy-start = (bf16[3,1280,320]{2,1,0:T(8,128)(2,1)}, bf16[3,1280,320]{2,1,0:T(8,128)(2,1)S(1)}, u32[]{:S(2)}) copy-start(bf16[3,1280,320]{2,1,0:T(8,128)(2,1)S(1)} %pad_maximum_fusion.mine) | copy-start | bytes 7372804
  55.4 5.3 %copy-start.8 = (bf16[4,320]{1,0:T(4,128)(2,1)S(1)}, bf16[4,320]{1,0:T(4,128)(2,1)}, u32[]{:S(2)}) copy-start(bf16[4,320]{1,0:T(4,128)(2,1)} %param.13) | copy-start | bytes 7684
  55.4 6.7 %copy-start.6 = (bf16[320,4]{0,1:T(4,128)(2,1)S(1)}, bf16[320,4]{0,1:T(4,128)(2,1)}, u32[]{:S(2)}) copy-start(bf16[320,4]{0,1:T(4,128)(2,1)} %param.14) | copy-start | bytes 7684
  59.2 39.6 %collective-permute-start.7 = (bf16[3,1280,320]{1,2,0:T(8,128)(2,1)}, bf16[3,1280,320]{1,2,0:T(8,128)(2,1)}, u32[]{:S(2)}, u32[]{:S(2)}) collective-permute-start(bf16[3,1280,320]{1,2,0:T(8,128)(2,1)} %copy.57), channel_id=1, source_target_pairs={{0,1},{1,0},{2,3},{3,2},{4,5},{5,4},{6,7},{7,6},{8,9},{9,8},{10,11... | collective-permute-start | bytes 7372808 | tf_op jit(solution)/shard_map/ppermute | solution.py:532
  63.8 6.1 %copy-start.2 = (bf16[1,3,640,320]{3,2,1,0:T(8,128)(2,1)S(1)}, bf16[1,3,640,320]{3,2,1,0:T(8,128)(2,1)}, u32[]{:S(2)}) copy-start(bf16[1,3,640,320]{3,2,1,0:T(8,128)(2,1)} %copy-done.1) | copy-start | bytes 3686404
  65.4 6.0 %copy-start.3 = (bf16[3,480,320]{2,1,0:T(8,128)(2,1)}, bf16[3,480,320]{2,1,0:T(8,128)(2,1)S(1)}, u32[]{:S(2)}) copy-start(bf16[3,480,320]{2,1,0:T(8,128)(2,1)S(1)} %pad_maximum_fusion.2.mine) | copy-start | bytes 2764804
  67.0 4.4 %collective-permute-start.3 = (bf16[3,480,320]{1,2,0:T(8,128)(2,1)}, bf16[3,480,320]{1,2,0:T(8,128)(2,1)}, u32[]{:S(2)}, u32[]{:S(2)}) collective-permute-start(bf16[3,480,320]{1,2,0:T(8,128)(2,1)} %copy.47), channel_id=1, source_target_pairs={{0,1},{1,0},{2,3},{3,2},{4,5},{5,4},{6,7},{7,6},{8,9},{9,8},{10,11... | collective-permute-start | bytes 2764808 | tf_op jit(solution)/shard_map/ppermute | solution.py:532
  199.1 1.7 copy-start.5
  199.1 1.7 copy-start.4
  200.5 1.9 collective-permute-start.8
  201.7 9.6 %collective-permute-start.9 = (f32[8,12800]{1,0:T(8,128)S(1)}, f32[8,12800]{1,0:T(8,128)S(1)}, u32[]{:S(2)}, u32[]{:S(2)}) collective-permute-start(f32[8,12800]{1,0:T(8,128)S(1)} %dynamic-slice_bitcast_fusion), channel_id=1, source_target_pairs={{0,1},{1,0},{2,3},{3,2},{4,5},{5,4},{6,7},{7,6},{8,9},{9,8},{10,11... | collective-permute-start | bytes 1228808 | tf_op jit(solution)/shard_map/ppermute | solution.py:532
  203.1 17.2 %all-to-all-start = ((f32[8,1,4800]{2,1,0:T(1,128)}), f32[8,1,4800]{2,1,0:T(1,128)S(1)}, u32[]{:S(2)}, u32[]{:S(2)}) async-start(f32[8,1,4800]{2,1,0:T(1,128)} %all_to_all.12), calls=%async_computation | async-start | bytes 311296 | tf_op jit(solution)/shard_map/all_to_all | solution.py:548
  220.4 17.0 %all-to-all-start.1 = ((f32[8,1,12800]{2,1,0:T(1,128)}), f32[8,1,12800]{2,1,0:T(1,128)S(1)}, u32[]{:S(2)}, u32[]{:S(2)}) async-start(f32[8,1,12800]{2,1,0:T(1,128)} %all_to_all.14), calls=%async_computation.1 | async-start | bytes 819200 | tf_op jit(solution)/shard_map/all_to_all | solution.py:548

commit v2 on v1

v2 whole, which is shorter than its diff:
```python
import functools
import math

import jax
import jax.numpy as jnp
import numpy as np
from jax import lax
from jax.experimental import pallas as pl
from jax.experimental.pallas import tpu as pltpu
from jax.sharding import Mesh
from jax.sharding import PartitionSpec as P

CH = 320
GROUPS = 32
SEGS = 4
TOK = 1024
FRAMES = 16
LANES = 128
TILES = TOK // LANES
ROWS = 32
BF = jnp.bfloat16
F32 = jnp.float32
DOWN_SEL = 80
UP_SEL = 160


def mix_bits(value):
    value = value ^ lax.shift_right_logical(value, jnp.int32(16))
    value = value * -2048144789
    value = value ^ lax.shift_right_logical(value, jnp.int32(13))
    value = value * -1028477387
    value = value ^ lax.shift_right_logical(value, jnp.int32(16))
    return value


def noise_field(seed_value, lat_dim, pix_dim):
    lat_ids = lax.broadcasted_iota(jnp.int32, (lat_dim, pix_dim * FRAMES), 0)
    tokens = lax.broadcasted_iota(jnp.int32, (lat_dim, pix_dim * FRAMES), 1)
    frame_ids = tokens % FRAMES
    pix_ids = tokens // FRAMES
    index = (frame_ids * lat_dim + lat_ids) * pix_dim + pix_ids
    salted = seed_value * -1640531535
    first = mix_bits(index * 2 + salted)
    second = mix_bits(index * 2 + 1 + salted)
    unit_a = (lax.shift_right_logical(first, jnp.int32(8)).astype(F32) + 0.5) / 16777216.0
    unit_b = (lax.shift_right_logical(second, jnp.int32(8)).astype(F32) + 0.5) / 16777216.0
    return jnp.sqrt(-2.0 * jnp.log(unit_a)) * jnp.cos(2.0 * math.pi * unit_b)


def time_embedding(step_value, channels):
    half = channels // 2
    frequency = jnp.exp(-math.log(10000.0) * jnp.arange(half, dtype=F32) / half)
    phase = step_value.astype(F32) * frequency
    return jnp.concatenate([jnp.sin(phase), jnp.cos(phase)])


def group_matrix(size):
    ids = np.arange(CH) // size
    return (ids[:, None] == ids[None, :]).astype(np.float32)


def dot(a, b):
    return jnp.dot(a, b, preferred_element_type=F32)


def dot_nt(a, b):
    return lax.dot_general(a, b, (((1,), (1,)), ((), ())), preferred_element_type=F32)


def tile(j):
    return slice(j * LANES, (j + 1) * LANES)


def row_block(r):
    return pl.ds(pl.multiple_of(r * ROWS, ROWS), ROWS)


def fold(value):
    for step in (16, 32, 64):
        value = value + pltpu.roll(value, step, 1)
    return value


def group_sums(group, values, parts):
    pieces = []
    for value in values:
        rest = value
        for _ in range(parts):
            piece = rest.astype(BF)
            pieces.append(piece)
            rest = rest - piece.astype(F32)
    sums = dot(group, jnp.concatenate(pieces, axis=1))
    out = []
    for i in range(len(values)):
        total = sums[:, tile(i * parts)]
        for q in range(1, parts):
            total = total + sums[:, tile(i * parts + q)]
        out.append(fold(total))
    return out


def gn_stats(x_at, group, size, m_scr, q_scr, mean_at, rstd_at):
    def body(r, carry):
        rows = row_block(r)
        parts = [x_at(rows, tile(j)) for j in range(TILES)]
        total = parts[0]
        for p in parts[1:]:
            total = total + p
        mid = total * (1.0 / TILES)
        square = None
        for p in parts:
            d = p - mid
            square = d * d if square is None else square + d * d
        m_scr[rows, :] = mid
        q_scr[rows, :] = square
        return carry

    lax.fori_loop(0, CH // ROWS, body, 0)
    mid = m_scr[...]
    (mean,) = group_sums(group, [mid], 3)
    mean = mean * (1.0 / (8 * size))
    away = mid - mean
    (spread,) = group_sums(group, [q_scr[...] + (TILES * 1.0) * away * away], 2)
    mean_at[...] = mean
    rstd_at[...] = lax.rsqrt(spread * (1.0 / (64 * size)) + 1e-05)


def shift_matrix():
    lane = np.arange(LANES)
    out = np.zeros((LANES, 2 * LANES), np.float32)
    for l in lane:
        if l % FRAMES != 0:
            out[l - 1, l] = 1.0
        if l % FRAMES != FRAMES - 1:
            out[l + 1, LANES + l] = 1.0
    return out


def neighbours(value, shift):
    both = dot(value, shift).astype(BF)
    return both[:, :LANES], both[:, LANES:]


def silu_parts(y):
    sig = 0.5 * jnp.tanh(0.5 * y) + 0.5
    return sig, y * sig


def norm_bwd(ga_ref, ga_off, x_at, group, size, mean_at, rstd_at, emb_ref, m_scr, q_scr, emit):
    def first(r, carry):
        rows = row_block(r)
        grows = pl.ds(pl.multiple_of(ga_off + r * ROWS, ROWS), ROWS)
        mean = mean_at[rows, :]
        rstd = rstd_at[rows, :]
        emb = None if emb_ref is None else emb_ref[rows, :]
        s1 = None
        s2 = None
        for j in range(TILES):
            xhat = (x_at(rows, tile(j)) - mean) * rstd
            y = xhat if emb is None else xhat + emb
            sig, act = silu_parts(y)
            dy = ga_ref[grows, tile(j)] * (sig + act * (1.0 - sig))
            ga_ref[grows, tile(j)] = dy
            s1 = dy if s1 is None else s1 + dy
            s2 = dy * xhat if s2 is None else s2 + dy * xhat
        m_scr[rows, :] = s1
        q_scr[rows, :] = s2
        return carry

    lax.fori_loop(0, CH // ROWS, first, 0)
    s1, s2 = group_sums(group, [m_scr[...], q_scr[...]], 2)
    scale = 1.0 / (64 * size)
    m_scr[...] = s1 * scale
    q_scr[...] = s2 * scale

    def second(r, carry):
        rows = row_block(r)
        grows = pl.ds(pl.multiple_of(ga_off + r * ROWS, ROWS), ROWS)
        mean = mean_at[rows, :]
        rstd = rstd_at[rows, :]
        m1 = m_scr[rows, :]
        m2 = q_scr[rows, :]
        for j in range(TILES):
            xhat = (x_at(rows, tile(j)) - mean) * rstd
            emit(rows, tile(j), rstd * (ga_ref[grows, tile(j)] - m1 - xhat * m2))
        return carry

    lax.fori_loop(0, CH // ROWS, second, 0)


MAIN = 256
REST = CH - MAIN


def copy_bytes(ref, sem):
    return pltpu.make_async_copy(ref, ref, sem)


def section_of(seg, slot):
    return lax.rem(seg + (1, 3, 2)[slot], SEGS)


def start_down_copies(ids, own, parts, dest, sems):
    half = 3 * CH // 2
    pltpu.make_async_copy(own, dest.at[ids[0]], sems.at[ids[0]]).start()
    for slot in range(3):
        s = section_of(ids[0], slot)
        for source, place in ((parts[slot], ids[1]), (parts[3 + slot], 1 - ids[1])):
            rows = pl.ds(pl.multiple_of(place * half, 32), half)
            pltpu.make_async_copy(source, dest.at[s, rows, :], sems.at[s]).start()


def start_up_copies(ids, own_up, own_skip, parts, dest, sems):
    half = CH // 2
    seg = ids[0]
    for k in range(4):
        source = own_up.at[k] if k < 3 else own_skip
        pltpu.make_async_copy(source, dest.at[seg, :, k * 640 : (k + 1) * 640], sems.at[seg]).start()
    for slot in range(3):
        s = section_of(seg, slot)
        for source, place in ((parts[slot], ids[1]), (parts[3 + slot], 1 - ids[1])):
            rows = pl.ds(pl.multiple_of(place * half, 32), half)
            for k in range(4):
                pltpu.make_async_copy(
                    source.at[k], dest.at[s, rows, k * 640 : (k + 1) * 640], sems.at[s]
                ).start()


def activate(x_at, mean_at, rstd_at, emb_ref, put):
    def act(r, carry):
        rows = row_block(r)
        mu = mean_at[rows, :]
        rs = rstd_at[rows, :]
        e = None if emb_ref is None else emb_ref[rows, :]
        for j in range(TILES):
            y = (x_at(rows, tile(j)) - mu) * rs
            if e is not None:
                y = y + e
            put(rows, tile(j), silu_parts(y)[1].astype(BF))
        return carry

    lax.fori_loop(0, CH // ROWS, act, 0)


def down_forward_kernel(
    ids, noisy, in_t, emb, g10, g20, shift, pick, own, p0, p1, p2, q0, q1, q2,
    xs, mean, rstd, asel, wnat, dstack, dmean, drstd,
    wt, stack, m_scr, q_scr, sems,
):
    start_down_copies(ids, own, (p0, p1, p2, q0, q1, q2), wnat, sems)
    xs[0] = dot(in_t[...], noisy[...]).astype(BF)

    def stage(s, carry):
        x_at = lambda rows, cols: xs[s, rows, cols].astype(F32)
        gn_stats(x_at, g10[...], 10, m_scr, q_scr, mean.at[s], rstd.at[s])

        def put(rows, cols, a):
            stack[1, rows, cols] = a

        activate(x_at, mean.at[s], rstd.at[s], emb, put)
        for j in range(TILES):
            before, after = neighbours(stack[1, :, tile(j)], shift[...])
            stack[0, :, tile(j)] = before
            stack[2, :, tile(j)] = after

        @pl.when(s == ids[0])
        def _():
            asel[...] = dot(pick[...], stack[1]).astype(BF)

        copy_bytes(wnat.at[s], sems.at[s]).wait()
        for begin in range(0, 3 * CH, LANES):
            size = min(LANES, 3 * CH - begin)
            wt[:, begin : begin + size] = wnat[s, begin : begin + size, :].T
        total = dot(wt[...], stack[...].reshape(3 * CH, TOK)) + xs[s].astype(F32)
        xs[s + 1] = total.astype(BF)
        return carry

    lax.fori_loop(0, SEGS, stage, 0)

    def ahead(s, carry):
        x_at = lambda rows, cols: xs[s + 1, rows, cols].astype(F32)
        gn_stats(x_at, g20[...], 20, m_scr, q_scr, dmean.at[s], drstd.at[s])

        def put(rows, cols, a):
            dstack[s, 1, rows, cols] = a

        activate(x_at, dmean.at[s], drstd.at[s], None, put)
        for j in range(TILES):
            before, after = neighbours(dstack[s, 1, :, tile(j)], shift[...])
            dstack[s, 0, :, tile(j)] = before
            dstack[s, 2, :, tile(j)] = after
        dstack[s, 3] = xs[s + 1]
        return carry

    lax.fori_loop(0, SEGS, ahead, 0)


def spread_grad(value, shift, gstack):
    for j in range(TILES):
        g = value(tile(j))
        before, after = neighbours(g, shift)
        for k, part in ((0, after), (1, g), (2, before)):
            gstack[k * MAIN : (k + 1) * MAIN, tile(j)] = part[:MAIN]
            gstack[3 * MAIN + k * REST : 3 * MAIN + (k + 1) * REST, tile(j)] = part[MAIN:]


def up_kernel(
    ids, xs, dmean, drstd, g20, shift, pick, out_t, out_wide, noise,
    dstack, own_up, own_skip, p0, p1, p2, q0, q1, q2,
    gu, kgrad, cgrad,
    wt, wb, stack, bsel, jsel, es, emean, erstd, ga, thru, gcur, gstack, m_scr, q_scr, sems, dsems, *, scale
):
    start_up_copies(ids, own_up, own_skip, (p0, p1, p2, q0, q1, q2), wt, sems)

    def fetch(s):
        slot = lax.rem(s, 2)
        for k in range(4):
            pltpu.make_async_copy(dstack.at[s, k], stack.at[slot, k, 1], dsems.at[slot, k]).start()

    fetch(jnp.int32(SEGS - 1))
    es[SEGS] = xs[SEGS]

    def forward(i, carry):
        s = SEGS - 1 - i
        slot = lax.rem(s, 2)

        @pl.when(s > 0)
        def _():
            fetch(s - 1)

        x_at = lambda rows, cols: es[s + 1, rows, cols].astype(F32)
        gn_stats(x_at, g20[...], 20, m_scr, q_scr, emean.at[s], erstd.at[s])

        def put(rows, cols, a):
            stack[slot, 1, 0, rows, cols] = a

        activate(x_at, emean.at[s], erstd.at[s], None, put)
        for j in range(TILES):
            before, after = neighbours(stack[slot, 1, 0, :, tile(j)], shift[...])
            stack[slot, 0, 0, :, tile(j)] = before
            stack[slot, 2, 0, :, tile(j)] = after
        stack[slot, 3, 0] = es[s + 1]
        for k in range(4):
            pltpu.make_async_copy(dstack.at[s, k], stack.at[slot, k, 1], dsems.at[slot, k]).wait()

        @pl.when(s == ids[0])
        def _():
            bsel[...] = dot(pick[...], stack[slot, 1].reshape(2 * CH, TOK)).astype(BF)
            jsel[...] = dot(pick[...], stack[slot, 3].reshape(2 * CH, TOK)).astype(BF)

        copy_bytes(wt.at[s], sems.at[s]).wait()
        es[s] = dot(wt[s], stack[slot].reshape(8 * CH, TOK)).astype(BF)
        return carry

    lax.fori_loop(0, SEGS, forward, 0)

    predicted = dot(out_t[...], es[0])
    thru[0:4, :] = (predicted[:4] - noise[...]) * scale

    def seed(r, carry):
        rows = row_block(r)
        for j in range(TILES):
            total = out_wide[rows, 0:1] * thru[0:1, tile(j)]
            for l in range(1, 4):
                total = total + out_wide[rows, l : l + 1] * thru[l : l + 1, tile(j)]
            gcur[rows, tile(j)] = total.astype(BF)
        return carry

    lax.fori_loop(0, CH // ROWS, seed, 0)

    def backward(s, carry):
        for k in range(3):
            for b in range(2):
                wb[:, k * MAIN + b * LANES : k * MAIN + (b + 1) * LANES] = wt[
                    s, b * LANES : (b + 1) * LANES, k * 640 : (k + 1) * 640
                ].T
        tops = [wt[s, MAIN:, k * 640 : (k + 1) * 640] for k in range(3)]
        wb[:, 3 * MAIN : 3 * MAIN + LANES] = jnp.concatenate(tops[:2], axis=0).T
        wb[:, 3 * MAIN + LANES : 3 * CH] = tops[2].T
        for b in range(2):
            wb[:, 1024 + b * LANES : 1024 + (b + 1) * LANES] = wt[s, b * LANES : (b + 1) * LANES, 1920:].T
        wb[:, 1024 + MAIN : 1024 + CH] = wt[s, MAIN:, 1920:].T
        spread_grad(lambda cols: gcur[:, cols], shift[...], gstack)

        @pl.when(s == ids[0])
        def _():
            gu[:, : 3 * CH] = dot_nt(bsel[...], gstack[...])
            gu[:, 3 * CH :] = dot_nt(jsel[...], gcur[...])

        ga[...] = dot(wb[:, : 3 * CH], gstack[...])
        thru[...] = dot(wb[:, 1024 : 1024 + CH], gcur[...])

        def emit_e(rows, cols, dx):
            gcur[rows, cols] = (dx + thru[rows, cols]).astype(BF)

        def emit_d(rows, cols, dx):
            trows = pl.ds(pl.multiple_of(rows.start + CH, ROWS), ROWS)
            kgrad[s, rows, cols] = (dx + thru[trows, cols]).astype(BF)

        e_at = lambda rows, cols: es[s + 1, rows, cols].astype(F32)
        d_at = lambda rows, cols: xs[s + 1, rows, cols].astype(F32)
        norm_bwd(ga, 0, e_at, g20[...], 20, emean.at[s], erstd.at[s], None, m_scr, q_scr, emit_e)
        norm_bwd(ga, CH, d_at, g20[...], 20, dmean.at[s], drstd.at[s], None, m_scr, q_scr, emit_d)
        return carry

    lax.fori_loop(0, SEGS, backward, 0)
    cgrad[...] = gcur[...]


def down_backward_kernel(
    ids, xs, mean, rstd, asel, wnat, emb, g10, shift, kgrad, cgrad,
    gd,
    wb, hstack, hcur, ga, ccur, m_scr, q_scr,
):
    ccur[...] = cgrad[...]

    def take(s):
        def value(cols):
            h = (kgrad[s, :, cols].astype(F32) + ccur[:, cols].astype(F32)).astype(BF)
            hcur[:, cols] = h
            return h

        spread_grad(value, shift[...], hstack)

        @pl.when(s == ids[0])
        def _():
            gd[...] = dot_nt(asel[...], hstack[...])

    def stage(i, carry):
        s = SEGS - 1 - i
        take(s)
        for k in range(3):
            wb[:, k * MAIN : (k + 1) * MAIN] = wnat[s, k * CH : (k + 1) * CH, :MAIN]
            wb[:, 3 * MAIN + k * REST : 3 * MAIN + (k + 1) * REST] = wnat[s, k * CH : (k + 1) * CH, MAIN:]
        ga[...] = dot(wb[...], hstack[...])
        x_at = lambda rows, cols: xs[s, rows, cols].astype(F32)

        def emit(rows, cols, dx):
            ccur[rows, cols] = (hcur[rows, cols].astype(F32) + dx).astype(BF)

        norm_bwd(ga, 0, x_at, g10[...], 10, mean.at[s], rstd.at[s], emb, m_scr, q_scr, emit)
        return carry

    lax.fori_loop(0, SEGS - 1, stage, 0)
    take(0)


VMEM = pl.BlockSpec(memory_space=pltpu.VMEM)
SMEM = pl.BlockSpec(memory_space=pltpu.SMEM)
ANY = pl.BlockSpec(memory_space=pl.ANY)
PARAMS = pltpu.CompilerParams(vmem_limit_bytes=60 * 1024 * 1024)


def shape(dims, dtype=BF):
    return jax.ShapeDtypeStruct(dims, dtype)


def cost(microseconds):
    return pl.CostEstimate(flops=int(microseconds * 1e9), bytes_accessed=0, transcendentals=0)


def run_down_forward(*args):
    return pl.pallas_call(
        down_forward_kernel,
        name="down_forward",
        out_shape=(
            shape((SEGS + 1, CH, TOK)),
            shape((SEGS, CH, LANES), F32),
            shape((SEGS, CH, LANES), F32),
            shape((DOWN_SEL, TOK)),
            shape((SEGS, 3 * CH, CH)),
            shape((SEGS, 4, CH, TOK)),
            shape((SEGS, CH, LANES), F32),
            shape((SEGS, CH, LANES), F32),
        ),
        in_specs=[SMEM] + [VMEM] * 7 + [ANY] * 7,
        out_specs=(VMEM,) * 8,
        scratch_shapes=[
            pltpu.VMEM((CH, 3 * CH), BF),
            pltpu.VMEM((3, CH, TOK), BF),
            pltpu.VMEM((CH, LANES), F32),
            pltpu.VMEM((CH, LANES), F32),
            pltpu.SemaphoreType.DMA((SEGS,)),
        ],
        compiler_params=PARAMS,
        cost_estimate=cost(20),
    )(*args)


def run_up(*args, scale):
    return pl.pallas_call(
        functools.partial(up_kernel, scale=scale),
        name="up_both",
        out_shape=(
            shape((UP_SEL, 4 * CH), F32),
            shape((SEGS, CH, TOK)),
            shape((CH, TOK)),
        ),
        in_specs=[SMEM] + [VMEM] * 9 + [ANY] * 9,
        out_specs=(VMEM,) * 3,
        scratch_shapes=[
            pltpu.VMEM((SEGS, CH, 8 * CH), BF),
            pltpu.VMEM((2 * CH, 1024 + 384), BF),
            pltpu.VMEM((2, 4, 2, CH, TOK), BF),
            pltpu.VMEM((UP_SEL, TOK), BF),
            pltpu.VMEM((UP_SEL, TOK), BF),
            pltpu.VMEM((SEGS + 1, CH, TOK), BF),
            pltpu.VMEM((SEGS, CH, LANES), F32),
            pltpu.VMEM((SEGS, CH, LANES), F32),
            pltpu.VMEM((2 * CH, TOK), F32),
            pltpu.VMEM((2 * CH, TOK), F32),
            pltpu.VMEM((CH, TOK), BF),
            pltpu.VMEM((3 * CH, TOK), BF),
            pltpu.VMEM((CH, LANES), F32),
            pltpu.VMEM((CH, LANES), F32),
            pltpu.SemaphoreType.DMA((SEGS,)),
            pltpu.SemaphoreType.DMA((2, 4)),
        ],
        compiler_params=PARAMS,
        cost_estimate=cost(50),
    )(*args)


def run_down_backward(*args):
    return pl.pallas_call(
        down_backward_kernel,
        name="down_backward",
        out_shape=shape((DOWN_SEL, 3 * CH), F32),
        in_specs=[SMEM] + [VMEM] * 10,
        out_specs=VMEM,
        scratch_shapes=[
            pltpu.VMEM((CH, 3 * CH), BF),
            pltpu.VMEM((3 * CH, TOK), BF),
            pltpu.VMEM((CH, TOK), BF),
            pltpu.VMEM((CH, TOK), F32),
            pltpu.VMEM((CH, TOK), BF),
            pltpu.VMEM((CH, LANES), F32),
            pltpu.VMEM((CH, LANES), F32),
        ],
        compiler_params=PARAMS,
        cost_estimate=cost(15),
    )(*args)


def pick_matrix(x_index, per_device, channels):
    row = lax.broadcasted_iota(jnp.int32, (16 * per_device, channels), 0)
    col = lax.broadcasted_iota(jnp.int32, (16 * per_device, channels), 1)
    core = row // (8 * per_device)
    dp = (row // per_device) % 8
    want = (dp * 8 + 2 * x_index + core) * per_device + row % per_device
    return (col == want).astype(BF)


def clip_inputs(clip, step_value, seed_value, in_weight, out_weight):
    lat_dim, pix_dim, frames = clip.shape
    noise = noise_field(seed_value, lat_dim, pix_dim)
    theta = step_value.astype(F32) * (0.5 * math.pi / 1000.0)
    noisy = (
        jnp.cos(theta) * clip.reshape(lat_dim, pix_dim * frames).astype(F32) + jnp.sin(theta) * noise
    ).astype(BF)
    noisy = jnp.pad(noisy, ((0, 16 - lat_dim), (0, 0)))
    in_t = jnp.pad(in_weight.T, ((0, 0), (0, 16 - lat_dim)))
    out_t = jnp.pad(out_weight.T, ((0, 16 - lat_dim), (0, 0)))
    emb = jnp.broadcast_to(time_embedding(step_value, CH)[:, None], (CH, LANES))
    return noise, noisy, in_t, out_t, emb


def swap_core(value):
    return lax.ppermute(value, "core", [(0, 1), (1, 0)])


def from_segment(value, away):
    return lax.ppermute(value, "segment", [((i + away) % SEGS, i) for i in range(SEGS)])


def fetch_sections(half):
    return [from_segment(half, away) for away in (1, 3, 2)]


def cores_sum(total, core, rows):
    size = 8 * rows
    keep = lax.dynamic_slice_in_dim(total, core * size, size, 0)
    give = lax.dynamic_slice_in_dim(total, (1 - core) * size, size, 0)
    return (keep + swap_core(give)).reshape(8, -1)


def dp_sum(both, rows):
    parts = lax.all_to_all(both, "dp", 0, 0, tiled=True)
    return jnp.sum(parts, axis=0).reshape(rows, -1)


def taps(value):
    return jnp.stack(
        [
            jnp.concatenate(
                [
                    value[:, k * MAIN : (k + 1) * MAIN],
                    value[:, 3 * MAIN + k * REST : 3 * MAIN + (k + 1) * REST],
                ],
                axis=1,
            )
            for k in range(3)
        ]
    )


def clip_gradients(ids, clip, step_value, seed_value, x_index, in_weight, out_weight, down, up, reduce_up):
    noise, noisy, in_t, out_t, emb = clip_inputs(clip, step_value, seed_value, in_weight, out_weight)
    g10 = jnp.asarray(group_matrix(10), BF)
    g20 = jnp.asarray(group_matrix(20), BF)
    shift = jnp.asarray(shift_matrix(), BF)
    pick_d = pick_matrix(x_index, 5, CH)
    pick_u = pick_matrix(x_index, 10, 2 * CH)
    xs, mean, rstd, asel, wnat, dstack, dmean, drstd = run_down_forward(
        ids, noisy, in_t, emb, g10, g20, shift, pick_d, *down()
    )
    xs, up_args = up(xs)
    gu, kgrad, cgrad = run_up(
        ids, xs, dmean, drstd, g20, shift, pick_u, out_t, out_weight.astype(F32), noise, dstack, *up_args,
        scale=64.0 / math.sqrt(16 * FRAMES * 4 * 64),
    )
    up_part, kgrad = reduce_up(gu, kgrad)
    gd = run_down_backward(ids, xs, mean, rstd, asel, wnat, emb, g10, shift, kgrad, cgrad)
    return gd, up_part


def local(latents, timesteps, seeds, in_weight, out_weight, down_weight, up_weight, skip_weight):
    seg = lax.axis_index("segment")
    core = lax.axis_index("core")
    x_index = lax.axis_index("x")
    ids = jnp.stack([seg, core]).astype(jnp.int32)
    down_nat = down_weight[0].reshape(3 * CH, CH)
    up_t = jnp.transpose(up_weight[0], (0, 2, 1))
    skip_t = skip_weight[0].T
    d_half = lax.dynamic_slice_in_dim(down_nat, core * (3 * CH // 2), 3 * CH // 2, 0)
    u_half = jnp.concatenate(
        [
            lax.dynamic_slice_in_dim(up_t, core * (CH // 2), CH // 2, 1),
            lax.dynamic_slice_in_dim(skip_t, core * (CH // 2), CH // 2, 0)[None],
        ],
        axis=0,
    )
    d_mine = fetch_sections(d_half)
    *d_mine, u_half = lax.optimization_barrier((*d_mine, u_half))
    u_mine = fetch_sections(u_half)

    clips = lax.all_gather(latents, ("x", "core"), axis=0)
    clip = lax.dynamic_index_in_dim(clips, core, 1, keepdims=False)
    clip = jnp.transpose(clip.reshape(FRAMES, 4, 64), (1, 2, 0))
    step_value = lax.dynamic_index_in_dim(timesteps, core, 0, keepdims=False)
    seed_value = lax.dynamic_index_in_dim(seeds, core, 0, keepdims=False)

    def down():
        return [down_nat, *d_mine, *[swap_core(p) for p in d_mine]]

    def up(xs):
        *parts, xs = lax.optimization_barrier((*u_mine, xs))
        return xs, [up_t, skip_t, *parts, *[swap_core(p) for p in parts]]

    def reduce_up(gu, kgrad):
        return lax.optimization_barrier((cores_sum(gu, core, 10), kgrad))

    gd, up_part = clip_gradients(
        ids, clip, step_value, seed_value, x_index, in_weight, out_weight, down, up, reduce_up
    )
    up_sum = dp_sum(up_part, 10)
    gd, up_sum = lax.optimization_barrier((gd, up_sum))
    down_sum = taps(dp_sum(cores_sum(gd, core, 5), 5))
    return down_sum[None], taps(up_sum[:, : 3 * CH])[None], up_sum[:, 3 * CH :][None]


def solution(mesh):
    devices = mesh.devices
    grid = Mesh(devices.reshape(devices.shape[0], devices.shape[1], 4, 2), ("dp", "segment", "x", "core"))
    tm = ("x", "core")
    return jax.shard_map(
        local,
        mesh=grid,
        in_specs=(
            P("dp", tm, None, None),
            P("dp"),
            P("dp"),
            P(),
            P(),
            P("segment", None, None, None),
            P("segment", None, None, None),
            P("segment", None, None),
        ),
        out_specs=(
            P("segment", None, ("dp",) + tm, None),
            P("segment", None, ("dp",) + tm, None),
            P("segment", ("dp",) + tm, None),
        ),
        check_vma=False,
    )
```

time: 241 us -> 183 us (0.76)
  waiting for transfers between devices: 33.2 us -> 13.5 us
  Pallas kernels: 119 us -> 101 us
  local copies, waits for them, and re-layouts: 34.7 us -> 17.2 us
  other arithmetic: 11 us -> 5.93 us
  starting transfers between devices: 23.6 us -> 27.6 us
    pallas_call x1, Pallas kernels: 74.9 us -> 53 us  [run_up(): pl.pallas_call(functools.partial(up_kernel, scale=scale), name='up_both',...]
    all_to_all x2, waiting for transfers between devices: 20.6 us -> 7.08 us  [dp_sum(): parts = lax.all_to_all(both, 'dp', 0, 0, tiled=True)]
    ppermute x5 -> x0, local copies, waits for them, and re-layouts: 11.5 us -> none  [the longest x2 7.56 us: swap_core(): return lax.ppermute(value, 'core', [(0, 1), (1, 0)])]
    ppermute x6, waiting for transfers between devices: 12.6 us -> 2.33 us  [from_segment(): lax.ppermute(value, 'segment', [((i + away) % SEGS, i) for i in range(SEG...]
    pallas_call x1, Pallas kernels: 24.3 us -> 31.7 us  [run_down_forward(): pl.pallas_call(down_forward_kernel, name='down_forward', out_shape=(shape...]
    another operation x3, local copies, waits for them, and re-layouts: 5.98 us -> 0.03 us  [taps(): jnp.stack([jnp.concatenate([value[:, k * MAIN:(k + 1) * MAIN], value[:, 3...]
    pallas_call x1, Pallas kernels: 20.2 us -> 15.9 us  [run_down_backward(): pl.pallas_call(down_backward_kernel, name='down_backward', out_shape=shap...]
    ppermute x4 -> x8, waiting for transfers between devices: 0.01 us -> 4.04 us  [swap_core(): return lax.ppermute(value, 'core', [(0, 1), (1, 0)])]
  transfers between devices with their start and end apart: 12 -> 16, of which waited for: 3 -> 7; matrix products, arithmetic and copies ran while one was open for 12% -> 8% of each run, Pallas kernels for 10% -> 26%
where the time goes in v2:
time: 183 us; the launch traced here: 182 us
  Pallas kernels  101 us (55%)
  starting transfers between devices  27.6 us (15%)
  local copies, waits for them, and re-layouts  17.2 us (9%)
  blocking collectives  14.6 us (8%)
  waiting for transfers between devices  13.5 us (7%)
  other arithmetic  5.93 us (3%)
  between operations  2.4 us (1%)
    pallas_call x1, Pallas kernels, run_up(): pl.pallas_call(functools.partial(up_kernel, scale=scale), name='up_both',...  53 us
    pallas_call x1, Pallas kernels, run_down_forward(): pl.pallas_call(down_forward_kernel, name='down_forward', out_shape=(shape...  31.7 us
    pallas_call x1, Pallas kernels, run_down_backward(): pl.pallas_call(down_backward_kernel, name='down_backward', out_shape=shap...  15.9 us
    all_to_all x2, starting transfers between devices, dp_sum(): parts = lax.all_to_all(both, 'dp', 0, 0, tiled=True)  15.1 us
    all_gather x1, blocking collectives, local(): clips = lax.all_gather(latents, ('x', 'core'), axis=0)  14.6 us
    ppermute x6, starting transfers between devices, from_segment(): lax.ppermute(value, 'segment', [((i + away) % SEGS, i) for i in range(SEG...  8.77 us
    all_to_all x2, waiting for transfers between devices, dp_sum(): parts = lax.all_to_all(both, 'dp', 0, 0, tiled=True)  7.08 us
    ppermute x8, waiting for transfers between devices, swap_core(): return lax.ppermute(value, 'core', [(0, 1), (1, 0)])  4.04 us
  transfers between devices with their start and end apart: 16, of which 7 were waited for; matrix products, arithmetic and copies ran while one was open for 8% of the time, Pallas kernels for 26%

profile of v2, /device:TPU:1, one launch (start us, length us, event | category | flops | bytes accessed | tf_op | source)
XLA Modules:
  0.0 181.8 jit_solution(13255841770692669382)
XLA Ops:
  0.6 1.0 constant_dynamic-slice_fusion.2
  1.7 3.6 %collective-permute-start = (bf16[480,320]{1,0:T(8,128)(2,1)S(1)}, bf16[480,320]{1,0:T(8,128)(2,1)S(1)}, u32[]{:S(2)}, u32[]{:S(2)}) collective-permute-start(bf16[480,320]{1,0:T(8,128)(2,1)S(1)} %constant_dynamic-slice_fusion.2), channel_id=1, source_target_pairs={{8,0},{16,8},{24,16},{0,24},{9,1},{17,9},{25,17},{1,25},{10,2},{18... | collective-permute-start | bytes 921608 | tf_op jit(solution)/shard_map/ppermute | solution.py:573
  5.3 1.6 collective-permute-start.2
  7.0 1.2 dynamic_slice.35
  9.1 14.6 %all-gather = bf16[16,2,4,64]{3,2,1,0:T(4,128)(2,1)S(1)} all-gather(bf16[2,2,4,64]{3,2,1,0:T(4,128)(2,1)} %param.11), channel_id=2, replica_groups=mesh['dp'=8,'segment'=4,'x'=4,'core'=2] {'x','core'}, dimensions={0}, use_global_device_ids=true | all-gather | bytes 18432 | tf_op jit(solution)/shard_map/all_gather | solution.py:647
  24.0 1.2 dynamic_slice.37
  25.3 0.9 dynamic-slice_bitcast_fusion.1
  26.9 0.8 add_convert_fusion
  27.7 0.8 copy.38
  29.9 1.1 dynamic-slice_bitcast_fusion
  34.1 0.8 collective-permute-start.4
  34.9 1.9 %collective-permute-start.5 = (bf16[4,160,640]{2,1,0:T(8,128)(2,1)S(1)}, bf16[4,160,640]{2,1,0:T(8,128)(2,1)}, u32[]{:S(2)}, u32[]{:S(2)}) collective-permute-start(bf16[4,160,640]{2,1,0:T(8,128)(2,1)S(1)} %pad_maximum_fusion), channel_id=1, source_target_pairs={{16,0},{24,8},{0,16},{8,24},{17,1},{25,9},{1,17},{9,25},{18,2},{26... | collective-permute-start | bytes 2457608 | tf_op jit(solution)/shard_map/ppermute | solution.py:573
  37.6 0.8 broadcast_in_dim.19.emb
  38.4 31.7 %down_forward.1 = (bf16[5,320,1024]{2,1,0:T(8,128)(2,1)}, f32[4,320,128]{2,1,0:T(8,128)}, f32[4,320,128]{2,1,0:T(8,128)}, bf16[80,1024]{1,0:T(8,128)(2,1)}, bf16...) custom-call(s32[2]{0:T(128)} %pad_add_fusion.ids, ...), custom_call_target="tpu_custom_call" | custom-call | flops 20000000000 | tf_op jit(solution)/shard_map/down_forward/pallas_call | solution.py:463
  70.1 2.3 %collective-permute-done.5.p2 = bf16[4,160,640]{2,1,0:T(8,128)(2,1)} collective-permute-done((bf16[4,160,640]{2,1,0:T(8,128)(2,1)S(1)}, bf16[4,160,640]{2,1,0:T(8,128)(2,1)}, u32[]{:S(2)}, u32[]{:S(2)}) %collective-permute-start.5) | collective-permute-done | bytes 819232 | tf_op jit(solution)/shard_map/ppermute | solution.py:573
  72.4 1.2 collective-permute-start.9
  74.1 0.8 copy.39.out_wide
  75.6 0.9 fusion.7.pick
  76.7 1.2 collective-permute-done.10.q1
  78.3 53.0 %up_both.1 = (f32[160,1280]{1,0:T(8,128)}, bf16[4,320,1024]{2,1,0:T(8,128)(2,1)}, bf16[320,1024]{1,0:T(8,128)(2,1)}) custom-call(s32[2]{0:T(128)} %pad_add_fusion.ids, bf16[5,320,1024]{2,1,0:T(8,128)(2,1)} %get-tuple-element.31.xs, f32[4,320,128]{2,1,0:T(8,128)} %get-tuple-element.36.dmean, f32[4,320,128]{2,1,0:T(8,128)} %get-tuple-element.37.drstd, ...), custom_call_target="tpu_custom_call" | custom-call | flops 49999998976 | tf_op jit(solution)/shard_map/up_both/pallas_call | solution.py:491
  131.3 1.0 constant_dynamic-slice_fusion.1
  132.8 1.4 collective-permute-done.12
  134.2 1.0 dynamic-slice_add_fusion
  135.4 1.0 all_to_all.12
  136.4 8.2 %all-to-all-start = ((f32[8,1,12800]{2,1,0:T(1,128)}), f32[8,1,12800]{2,1,0:T(1,128)S(1)}, u32[]{:S(2)}, u32[]{:S(2)}) async-start(f32[8,1,12800]{2,1,0:T(1,128)} %all_to_all.12), calls=%async_computation | async-start | bytes 819200 | tf_op jit(solution)/shard_map/all_to_all | solution.py:588
  144.6 15.9 %down_backward.1 = f32[80,960]{1,0:T(8,128)} custom-call(s32[2]{0:T(128)} %pad_add_fusion.ids, bf16[5,320,1024]{2,1,0:T(8,128)(2,1)} %get-tuple-element.31.xs, f32[4,320,128]{2,1,0:T(8,128)} %get-tuple-element.32.mean, f32[4,320,128]{2,1,0:T(8,128)} %get-tuple-element.33.rstd, bf16[80,1024]{1,0:T(8,128)(2,1)} %get-tuple-element.34.asel, ...), custom_call_target="tpu_custom_call" | custom-call | flops 15000000512 | tf_op jit(solution)/shard_map/down_backward/pallas_call | solution.py:525
  160.8 0.9 constant_dynamic-slice_fusion
  162.6 0.9 collective-permute-done.13
  163.5 0.9 dynamic-slice_add_fusion.1
  164.5 0.9 all_to_all.16
  165.3 6.9 %all-to-all-start.1 = ((f32[8,1,4800]{2,1,0:T(1,128)}), f32[8,1,4800]{2,1,0:T(1,128)S(1)}, u32[]{:S(2)}, u32[]{:S(2)}) async-start(f32[8,1,4800]{2,1,0:T(1,128)} %all_to_all.16), calls=%async_computation.1 | async-start | bytes 311296 | tf_op jit(solution)/shard_map/all_to_all | solution.py:588
  173.6 7.1 %all-to-all-done.1 = f32[8,1,4800]{2,1,0:T(1,128)S(1)} async-done(((f32[8,1,4800]{2,1,0:T(1,128)}), f32[8,1,4800]{2,1,0:T(1,128)S(1)}, u32[]{:S(2)}, u32[]{:S(2)}) %all-to-all-start.1) | async-done | bytes 153632 | tf_op jit(solution)/shard_map/all_to_all | solution.py:588
  (85 shorter events, 11.3 us)
Async XLA Ops:
  1.7 29.4 %collective-permute-start = (bf16[480,320]{1,0:T(8,128)(2,1)S(1)}, bf16[480,320]{1,0:T(8,128)(2,1)S(1)}, u32[]{:S(2)}, u32[]{:S(2)}) collective-permute-start(bf16[480,320]{1,0:T(8,128)(2,1)S(1)} %constant_dynamic-slice_fusion.2), channel_id=1, source_target_pairs={{8,0},{16,8},{24,16},{0,24},{9,1},{17,9},{25,17},{1,25},{10,2},{18... | collective-permute-start | bytes 921608 | tf_op jit(solution)/shard_map/ppermute | solution.py:573
  5.3 25.8 %collective-permute-start.1 = (bf16[480,320]{1,0:T(8,128)(2,1)S(1)}, bf16[480,320]{1,0:T(8,128)(2,1)}, u32[]{:S(2)}, u32[]{:S(2)}) collective-permute-start(bf16[480,320]{1,0:T(8,128)(2,1)S(1)} %constant_dynamic-slice_fusion.2), channel_id=1, source_target_pairs={{24,0},{0,8},{8,16},{16,24},{25,1},{1,9},{9,17},{17,25},{26,2},{2,... | collective-permute-start | bytes 921608 | tf_op jit(solution)/shard_map/ppermute | solution.py:573
  5.3 25.8 %collective-permute-start.2 = (bf16[480,320]{1,0:T(8,128)(2,1)S(1)}, bf16[480,320]{1,0:T(8,128)(2,1)}, u32[]{:S(2)}, u32[]{:S(2)}) collective-permute-start(bf16[480,320]{1,0:T(8,128)(2,1)S(1)} %constant_dynamic-slice_fusion.2), channel_id=1, source_target_pairs={{16,0},{24,8},{0,16},{8,24},{17,1},{25,9},{1,17},{9,25},{18,2},{26... | collective-permute-start | bytes 921608 | tf_op jit(solution)/shard_map/ppermute | solution.py:573
  31.1 7.3 %copy-start.4 = (bf16[480,320]{1,0:T(8,128)(2,1)}, bf16[480,320]{1,0:T(8,128)(2,1)S(1)}, u32[]{:S(2)}) copy-start(bf16[480,320]{1,0:T(8,128)(2,1)S(1)} %collective-permute-done.p0) | copy-start | bytes 921604
  31.1 3.8 %collective-permute-start.6 = (bf16[480,320]{1,0:T(8,128)(2,1)S(1)}, bf16[480,320]{1,0:T(8,128)(2,1)S(1)}, u32[]{:S(2)}, u32[]{:S(2)}) collective-permute-start(bf16[480,320]{1,0:T(8,128)(2,1)S(1)} %collective-permute-done.p0), channel_id=1, source_target_pairs={{0,1},{1,0},{2,3},{3,2},{4,5},{5,4},{6,7},{7,6},{8,9},{9,8},{10,11... | collective-permute-start | bytes 921608 | tf_op jit(solution)/shard_map/ppermute | solution.py:569
  31.4 5.4 %collective-permute-start.7 = (bf16[480,320]{1,0:T(8,128)(2,1)}, bf16[480,320]{1,0:T(8,128)(2,1)S(1)}, u32[]{:S(2)}, u32[]{:S(2)}) collective-permute-start(bf16[480,320]{1,0:T(8,128)(2,1)} %collective-permute-done.1.p1), channel_id=1, source_target_pairs={{0,1},{1,0},{2,3},{3,2},{4,5},{5,4},{6,7},{7,6},{8,9},{9,8},{10,11... | collective-permute-start | bytes 921608 | tf_op jit(solution)/shard_map/ppermute | solution.py:569
  31.7 5.1 %collective-permute-start.8 = (bf16[480,320]{1,0:T(8,128)(2,1)}, bf16[480,320]{1,0:T(8,128)(2,1)S(1)}, u32[]{:S(2)}, u32[]{:S(2)}) collective-permute-start(bf16[480,320]{1,0:T(8,128)(2,1)} %collective-permute-done.2.p2), channel_id=1, source_target_pairs={{0,1},{1,0},{2,3},{3,2},{4,5},{5,4},{6,7},{7,6},{8,9},{9,8},{10,11... | collective-permute-start | bytes 921608 | tf_op jit(solution)/shard_map/ppermute | solution.py:569
  33.3 36.8 %collective-permute-start.3 = (bf16[4,160,640]{2,1,0:T(8,128)(2,1)S(1)}, bf16[4,160,640]{2,1,0:T(8,128)(2,1)S(1)}, u32[]{:S(2)}, u32[]{:S(2)}) collective-permute-start(bf16[4,160,640]{2,1,0:T(8,128)(2,1)S(1)} %pad_maximum_fusion), channel_id=1, source_target_pairs={{8,0},{16,8},{24,16},{0,24},{9,1},{17,9},{25,17},{1,25},{10,2},{18... | collective-permute-start | bytes 2457608 | tf_op jit(solution)/shard_map/ppermute | solution.py:573
  34.1 36.0 %collective-permute-start.4 = (bf16[4,160,640]{2,1,0:T(8,128)(2,1)S(1)}, bf16[4,160,640]{2,1,0:T(8,128)(2,1)S(1)}, u32[]{:S(2)}, u32[]{:S(2)}) collective-permute-start(bf16[4,160,640]{2,1,0:T(8,128)(2,1)S(1)} %pad_maximum_fusion), channel_id=1, source_target_pairs={{24,0},{0,8},{8,16},{16,24},{25,1},{1,9},{9,17},{17,25},{26,2},{2,... | collective-permute-start | bytes 2457608 | tf_op jit(solution)/shard_map/ppermute | solution.py:573
  34.9 3.5 %copy-start.5 = (bf16[480,320]{1,0:T(8,128)(2,1)}, bf16[480,320]{1,0:T(8,128)(2,1)S(1)}, u32[]{:S(2)}) copy-start(bf16[480,320]{1,0:T(8,128)(2,1)S(1)} %collective-permute-done.6.q0) | copy-start | bytes 921604
  34.9 37.5 %collective-permute-start.5 = (bf16[4,160,640]{2,1,0:T(8,128)(2,1)S(1)}, bf16[4,160,640]{2,1,0:T(8,128)(2,1)}, u32[]{:S(2)}, u32[]{:S(2)}) collective-permute-start(bf16[4,160,640]{2,1,0:T(8,128)(2,1)S(1)} %pad_maximum_fusion), channel_id=1, source_target_pairs={{16,0},{24,8},{0,16},{8,24},{17,1},{25,9},{1,17},{9,25},{18,2},{26... | collective-permute-start | bytes 2457608 | tf_op jit(solution)/shard_map/ppermute | solution.py:573
  36.8 1.6 copy-start.6
  36.8 0.8 copy-start.7
  38.4 35.7 %copy-start = (bf16[320,4]{0,1:T(4,128)(2,1)S(1)}, bf16[320,4]{0,1:T(4,128)(2,1)}, u32[]{:S(2)}) copy-start(bf16[320,4]{0,1:T(4,128)(2,1)} %param.15) | copy-start | bytes 7684
  70.1 8.2 %copy-start.1 = (bf16[4,160,640]{2,1,0:T(8,128)(2,1)}, bf16[4,160,640]{2,1,0:T(8,128)(2,1)S(1)}, u32[]{:S(2)}) copy-start(bf16[4,160,640]{2,1,0:T(8,128)(2,1)S(1)} %collective-permute-done.3.p0) | copy-start | bytes 2457604
  70.1 8.2 %copy-start.2 = (bf16[4,160,640]{2,1,0:T(8,128)(2,1)}, bf16[4,160,640]{2,1,0:T(8,128)(2,1)S(1)}, u32[]{:S(2)}) copy-start(bf16[4,160,640]{2,1,0:T(8,128)(2,1)S(1)} %collective-permute-done.4.p1) | copy-start | bytes 2457604
  72.4 4.3 %collective-permute-start.9 = (bf16[4,160,640]{2,1,0:T(8,128)(2,1)S(1)}, bf16[4,160,640]{2,1,0:T(8,128)(2,1)S(1)}, u32[]{:S(2)}, u32[]{:S(2)}) collective-permute-start(bf16[4,160,640]{2,1,0:T(8,128)(2,1)S(1)} %collective-permute-done.3.p0), channel_id=1, source_target_pairs={{0,1},{1,0},{2,3},{3,2},{4,5},{5,4},{6,7},{7,6},{8,9},{9,8},{10,11... | collective-permute-start | bytes 2457608 | tf_op jit(solution)/shard_map/ppermute | solution.py:569
  73.6 4.3 %collective-permute-start.10 = (bf16[4,160,640]{2,1,0:T(8,128)(2,1)S(1)}, bf16[4,160,640]{2,1,0:T(8,128)(2,1)}, u32[]{:S(2)}, u32[]{:S(2)}) collective-permute-start(bf16[4,160,640]{2,1,0:T(8,128)(2,1)S(1)} %collective-permute-done.4.p1), channel_id=1, source_target_pairs={{0,1},{1,0},{2,3},{3,2},{4,5},{5,4},{6,7},{7,6},{8,9},{9,8},{10,11... | collective-permute-start | bytes 2457608 | tf_op jit(solution)/shard_map/ppermute | solution.py:569
  73.6 4.6 %collective-permute-start.11 = (bf16[4,160,640]{2,1,0:T(8,128)(2,1)}, bf16[4,160,640]{2,1,0:T(8,128)(2,1)}, u32[]{:S(2)}, u32[]{:S(2)}) collective-permute-start(bf16[4,160,640]{2,1,0:T(8,128)(2,1)} %collective-permute-done.5.p2), channel_id=1, source_target_pairs={{0,1},{1,0},{2,3},{3,2},{4,5},{5,4},{6,7},{7,6},{8,9},{9,8},{10,11... | collective-permute-start | bytes 2457608 | tf_op jit(solution)/shard_map/ppermute | solution.py:569
  76.7 1.6 copy-start.3
  132.4 1.9 %collective-permute-start.12 = (f32[80,1280]{1,0:T(8,128)S(1)}, f32[80,1280]{1,0:T(8,128)S(1)}, u32[]{:S(2)}, u32[]{:S(2)}) collective-permute-start(f32[80,1280]{1,0:T(8,128)S(1)} %constant_dynamic-slice_fusion.1), channel_id=1, source_target_pairs={{0,1},{1,0},{2,3},{3,2},{4,5},{5,4},{6,7},{7,6},{8,9},{9,8},{10,11... | collective-permute-start | bytes 1228808 | tf_op jit(solution)/shard_map/ppermute | solution.py:569
  136.4 24.1 %all-to-all-start = ((f32[8,1,12800]{2,1,0:T(1,128)}), f32[8,1,12800]{2,1,0:T(1,128)S(1)}, u32[]{:S(2)}, u32[]{:S(2)}) async-start(f32[8,1,12800]{2,1,0:T(1,128)} %all_to_all.12), calls=%async_computation | async-start | bytes 819200 | tf_op jit(solution)/shard_map/all_to_all | solution.py:588
  161.8 1.8 collective-permute-start.13
  165.3 15.4 %all-to-all-start.1 = ((f32[8,1,4800]{2,1,0:T(1,128)}), f32[8,1,4800]{2,1,0:T(1,128)S(1)}, u32[]{:S(2)}, u32[]{:S(2)}) async-start(f32[8,1,4800]{2,1,0:T(1,128)} %all_to_all.16), calls=%async_computation.1 | async-start | bytes 311296 | tf_op jit(solution)/shard_map/all_to_all | solution.py:588

commit v3 on v2

--- a/solution.py
+++ b/solution.py
@@ -115,7 +115,7 @@
         q_scr[rows, :] = square
         return carry
 
-    lax.fori_loop(0, CH // ROWS, body, 0)
+    lax.fori_loop(0, CH // ROWS, body, 0, unroll=True)
     mid = m_scr[...]
     (mean,) = group_sums(group, [mid], 3)
     mean = mean * (1.0 / (8 * size))
@@ -167,7 +167,7 @@
         q_scr[rows, :] = s2
         return carry
 
-    lax.fori_loop(0, CH // ROWS, first, 0)
+    lax.fori_loop(0, CH // ROWS, first, 0, unroll=True)
     s1, s2 = group_sums(group, [m_scr[...], q_scr[...]], 2)
     scale = 1.0 / (64 * size)
     m_scr[...] = s1 * scale
@@ -185,7 +185,7 @@
             emit(rows, tile(j), rstd * (ga_ref[grows, tile(j)] - m1 - xhat * m2))
         return carry
 
-    lax.fori_loop(0, CH // ROWS, second, 0)
+    lax.fori_loop(0, CH // ROWS, second, 0, unroll=True)
 
 
 MAIN = 256
@@ -239,7 +239,7 @@
             put(rows, tile(j), silu_parts(y)[1].astype(BF))
         return carry
 
-    lax.fori_loop(0, CH // ROWS, act, 0)
+    lax.fori_loop(0, CH // ROWS, act, 0, unroll=True)
 
 
 def down_forward_kernel(
@@ -329,7 +329,7 @@
             fetch(s - 1)
 
         x_at = lambda rows, cols: es[s + 1, rows, cols].astype(F32)
-        gn_stats(x_at, g20[...], 20, m_scr, q_scr, emean.at[s], erstd.at[s])
+        gn_stats(x_at, g20[...], 20, m_scr.at[0], q_scr.at[0], emean.at[s], erstd.at[s])
 
         def put(rows, cols, a):
             stack[slot, 1, 0, rows, cols] = a
@@ -366,7 +366,7 @@
             gcur[rows, tile(j)] = total.astype(BF)
         return carry
 
-    lax.fori_loop(0, CH // ROWS, seed, 0)
+    lax.fori_loop(0, CH // ROWS, seed, 0, unroll=True)
 
     def backward(s, carry):
         for k in range(3):
@@ -399,8 +399,8 @@
 
         e_at = lambda rows, cols: es[s + 1, rows, cols].astype(F32)
         d_at = lambda rows, cols: xs[s + 1, rows, cols].astype(F32)
-        norm_bwd(ga, 0, e_at, g20[...], 20, emean.at[s], erstd.at[s], None, m_scr, q_scr, emit_e)
-        norm_bwd(ga, CH, d_at, g20[...], 20, dmean.at[s], drstd.at[s], None, m_scr, q_scr, emit_d)
+        norm_bwd(ga, 0, e_at, g20[...], 20, emean.at[s], erstd.at[s], None, m_scr.at[0], q_scr.at[0], emit_e)
+        norm_bwd(ga, CH, d_at, g20[...], 20, dmean.at[s], drstd.at[s], None, m_scr.at[1], q_scr.at[1], emit_d)
         return carry
 
     lax.fori_loop(0, SEGS, backward, 0)
@@ -511,8 +511,8 @@
             pltpu.VMEM((2 * CH, TOK), F32),
             pltpu.VMEM((CH, TOK), BF),
             pltpu.VMEM((3 * CH, TOK), BF),
-            pltpu.VMEM((CH, LANES), F32),
-            pltpu.VMEM((CH, LANES), F32),
+            pltpu.VMEM((2, CH, LANES), F32),
+            pltpu.VMEM((2, CH, LANES), F32),
             pltpu.SemaphoreType.DMA((SEGS,)),
             pltpu.SemaphoreType.DMA((2, 4)),
         ],
@@ -542,12 +542,12 @@
     )(*args)
 
 
-def pick_matrix(x_index, per_device, channels):
+def pick_matrix(x_index, core, per_device, channels):
     row = lax.broadcasted_iota(jnp.int32, (16 * per_device, channels), 0)
     col = lax.broadcasted_iota(jnp.int32, (16 * per_device, channels), 1)
-    core = row // (8 * per_device)
+    place = core ^ (row // (8 * per_device))
     dp = (row // per_device) % 8
-    want = (dp * 8 + 2 * x_index + core) * per_device + row % per_device
+    want = (dp * 8 + 2 * x_index + place) * per_device + row % per_device
     return (col == want).astype(BF)
 
 
@@ -577,16 +577,8 @@
     return [from_segment(half, away) for away in (1, 3, 2)]
 
 
-def cores_sum(total, core, rows):
-    size = 8 * rows
-    keep = lax.dynamic_slice_in_dim(total, core * size, size, 0)
-    give = lax.dynamic_slice_in_dim(total, (1 - core) * size, size, 0)
-    return (keep + swap_core(give)).reshape(8, -1)
-
-
-def dp_sum(both, rows):
-    parts = lax.all_to_all(both, "dp", 0, 0, tiled=True)
-    return jnp.sum(parts, axis=0).reshape(rows, -1)
+def cores_sum(total):
+    return (total[0] + swap_core(total[1])).reshape(8, -1)
 
 
 def taps(value):
@@ -609,8 +601,8 @@
     g10 = jnp.asarray(group_matrix(10), BF)
     g20 = jnp.asarray(group_matrix(20), BF)
     shift = jnp.asarray(shift_matrix(), BF)
-    pick_d = pick_matrix(x_index, 5, CH)
-    pick_u = pick_matrix(x_index, 10, 2 * CH)
+    pick_d = pick_matrix(x_index, ids[1], 5, CH)
+    pick_u = pick_matrix(x_index, ids[1], 10, 2 * CH)
     xs, mean, rstd, asel, wnat, dstack, dmean, drstd = run_down_forward(
         ids, noisy, in_t, emb, g10, g20, shift, pick_d, *down()
     )
@@ -619,9 +611,24 @@
         ids, xs, dmean, drstd, g20, shift, pick_u, out_t, out_weight.astype(F32), noise, dstack, *up_args,
         scale=64.0 / math.sqrt(16 * FRAMES * 4 * 64),
     )
-    up_part, kgrad = reduce_up(gu, kgrad)
+    up_part = reduce_up(gu)
     gd = run_down_backward(ids, xs, mean, rstd, asel, wnat, emb, g10, shift, kgrad, cgrad)
     return gd, up_part
+
+
+def whole_clip(latents, core, x_index):
+    own = lax.dynamic_index_in_dim(latents, core, 0, keepdims=False)
+    got = swap_core(lax.dynamic_index_in_dim(latents, 1 - core, 0, keepdims=False))
+    half = lax.broadcasted_iota(jnp.int32, (2,) + own.shape, 0)
+    quad = jnp.where(half == core, own[None], got[None])
+    quads = [quad] + [
+        lax.ppermute(quad, "x", [((i + away) % 4, i) for i in range(4)]) for away in (1, 2, 3)
+    ]
+    away = (lax.broadcasted_iota(jnp.int32, (4,) + quad.shape, 0) - x_index) & 3
+    whole = quads[3][None]
+    for i in (2, 1, 0):
+        whole = jnp.where(away == i, quads[i][None], whole)
+    return whole.reshape((FRAMES,) + own.shape[1:])
 
 
 def local(latents, timesteps, seeds, in_weight, out_weight, down_weight, up_weight, skip_weight):
@@ -644,9 +651,7 @@
     *d_mine, u_half = lax.optimization_barrier((*d_mine, u_half))
     u_mine = fetch_sections(u_half)
 
-    clips = lax.all_gather(latents, ("x", "core"), axis=0)
-    clip = lax.dynamic_index_in_dim(clips, core, 1, keepdims=False)
-    clip = jnp.transpose(clip.reshape(FRAMES, 4, 64), (1, 2, 0))
+    clip = jnp.transpose(whole_clip(latents, core, x_index), (1, 2, 0))
     step_value = lax.dynamic_index_in_dim(timesteps, core, 0, keepdims=False)
     seed_value = lax.dynamic_index_in_dim(seeds, core, 0, keepdims=False)
 
@@ -657,15 +662,17 @@
         *parts, xs = lax.optimization_barrier((*u_mine, xs))
         return xs, [up_t, skip_t, *parts, *[swap_core(p) for p in parts]]
 
-    def reduce_up(gu, kgrad):
-        return lax.optimization_barrier((cores_sum(gu, core, 10), kgrad))
+    def reduce_up(gu):
+        return cores_sum(gu.reshape(2, UP_SEL // 2, 4 * CH))
 
     gd, up_part = clip_gradients(
         ids, clip, step_value, seed_value, x_index, in_weight, out_weight, down, up, reduce_up
     )
-    up_sum = dp_sum(up_part, 10)
-    gd, up_sum = lax.optimization_barrier((gd, up_sum))
-    down_sum = taps(dp_sum(cores_sum(gd, core, 5), 5))
+    down_part = cores_sum(gd.reshape(2, DOWN_SEL // 2, 3 * CH))
+    parts = lax.all_to_all(jnp.concatenate([down_part, up_part], axis=1), "dp", 0, 0, tiled=True)
+    total = jnp.sum(parts, axis=0)
+    down_sum = taps(total[: down_part.shape[1]].reshape(5, -1))
+    up_sum = total[down_part.shape[1] :].reshape(10, -1)
     return down_sum[None], taps(up_sum[:, : 3 * CH])[None], up_sum[:, 3 * CH :][None]
 
 

time: 183 us -> 165 us (0.902)
  Pallas kernels: 101 us -> 84.7 us
  blocking collectives: 14.6 us -> 26.3 us
  starting transfers between devices: 27.6 us -> 19.4 us
  local copies, waits for them, and re-layouts: 17.2 us -> 15 us
  waiting for transfers between devices: 13.5 us -> 11.4 us
    all_to_all x0 -> x1, blocking collectives: none -> 26.3 us  [local(): lax.all_to_all(jnp.concatenate([down_part, up_part], axis=1), 'dp', 0, 0,...]
    all_to_all x2 -> x0, starting transfers between devices: 15.1 us -> none  [dp_sum(): parts = lax.all_to_all(both, 'dp', 0, 0, tiled=True)]
    all_gather x1 -> x0, blocking collectives: 14.6 us -> none  [local(): clips = lax.all_gather(latents, ('x', 'core'), axis=0)]
    pallas_call x1, Pallas kernels: 53 us -> 44 us  [run_up(): pl.pallas_call(functools.partial(up_kernel, scale=scale), name='up_both',...]
    all_to_all x2 -> x0, waiting for transfers between devices: 7.08 us -> none  [dp_sum(): parts = lax.all_to_all(both, 'dp', 0, 0, tiled=True)]
    ppermute x6, waiting for transfers between devices: 2.33 us -> 8.65 us  [from_segment(): lax.ppermute(value, 'segment', [((i + away) % SEGS, i) for i in range(SEG...]
    pallas_call x1, Pallas kernels: 31.7 us -> 26.5 us  [run_down_forward(): pl.pallas_call(down_forward_kernel, name='down_forward', out_shape=(shape...]
    ppermute x0 -> x3, starting transfers between devices: none -> 4.85 us  [whole_clip(): lax.ppermute(quad, 'x', [((i + away) % 4, i) for i in range(4)])]
  transfers between devices with their start and end apart: 16 -> 18, of which waited for: 7 -> 4; matrix products, arithmetic and copies ran while one was open for 8% -> 9% of each run, Pallas kernels for 26% -> 25%
where the time goes in v3:
time: 165 us
  Pallas kernels  84.7 us (51%)
  blocking collectives  26.3 us (16%)
  starting transfers between devices  19.4 us (12%)
  local copies, waits for them, and re-layouts  15 us (9%)
  waiting for transfers between devices  11.4 us (7%)
  other arithmetic  5.31 us (3%)
  between operations  2.5 us (2%)
    pallas_call x1, Pallas kernels, run_up(): pl.pallas_call(functools.partial(up_kernel, scale=scale), name='up_both',...  44 us
    pallas_call x1, Pallas kernels, run_down_forward(): pl.pallas_call(down_forward_kernel, name='down_forward', out_shape=(shape...  26.5 us
    all_to_all x1, blocking collectives, local(): lax.all_to_all(jnp.concatenate([down_part, up_part], axis=1), 'dp', 0, 0,...  26.3 us
    pallas_call x1, Pallas kernels, run_down_backward(): pl.pallas_call(down_backward_kernel, name='down_backward', out_shape=shap...  14.2 us
    ppermute x6, starting transfers between devices, from_segment(): lax.ppermute(value, 'segment', [((i + away) % SEGS, i) for i in range(SEG...  9.77 us
    ppermute x6, waiting for transfers between devices, from_segment(): lax.ppermute(value, 'segment', [((i + away) % SEGS, i) for i in range(SEG...  8.65 us
    ppermute x3, starting transfers between devices, whole_clip(): lax.ppermute(quad, 'x', [((i + away) % 4, i) for i in range(4)])  4.85 us
    ppermute x9, starting transfers between devices, swap_core(): return lax.ppermute(value, 'core', [(0, 1), (1, 0)])  4.8 us
  transfers between devices with their start and end apart: 18, of which 4 were waited for; matrix products, arithmetic and copies ran while one was open for 9% of the time, Pallas kernels for 25%

profile of v3, /device:TPU:1, one launch (start us, length us, event | category | flops | bytes accessed | tf_op | source)
XLA Modules:
  0.0 164.6 jit_solution(10477943063879074819)
XLA Ops:
  0.7 1.0 constant_dynamic-slice_fusion
  1.7 3.8 %collective-permute-start.2 = (bf16[480,320]{1,0:T(8,128)(2,1)S(1)}, bf16[480,320]{1,0:T(8,128)(2,1)S(1)}, u32[]{:S(2)}, u32[]{:S(2)}) collective-permute-start(bf16[480,320]{1,0:T(8,128)(2,1)S(1)} %constant_dynamic-slice_fusion), channel_id=1, source_target_pairs={{16,0},{24,8},{0,16},{8,24},{17,1},{25,9},{1,17},{9,25},{18,2},{26... | collective-permute-start | bytes 921608 | tf_op jit(solution)/shard_map/ppermute | solution.py:573
  5.9 2.3 %collective-permute-start = (bf16[480,320]{1,0:T(8,128)(2,1)S(1)}, bf16[480,320]{1,0:T(8,128)(2,1)}, u32[]{:S(2)}, u32[]{:S(2)}) collective-permute-start(bf16[480,320]{1,0:T(8,128)(2,1)S(1)} %constant_dynamic-slice_fusion), channel_id=1, source_target_pairs={{8,0},{16,8},{24,16},{0,24},{9,1},{17,9},{25,17},{1,25},{10,2},{18... | collective-permute-start | bytes 921608 | tf_op jit(solution)/shard_map/ppermute | solution.py:573
  8.2 0.7 dynamic-slice_bitcast_fusion.3
  8.9 1.5 collective-permute-start.6
  10.5 1.2 dynamic_slice.26
  12.5 1.0 dynamic-slice_bitcast_fusion.1
  13.4 1.1 dynamic-slice_bitcast_fusion
  14.8 0.8 fusion.15.pick
  15.7 1.2 collective-permute-start.9
  16.9 2.5 %collective-permute-start.8 = (bf16[2,2,4,64]{3,1,0,2:T(2,128)(2,1)S(1)}, bf16[2,2,4,64]{3,1,0,2:T(2,128)(2,1)S(1)}, u32[]{:S(2)}, u32[]{:S(2)}) collective-permute-start(bf16[2,2,4,64]{3,1,0,2:T(2,128)(2,1)S(1)} %broadcast_select_fusion), channel_id=1, source_target_pairs={{4,0},{6,2},{0,4},{2,6},{5,1},{7,3},{1,5},{3,7},{12,8},{14,10},{8,... | collective-permute-start | bytes 6152 | tf_op jit(solution)/shard_map/ppermute | solution.py:625
  19.4 1.2 collective-permute-start.7
  23.2 0.7 pad.13.in_t
  23.9 0.9 collective-permute-start.10
  25.6 0.8 add_convert_fusion
  27.6 1.1 collective-permute-start.4
  28.8 1.6 collective-permute-start.3
  30.3 0.8 broadcast_in_dim.91.emb
  31.1 26.5 %down_forward.1 = (bf16[5,320,1024]{2,1,0:T(8,128)(2,1)}, f32[4,320,128]{2,1,0:T(8,128)}, f32[4,320,128]{2,1,0:T(8,128)}, bf16[80,1024]{1,0:T(8,128)(2,1)}, bf16...) custom-call(s32[2]{0:T(128)} %pad_add_fusion.ids, ...), custom_call_target="tpu_custom_call" | custom-call | flops 20000000000 | tf_op jit(solution)/shard_map/down_forward/pallas_call | solution.py:463
  57.7 8.6 %collective-permute-done.4.p1 = bf16[4,160,640]{2,1,0:T(8,128)(2,1)S(1)} collective-permute-done((bf16[4,160,640]{2,1,0:T(8,128)(2,1)S(1)}, bf16[4,160,640]{2,1,0:T(8,128)(2,1)S(1)}, u32[]{:S(2)}, u32[]{:S(2)}) %collective-permute-start.4) | collective-permute-done | bytes 819232 | tf_op jit(solution)/shard_map/ppermute | solution.py:573
  67.3 0.8 copy.40.out_wide
  68.8 1.0 fusion.7.pick
  70.1 1.2 collective-permute-done.15.q2
  71.2 44.0 %up_both.1 = (f32[160,1280]{1,0:T(8,128)}, bf16[4,320,1024]{2,1,0:T(8,128)(2,1)}, bf16[320,1024]{1,0:T(8,128)(2,1)}) custom-call(s32[2]{0:T(128)} %pad_add_fusion.ids, bf16[5,320,1024]{2,1,0:T(8,128)(2,1)} %get-tuple-element.27.xs, f32[4,320,128]{2,1,0:T(8,128)} %get-tuple-element.32.dmean, f32[4,320,128]{2,1,0:T(8,128)} %get-tuple-element.33.drstd, ...), custom_call_target="tpu_custom_call" | custom-call | flops 49999998976 | tf_op jit(solution)/shard_map/up_both/pallas_call | solution.py:491
  115.3 1.0 slice.71
  116.3 0.7 collective-permute-start.17
  117.0 14.2 %down_backward.1 = f32[80,960]{1,0:T(8,128)} custom-call(s32[2]{0:T(128)} %pad_add_fusion.ids, bf16[5,320,1024]{2,1,0:T(8,128)(2,1)} %get-tuple-element.27.xs, f32[4,320,128]{2,1,0:T(8,128)} %get-tuple-element.28.mean, f32[4,320,128]{2,1,0:T(8,128)} %get-tuple-element.29.rstd, bf16[80,1024]{1,0:T(8,128)(2,1)} %get-tuple-element.30.asel, ...), custom_call_target="tpu_custom_call" | custom-call | flops 15000000512 | tf_op jit(solution)/shard_map/down_backward/pallas_call | solution.py:525
  131.2 0.9 slice.88
  132.3 1.3 collective-permute-done.16
  133.6 0.9 slice_add_fusion.1
  135.4 26.3 %all_to_all.9 = f32[8,1,17600]{2,1,0:T(1,128)S(1)} all-to-all(f32[8,1,17600]{2,1,0:T(1,128)S(1)} %all_to_all.6), channel_id=1, replica_groups=mesh['dp'=8,'segment'=4,'x'=4,'core'=2] {'dp'}, dimensions={0} | all-to-all | bytes 1126400 | tf_op jit(solution)/shard_map/all_to_all | solution.py:672
  164.0 0.7 copy.45
  (107 shorter events, 9.9 us)
Async XLA Ops:
  0.6 20.7 %copy-start.7 = (s32[2]{0:T(128)S(1)}, s32[2]{0:T(128)}, u32[]{:S(2)}) copy-start(s32[2]{0:T(128)} %param.13) | copy-start | bytes 28
  0.6 21.7 %copy-start.2 = (bf16[4,320]{1,0:T(4,128)(2,1)S(1)}, bf16[4,320]{1,0:T(4,128)(2,1)}, u32[]{:S(2)}) copy-start(bf16[4,320]{1,0:T(4,128)(2,1)} %param.14) | copy-start | bytes 7684
  1.7 17.7 %collective-permute-start.2 = (bf16[480,320]{1,0:T(8,128)(2,1)S(1)}, bf16[480,320]{1,0:T(8,128)(2,1)S(1)}, u32[]{:S(2)}, u32[]{:S(2)}) collective-permute-start(bf16[480,320]{1,0:T(8,128)(2,1)S(1)} %constant_dynamic-slice_fusion), channel_id=1, source_target_pairs={{16,0},{24,8},{0,16},{8,24},{17,1},{25,9},{1,17},{9,25},{18,2},{26... | collective-permute-start | bytes 921608 | tf_op jit(solution)/shard_map/ppermute | solution.py:573
  5.5 18.4 %collective-permute-start.1 = (bf16[480,320]{1,0:T(8,128)(2,1)S(1)}, bf16[480,320]{1,0:T(8,128)(2,1)}, u32[]{:S(2)}, u32[]{:S(2)}) collective-permute-start(bf16[480,320]{1,0:T(8,128)(2,1)S(1)} %constant_dynamic-slice_fusion), channel_id=1, source_target_pairs={{24,0},{0,8},{8,16},{16,24},{25,1},{1,9},{9,17},{17,25},{26,2},{2,... | collective-permute-start | bytes 921608 | tf_op jit(solution)/shard_map/ppermute | solution.py:573
  5.9 18.0 %collective-permute-start = (bf16[480,320]{1,0:T(8,128)(2,1)S(1)}, bf16[480,320]{1,0:T(8,128)(2,1)}, u32[]{:S(2)}, u32[]{:S(2)}) collective-permute-start(bf16[480,320]{1,0:T(8,128)(2,1)S(1)} %constant_dynamic-slice_fusion), channel_id=1, source_target_pairs={{8,0},{16,8},{24,16},{0,24},{9,1},{17,9},{25,17},{1,25},{10,2},{18... | collective-permute-start | bytes 921608 | tf_op jit(solution)/shard_map/ppermute | solution.py:573
  8.9 6.7 %collective-permute-start.6 = (bf16[2,4,64]{2,1,0:T(4,128)(2,1)S(1)}, bf16[2,4,64]{2,1,0:T(4,128)(2,1)S(1)}, u32[]{:S(2)}, u32[]{:S(2)}) collective-permute-start(bf16[2,4,64]{2,1,0:T(4,128)(2,1)S(1)} %get-tuple-element.65), channel_id=1, source_target_pairs={{0,1},{1,0},{2,3},{3,2},{4,5},{5,4},{6,7},{7,6},{8,9},{9,8},{10,11... | collective-permute-start | bytes 3080 | tf_op jit(solution)/shard_map/ppermute | solution.py:569
  15.7 9.2 %collective-permute-start.9 = (bf16[2,2,4,64]{3,1,0,2:T(2,128)(2,1)S(1)}, bf16[2,2,4,64]{3,1,0,2:T(2,128)(2,1)S(1)}, u32[]{:S(2)}, u32[]{:S(2)}) collective-permute-start(bf16[2,2,4,64]{3,1,0,2:T(2,128)(2,1)S(1)} %broadcast_select_fusion), channel_id=1, source_target_pairs={{6,0},{0,2},{2,4},{4,6},{7,1},{1,3},{3,5},{5,7},{14,8},{8,10},{10,... | collective-permute-start | bytes 6152 | tf_op jit(solution)/shard_map/ppermute | solution.py:625
  16.9 8.3 %collective-permute-start.8 = (bf16[2,2,4,64]{3,1,0,2:T(2,128)(2,1)S(1)}, bf16[2,2,4,64]{3,1,0,2:T(2,128)(2,1)S(1)}, u32[]{:S(2)}, u32[]{:S(2)}) collective-permute-start(bf16[2,2,4,64]{3,1,0,2:T(2,128)(2,1)S(1)} %broadcast_select_fusion), channel_id=1, source_target_pairs={{4,0},{6,2},{0,4},{2,6},{5,1},{7,3},{1,5},{3,7},{12,8},{14,10},{8,... | collective-permute-start | bytes 6152 | tf_op jit(solution)/shard_map/ppermute | solution.py:625
  19.4 11.7 %copy-start.6 = (bf16[480,320]{1,0:T(8,128)(2,1)}, bf16[480,320]{1,0:T(8,128)(2,1)S(1)}, u32[]{:S(2)}) copy-start(bf16[480,320]{1,0:T(8,128)(2,1)S(1)} %collective-permute-done.2.p2) | copy-start | bytes 921604
  19.4 5.9 %collective-permute-start.7 = (bf16[2,2,4,64]{3,1,0,2:T(2,128)(2,1)S(1)}, bf16[2,2,4,64]{3,1,0,2:T(2,128)(2,1)S(1)}, u32[]{:S(2)}, u32[]{:S(2)}) collective-permute-start(bf16[2,2,4,64]{3,1,0,2:T(2,128)(2,1)S(1)} %broadcast_select_fusion), channel_id=1, source_target_pairs={{2,0},{4,2},{6,4},{0,6},{3,1},{5,3},{7,5},{1,7},{10,8},{12,10},{14... | collective-permute-start | bytes 6152 | tf_op jit(solution)/shard_map/ppermute | solution.py:625
  23.9 4.9 %collective-permute-start.10 = (bf16[480,320]{1,0:T(8,128)(2,1)}, bf16[480,320]{1,0:T(8,128)(2,1)}, u32[]{:S(2)}, u32[]{:S(2)}) collective-permute-start(bf16[480,320]{1,0:T(8,128)(2,1)} %collective-permute-done.p0), channel_id=1, source_target_pairs={{0,1},{1,0},{2,3},{3,2},{4,5},{5,4},{6,7},{7,6},{8,9},{9,8},{10,11... | collective-permute-start | bytes 921608 | tf_op jit(solution)/shard_map/ppermute | solution.py:569
  24.7 5.6 %collective-permute-start.11 = (bf16[480,320]{1,0:T(8,128)(2,1)}, bf16[480,320]{1,0:T(8,128)(2,1)}, u32[]{:S(2)}, u32[]{:S(2)}) collective-permute-start(bf16[480,320]{1,0:T(8,128)(2,1)} %collective-permute-done.1.p1), channel_id=1, source_target_pairs={{0,1},{1,0},{2,3},{3,2},{4,5},{5,4},{6,7},{7,6},{8,9},{9,8},{10,11... | collective-permute-start | bytes 921608 | tf_op jit(solution)/shard_map/ppermute | solution.py:569
  24.8 5.5 %collective-permute-start.12 = (bf16[480,320]{1,0:T(8,128)(2,1)S(1)}, bf16[480,320]{1,0:T(8,128)(2,1)}, u32[]{:S(2)}, u32[]{:S(2)}) collective-permute-start(bf16[480,320]{1,0:T(8,128)(2,1)S(1)} %collective-permute-done.2.p2), channel_id=1, source_target_pairs={{0,1},{1,0},{2,3},{3,2},{4,5},{5,4},{6,7},{7,6},{8,9},{9,8},{10,11... | collective-permute-start | bytes 921608 | tf_op jit(solution)/shard_map/ppermute | solution.py:569
  27.1 30.6 %collective-permute-start.5 = (bf16[4,160,640]{2,1,0:T(8,128)(2,1)S(1)}, bf16[4,160,640]{2,1,0:T(8,128)(2,1)S(1)}, u32[]{:S(2)}, u32[]{:S(2)}) collective-permute-start(bf16[4,160,640]{2,1,0:T(8,128)(2,1)S(1)} %pad_maximum_fusion), channel_id=1, source_target_pairs={{16,0},{24,8},{0,16},{8,24},{17,1},{25,9},{1,17},{9,25},{18,2},{26... | collective-permute-start | bytes 2457608 | tf_op jit(solution)/shard_map/ppermute | solution.py:573
  27.6 38.7 %collective-permute-start.4 = (bf16[4,160,640]{2,1,0:T(8,128)(2,1)S(1)}, bf16[4,160,640]{2,1,0:T(8,128)(2,1)S(1)}, u32[]{:S(2)}, u32[]{:S(2)}) collective-permute-start(bf16[4,160,640]{2,1,0:T(8,128)(2,1)S(1)} %pad_maximum_fusion), channel_id=1, source_target_pairs={{24,0},{0,8},{8,16},{16,24},{25,1},{1,9},{9,17},{17,25},{26,2},{2,... | collective-permute-start | bytes 2457608 | tf_op jit(solution)/shard_map/ppermute | solution.py:573
  28.8 37.6 %collective-permute-start.3 = (bf16[4,160,640]{2,1,0:T(8,128)(2,1)S(1)}, bf16[4,160,640]{2,1,0:T(8,128)(2,1)}, u32[]{:S(2)}, u32[]{:S(2)}) collective-permute-start(bf16[4,160,640]{2,1,0:T(8,128)(2,1)S(1)} %pad_maximum_fusion), channel_id=1, source_target_pairs={{8,0},{16,8},{24,16},{0,24},{9,1},{17,9},{25,17},{1,25},{10,2},{18... | collective-permute-start | bytes 2457608 | tf_op jit(solution)/shard_map/ppermute | solution.py:573
  31.1 36.2 %copy-start.1 = (bf16[320,4]{0,1:T(4,128)(2,1)S(1)}, bf16[320,4]{0,1:T(4,128)(2,1)}, u32[]{:S(2)}) copy-start(bf16[320,4]{0,1:T(4,128)(2,1)} %param.15) | copy-start | bytes 7684
  57.7 13.6 %copy-start.3 = (bf16[4,160,640]{2,1,0:T(8,128)(2,1)}, bf16[4,160,640]{2,1,0:T(8,128)(2,1)S(1)}, u32[]{:S(2)}) copy-start(bf16[4,160,640]{2,1,0:T(8,128)(2,1)S(1)} %collective-permute-done.5.p2) | copy-start | bytes 2457604
  66.3 4.9 %copy-start.4 = (bf16[4,160,640]{2,1,0:T(8,128)(2,1)}, bf16[4,160,640]{2,1,0:T(8,128)(2,1)S(1)}, u32[]{:S(2)}) copy-start(bf16[4,160,640]{2,1,0:T(8,128)(2,1)S(1)} %collective-permute-done.4.p1) | copy-start | bytes 2457604
  66.3 3.4 %collective-permute-start.13 = (bf16[4,160,640]{2,1,0:T(8,128)(2,1)}, bf16[4,160,640]{2,1,0:T(8,128)(2,1)S(1)}, u32[]{:S(2)}, u32[]{:S(2)}) collective-permute-start(bf16[4,160,640]{2,1,0:T(8,128)(2,1)} %collective-permute-done.3.p0), channel_id=1, source_target_pairs={{0,1},{1,0},{2,3},{3,2},{4,5},{5,4},{6,7},{7,6},{8,9},{9,8},{10,11... | collective-permute-start | bytes 2457608 | tf_op jit(solution)/shard_map/ppermute | solution.py:569
  66.8 3.3 %collective-permute-start.14 = (bf16[4,160,640]{2,1,0:T(8,128)(2,1)S(1)}, bf16[4,160,640]{2,1,0:T(8,128)(2,1)}, u32[]{:S(2)}, u32[]{:S(2)}) collective-permute-start(bf16[4,160,640]{2,1,0:T(8,128)(2,1)S(1)} %collective-permute-done.4.p1), channel_id=1, source_target_pairs={{0,1},{1,0},{2,3},{3,2},{4,5},{5,4},{6,7},{7,6},{8,9},{9,8},{10,11... | collective-permute-start | bytes 2457608 | tf_op jit(solution)/shard_map/ppermute | solution.py:569
  66.9 4.3 %collective-permute-start.15 = (bf16[4,160,640]{2,1,0:T(8,128)(2,1)S(1)}, bf16[4,160,640]{2,1,0:T(8,128)(2,1)}, u32[]{:S(2)}, u32[]{:S(2)}) collective-permute-start(bf16[4,160,640]{2,1,0:T(8,128)(2,1)S(1)} %collective-permute-done.5.p2), channel_id=1, source_target_pairs={{0,1},{1,0},{2,3},{3,2},{4,5},{5,4},{6,7},{7,6},{8,9},{9,8},{10,11... | collective-permute-start | bytes 2457608 | tf_op jit(solution)/shard_map/ppermute | solution.py:569
  69.7 1.5 copy-start.5
  116.3 18.4 %collective-permute-start.17 = (f32[80,1280]{1,0:T(8,128)S(1)}, f32[80,1280]{1,0:T(8,128)S(1)}, u32[]{:S(2)}, u32[]{:S(2)}) collective-permute-start(f32[80,1280]{1,0:T(8,128)S(1)} %slice.71), channel_id=1, source_target_pairs={{0,1},{1,0},{2,3},{3,2},{4,5},{5,4},{6,7},{7,6},{8,9},{9,8},{10,11... | collective-permute-start | bytes 1228808 | tf_op jit(solution)/shard_map/ppermute | solution.py:569
  117.0 17.6 %copy-start = (f32[160,1280]{1,0:T(8,128)S(1)}, f32[160,1280]{1,0:T(8,128)}, u32[]{:S(2)}) copy-start(f32[160,1280]{1,0:T(8,128)} %get-tuple-element.40) | copy-start | bytes 2457604
  132.1 1.5 collective-permute-start.16

commit v4 on v3

--- a/solution.py
+++ b/solution.py
@@ -178,11 +178,11 @@
         grows = pl.ds(pl.multiple_of(ga_off + r * ROWS, ROWS), ROWS)
         mean = mean_at[rows, :]
         rstd = rstd_at[rows, :]
-        m1 = m_scr[rows, :]
-        m2 = q_scr[rows, :]
+        m1 = m_scr[rows, :] * rstd
+        m2 = q_scr[rows, :] * (rstd * rstd)
         for j in range(TILES):
-            xhat = (x_at(rows, tile(j)) - mean) * rstd
-            emit(rows, tile(j), rstd * (ga_ref[grows, tile(j)] - m1 - xhat * m2))
+            away = x_at(rows, tile(j)) - mean
+            emit(rows, tile(j), rstd * ga_ref[grows, tile(j)] - m1 - away * m2)
         return carry
 
     lax.fori_loop(0, CH // ROWS, second, 0, unroll=True)
@@ -226,29 +226,39 @@
                 ).start()
 
 
+def pick_matrix(ids, per_device, channels):
+    row = lax.broadcasted_iota(jnp.int32, (16 * per_device, channels), 0)
+    col = lax.broadcasted_iota(jnp.int32, (16 * per_device, channels), 1)
+    block = (row * 205) >> (10 if per_device == 5 else 11)
+    place = ids[1] ^ (block >> 3)
+    want = ((block & 7) * 8 + 2 * ids[2] + place) * per_device + row - block * per_device
+    return (col == want).astype(F32).astype(BF)
+
+
 def activate(x_at, mean_at, rstd_at, emb_ref, put):
     def act(r, carry):
         rows = row_block(r)
         mu = mean_at[rows, :]
-        rs = rstd_at[rows, :]
-        e = None if emb_ref is None else emb_ref[rows, :]
+        rs = rstd_at[rows, :] * 0.5
+        e = None if emb_ref is None else emb_ref[rows, :] * 0.5
         for j in range(TILES):
-            y = (x_at(rows, tile(j)) - mu) * rs
+            half = (x_at(rows, tile(j)) - mu) * rs
             if e is not None:
-                y = y + e
-            put(rows, tile(j), silu_parts(y)[1].astype(BF))
+                half = half + e
+            put(rows, tile(j), (half + half * jnp.tanh(half)).astype(BF))
         return carry
 
     lax.fori_loop(0, CH // ROWS, act, 0, unroll=True)
 
 
 def down_forward_kernel(
-    ids, noisy, in_t, emb, g10, g20, shift, pick, own, p0, p1, p2, q0, q1, q2,
+    ids, noisy, in_weight, emb, g10, g20, shift, own, p0, p1, p2, q0, q1, q2,
     xs, mean, rstd, asel, wnat, dstack, dmean, drstd,
     wt, stack, m_scr, q_scr, sems,
 ):
     start_down_copies(ids, own, (p0, p1, p2, q0, q1, q2), wnat, sems)
-    xs[0] = dot(in_t[...], noisy[...]).astype(BF)
+    x0 = lax.dot_general(in_weight[...], noisy[...], (((0,), (0,)), ((), ())), preferred_element_type=F32)
+    xs[0] = x0.astype(BF)
 
     def stage(s, carry):
         x_at = lambda rows, cols: xs[s, rows, cols].astype(F32)
@@ -265,7 +275,7 @@
 
         @pl.when(s == ids[0])
         def _():
-            asel[...] = dot(pick[...], stack[1]).astype(BF)
+            asel[...] = dot(pick_matrix(ids, 5, CH), stack[1]).astype(BF)
 
         copy_bytes(wnat.at[s], sems.at[s]).wait()
         for begin in range(0, 3 * CH, LANES):
@@ -305,9 +315,9 @@
 
 
 def up_kernel(
-    ids, xs, dmean, drstd, g20, shift, pick, out_t, out_wide, noise,
+    ids, xs, dmean, drstd, g20, shift, out_t, out_wide, noise,
     dstack, own_up, own_skip, p0, p1, p2, q0, q1, q2,
-    gu, kgrad, cgrad,
+    gu_keep, gu_give, kgrad, cgrad,
     wt, wb, stack, bsel, jsel, es, emean, erstd, ga, thru, gcur, gstack, m_scr, q_scr, sems, dsems, *, scale
 ):
     start_up_copies(ids, own_up, own_skip, (p0, p1, p2, q0, q1, q2), wt, sems)
@@ -345,8 +355,9 @@
 
         @pl.when(s == ids[0])
         def _():
-            bsel[...] = dot(pick[...], stack[slot, 1].reshape(2 * CH, TOK)).astype(BF)
-            jsel[...] = dot(pick[...], stack[slot, 3].reshape(2 * CH, TOK)).astype(BF)
+            pick = pick_matrix(ids, 10, 2 * CH)
+            bsel[...] = dot(pick, stack[slot, 1].reshape(2 * CH, TOK)).astype(BF)
+            jsel[...] = dot(pick, stack[slot, 3].reshape(2 * CH, TOK)).astype(BF)
 
         copy_bytes(wt.at[s], sems.at[s]).wait()
         es[s] = dot(wt[s], stack[slot].reshape(8 * CH, TOK)).astype(BF)
@@ -384,8 +395,10 @@
 
         @pl.when(s == ids[0])
         def _():
-            gu[:, : 3 * CH] = dot_nt(bsel[...], gstack[...])
-            gu[:, 3 * CH :] = dot_nt(jsel[...], gcur[...])
+            for i, gu in enumerate((gu_keep, gu_give)):
+                rows = slice(i * (UP_SEL // 2), (i + 1) * (UP_SEL // 2))
+                gu[:, : 3 * CH] = dot_nt(bsel[rows, :], gstack[...])
+                gu[:, 3 * CH :] = dot_nt(jsel[rows, :], gcur[...])
 
         ga[...] = dot(wb[:, : 3 * CH], gstack[...])
         thru[...] = dot(wb[:, 1024 : 1024 + CH], gcur[...])
@@ -409,7 +422,7 @@
 
 def down_backward_kernel(
     ids, xs, mean, rstd, asel, wnat, emb, g10, shift, kgrad, cgrad,
-    gd,
+    gd_keep, gd_give,
     wb, hstack, hcur, ga, ccur, m_scr, q_scr,
 ):
     ccur[...] = cgrad[...]
@@ -424,7 +437,8 @@
 
         @pl.when(s == ids[0])
         def _():
-            gd[...] = dot_nt(asel[...], hstack[...])
+            for i, gd in enumerate((gd_keep, gd_give)):
+                gd[...] = dot_nt(asel[i * (DOWN_SEL // 2) : (i + 1) * (DOWN_SEL // 2), :], hstack[...])
 
     def stage(i, carry):
         s = SEGS - 1 - i
@@ -473,7 +487,7 @@
             shape((SEGS, CH, LANES), F32),
             shape((SEGS, CH, LANES), F32),
         ),
-        in_specs=[SMEM] + [VMEM] * 7 + [ANY] * 7,
+        in_specs=[SMEM] + [VMEM] * 6 + [ANY] * 7,
         out_specs=(VMEM,) * 8,
         scratch_shapes=[
             pltpu.VMEM((CH, 3 * CH), BF),
@@ -483,7 +497,7 @@
             pltpu.SemaphoreType.DMA((SEGS,)),
         ],
         compiler_params=PARAMS,
-        cost_estimate=cost(20),
+        cost_estimate=cost(1),
     )(*args)
 
 
@@ -492,12 +506,13 @@
         functools.partial(up_kernel, scale=scale),
         name="up_both",
         out_shape=(
-            shape((UP_SEL, 4 * CH), F32),
+            shape((UP_SEL // 2, 4 * CH), F32),
+            shape((UP_SEL // 2, 4 * CH), F32),
             shape((SEGS, CH, TOK)),
             shape((CH, TOK)),
         ),
-        in_specs=[SMEM] + [VMEM] * 9 + [ANY] * 9,
-        out_specs=(VMEM,) * 3,
+        in_specs=[SMEM] + [VMEM] * 8 + [ANY] * 9,
+        out_specs=(VMEM,) * 4,
         scratch_shapes=[
             pltpu.VMEM((SEGS, CH, 8 * CH), BF),
             pltpu.VMEM((2 * CH, 1024 + 384), BF),
@@ -525,9 +540,9 @@
     return pl.pallas_call(
         down_backward_kernel,
         name="down_backward",
-        out_shape=shape((DOWN_SEL, 3 * CH), F32),
+        out_shape=(shape((DOWN_SEL // 2, 3 * CH), F32),) * 2,
         in_specs=[SMEM] + [VMEM] * 10,
-        out_specs=VMEM,
+        out_specs=(VMEM,) * 2,
         scratch_shapes=[
             pltpu.VMEM((CH, 3 * CH), BF),
             pltpu.VMEM((3 * CH, TOK), BF),
@@ -542,27 +557,16 @@
     )(*args)
 
 
-def pick_matrix(x_index, core, per_device, channels):
-    row = lax.broadcasted_iota(jnp.int32, (16 * per_device, channels), 0)
-    col = lax.broadcasted_iota(jnp.int32, (16 * per_device, channels), 1)
-    place = core ^ (row // (8 * per_device))
-    dp = (row // per_device) % 8
-    want = (dp * 8 + 2 * x_index + place) * per_device + row % per_device
-    return (col == want).astype(BF)
-
-
-def clip_inputs(clip, step_value, seed_value, in_weight, out_weight):
+def clip_inputs(clip, step_value, seed_value, out_weight):
     lat_dim, pix_dim, frames = clip.shape
     noise = noise_field(seed_value, lat_dim, pix_dim)
     theta = step_value.astype(F32) * (0.5 * math.pi / 1000.0)
     noisy = (
         jnp.cos(theta) * clip.reshape(lat_dim, pix_dim * frames).astype(F32) + jnp.sin(theta) * noise
     ).astype(BF)
-    noisy = jnp.pad(noisy, ((0, 16 - lat_dim), (0, 0)))
-    in_t = jnp.pad(in_weight.T, ((0, 0), (0, 16 - lat_dim)))
     out_t = jnp.pad(out_weight.T, ((0, 16 - lat_dim), (0, 0)))
     emb = jnp.broadcast_to(time_embedding(step_value, CH)[:, None], (CH, LANES))
-    return noise, noisy, in_t, out_t, emb
+    return noise, noisy, out_t, emb
 
 
 def swap_core(value):
@@ -577,8 +581,8 @@
     return [from_segment(half, away) for away in (1, 3, 2)]
 
 
-def cores_sum(total):
-    return (total[0] + swap_core(total[1])).reshape(8, -1)
+def cores_sum(keep, give):
+    return (keep + swap_core(give)).reshape(8, -1)
 
 
 def taps(value):
@@ -596,46 +600,46 @@
     )
 
 
-def clip_gradients(ids, clip, step_value, seed_value, x_index, in_weight, out_weight, down, up, reduce_up):
-    noise, noisy, in_t, out_t, emb = clip_inputs(clip, step_value, seed_value, in_weight, out_weight)
+def clip_gradients(ids, clip, step_value, seed_value, in_weight, out_weight, down, up, reduce_up):
+    noise, noisy, out_t, emb = clip_inputs(clip, step_value, seed_value, out_weight)
     g10 = jnp.asarray(group_matrix(10), BF)
     g20 = jnp.asarray(group_matrix(20), BF)
     shift = jnp.asarray(shift_matrix(), BF)
-    pick_d = pick_matrix(x_index, ids[1], 5, CH)
-    pick_u = pick_matrix(x_index, ids[1], 10, 2 * CH)
     xs, mean, rstd, asel, wnat, dstack, dmean, drstd = run_down_forward(
-        ids, noisy, in_t, emb, g10, g20, shift, pick_d, *down()
+        ids, noisy, in_weight, emb, g10, g20, shift, *down()
     )
     xs, up_args = up(xs)
-    gu, kgrad, cgrad = run_up(
-        ids, xs, dmean, drstd, g20, shift, pick_u, out_t, out_weight.astype(F32), noise, dstack, *up_args,
+    gu_keep, gu_give, kgrad, cgrad = run_up(
+        ids, xs, dmean, drstd, g20, shift, out_t, out_weight.astype(F32), noise, dstack, *up_args,
         scale=64.0 / math.sqrt(16 * FRAMES * 4 * 64),
     )
-    up_part = reduce_up(gu)
+    up_part = reduce_up(gu_keep, gu_give)
     gd = run_down_backward(ids, xs, mean, rstd, asel, wnat, emb, g10, shift, kgrad, cgrad)
     return gd, up_part
 
 
-def whole_clip(latents, core, x_index):
-    own = lax.dynamic_index_in_dim(latents, core, 0, keepdims=False)
-    got = swap_core(lax.dynamic_index_in_dim(latents, 1 - core, 0, keepdims=False))
+def clip_parts(latents, core):
+    own = jnp.where(core == 0, latents[0], latents[1])
+    got = swap_core(jnp.where(core == 0, latents[1], latents[0]))
     half = lax.broadcasted_iota(jnp.int32, (2,) + own.shape, 0)
     quad = jnp.where(half == core, own[None], got[None])
-    quads = [quad] + [
-        lax.ppermute(quad, "x", [((i + away) % 4, i) for i in range(4)]) for away in (1, 2, 3)
-    ]
+    return [quad] + [lax.ppermute(quad, "x", [((i + away) % 4, i) for i in range(4)]) for away in (1, 2, 3)]
+
+
+def whole_clip(quads, x_index):
+    quad = quads[0]
     away = (lax.broadcasted_iota(jnp.int32, (4,) + quad.shape, 0) - x_index) & 3
     whole = quads[3][None]
     for i in (2, 1, 0):
         whole = jnp.where(away == i, quads[i][None], whole)
-    return whole.reshape((FRAMES,) + own.shape[1:])
+    return whole.reshape((FRAMES,) + quad.shape[2:])
 
 
 def local(latents, timesteps, seeds, in_weight, out_weight, down_weight, up_weight, skip_weight):
     seg = lax.axis_index("segment")
     core = lax.axis_index("core")
     x_index = lax.axis_index("x")
-    ids = jnp.stack([seg, core]).astype(jnp.int32)
+    ids = jnp.stack([seg, core, x_index]).astype(jnp.int32)
     down_nat = down_weight[0].reshape(3 * CH, CH)
     up_t = jnp.transpose(up_weight[0], (0, 2, 1))
     skip_t = skip_weight[0].T
@@ -648,12 +652,14 @@
         axis=0,
     )
     d_mine = fetch_sections(d_half)
-    *d_mine, u_half = lax.optimization_barrier((*d_mine, u_half))
+    quads = clip_parts(latents, core)
+    *moved, u_half = lax.optimization_barrier((*d_mine, *quads, u_half))
+    d_mine, quads = moved[:3], moved[3:]
     u_mine = fetch_sections(u_half)
 
-    clip = jnp.transpose(whole_clip(latents, core, x_index), (1, 2, 0))
-    step_value = lax.dynamic_index_in_dim(timesteps, core, 0, keepdims=False)
-    seed_value = lax.dynamic_index_in_dim(seeds, core, 0, keepdims=False)
+    clip = jnp.transpose(whole_clip(quads, x_index), (1, 2, 0))
+    step_value = jnp.where(core == 0, timesteps[0], timesteps[1])
+    seed_value = jnp.where(core == 0, seeds[0], seeds[1])
 
     def down():
         return [down_nat, *d_mine, *[swap_core(p) for p in d_mine]]
@@ -662,13 +668,10 @@
         *parts, xs = lax.optimization_barrier((*u_mine, xs))
         return xs, [up_t, skip_t, *parts, *[swap_core(p) for p in parts]]
 
-    def reduce_up(gu):
-        return cores_sum(gu.reshape(2, UP_SEL // 2, 4 * CH))
-
     gd, up_part = clip_gradients(
-        ids, clip, step_value, seed_value, x_index, in_weight, out_weight, down, up, reduce_up
+        ids, clip, step_value, seed_value, in_weight, out_weight, down, up, cores_sum
     )
-    down_part = cores_sum(gd.reshape(2, DOWN_SEL // 2, 3 * CH))
+    down_part = cores_sum(*gd)
     parts = lax.all_to_all(jnp.concatenate([down_part, up_part], axis=1), "dp", 0, 0, tiled=True)
     total = jnp.sum(parts, axis=0)
     down_sum = taps(total[: down_part.shape[1]].reshape(5, -1))

time: 165 us -> 161 us (0.976)
  waiting for transfers between devices: 11.4 us -> 6.28 us
  local copies, waits for them, and re-layouts: 15 us -> 11.8 us
  starting transfers between devices: 19.4 us -> 21.7 us
  Pallas kernels: 84.7 us -> 86.5 us
    ppermute x6, waiting for transfers between devices: 8.65 us -> 0.27 us  [from_segment(): lax.ppermute(value, 'segment', [((i + away) % SEGS, i) for i in range(SEG...]
    ppermute x9, starting transfers between devices: 4.8 us -> 6.71 us  [swap_core(): return lax.ppermute(value, 'core', [(0, 1), (1, 0)])]
    ppermute x9, waiting for transfers between devices: 2.78 us -> 4.65 us  [swap_core(): return lax.ppermute(value, 'core', [(0, 1), (1, 0)])]
    dynamic_slice x2 -> x0, local copies, waits for them, and re-layouts: 1.83 us -> none  [the longest x1 1.24 us: local(): step_value = lax.dynamic_index_in_dim(timesteps, core, 0, keepdims=False)]
    convert_element_type x2 -> x0, other arithmetic: 1.75 us -> none  [pick_matrix(): return (col == want).astype(BF)]
  transfers between devices with their start and end apart: 18 -> 18, of which waited for: 4 -> 9; matrix products, arithmetic and copies ran while one was open for 9% -> 7% of each run, Pallas kernels for 25% -> 26%
where the time goes in v4:
time: 161 us; the launch traced here: 160 us
  Pallas kernels  86.5 us (54%)
  blocking collectives  26.3 us (16%)
  starting transfers between devices  21.7 us (13%)
  local copies, waits for them, and re-layouts  11.8 us (7%)
  waiting for transfers between devices  6.28 us (4%)
  other arithmetic  4.12 us (3%)
  between operations  3.76 us (2%)
    pallas_call x1, Pallas kernels, run_up(): pl.pallas_call(functools.partial(up_kernel, scale=scale), name='up_both',...  44.7 us
    pallas_call x1, Pallas kernels, run_down_forward(): pl.pallas_call(down_forward_kernel, name='down_forward', out_shape=(shape...  27.1 us
    all_to_all x1, blocking collectives, local(): lax.all_to_all(jnp.concatenate([down_part, up_part], axis=1), 'dp', 0, 0,...  26.3 us
    pallas_call x1, Pallas kernels, run_down_backward(): pl.pallas_call(down_backward_kernel, name='down_backward', out_shape=(sha...  14.8 us
    ppermute x6, starting transfers between devices, from_segment(): lax.ppermute(value, 'segment', [((i + away) % SEGS, i) for i in range(SEG...  9.96 us
    ppermute x9, starting transfers between devices, swap_core(): return lax.ppermute(value, 'core', [(0, 1), (1, 0)])  6.71 us
    ppermute x3, starting transfers between devices, clip_parts(): lax.ppermute(quad, 'x', [((i + away) % 4, i) for i in range(4)])  5.06 us
    ppermute x9, waiting for transfers between devices, swap_core(): return lax.ppermute(value, 'core', [(0, 1), (1, 0)])  4.65 us
  transfers between devices with their start and end apart: 18, of which 9 were waited for; matrix products, arithmetic and copies ran while one was open for 7% of the time, Pallas kernels for 26%

profile of v4, /device:TPU:1, one launch (start us, length us, event | category | flops | bytes accessed | tf_op | source)
XLA Modules:
  0.0 160.5 jit_solution(4455899255952258197)
XLA Ops:
  0.6 1.0 constant_dynamic-slice_fusion
  1.7 3.8 %collective-permute-start.2 = (bf16[480,320]{1,0:T(8,128)(2,1)S(1)}, bf16[480,320]{1,0:T(8,128)(2,1)S(1)}, u32[]{:S(2)}, u32[]{:S(2)}) collective-permute-start(bf16[480,320]{1,0:T(8,128)(2,1)S(1)} %constant_dynamic-slice_fusion), channel_id=1, source_target_pairs={{16,0},{24,8},{0,16},{8,24},{17,1},{25,9},{1,17},{9,25},{18,2},{26... | collective-permute-start | bytes 921608 | tf_op jit(solution)/shard_map/ppermute | solution.py:577
  5.9 2.3 %collective-permute-start = (bf16[480,320]{1,0:T(8,128)(2,1)S(1)}, bf16[480,320]{1,0:T(8,128)(2,1)}, u32[]{:S(2)}, u32[]{:S(2)}) collective-permute-start(bf16[480,320]{1,0:T(8,128)(2,1)S(1)} %constant_dynamic-slice_fusion), channel_id=1, source_target_pairs={{8,0},{16,8},{24,16},{0,24},{9,1},{17,9},{25,17},{1,25},{10,2},{18... | collective-permute-start | bytes 921608 | tf_op jit(solution)/shard_map/ppermute | solution.py:577
  8.2 0.7 select_bitcast_fusion.1
  8.9 1.5 collective-permute-start.3
  10.4 1.3 fusion.31
  13.0 1.4 fusion.30
  14.5 1.0 dynamic-slice_bitcast_fusion.1
  15.4 1.1 dynamic-slice_bitcast_fusion
  16.9 1.2 collective-permute-start.6
  18.1 2.5 %collective-permute-start.5 = (bf16[2,2,4,64]{3,1,0,2:T(2,128)(2,1)S(1)}, bf16[2,2,4,64]{3,1,0,2:T(2,128)(2,1)S(1)}, u32[]{:S(2)}, u32[]{:S(2)}) collective-permute-start(bf16[2,2,4,64]{3,1,0,2:T(2,128)(2,1)S(1)} %broadcast_select_fusion), channel_id=1, source_target_pairs={{4,0},{6,2},{0,4},{2,6},{5,1},{7,3},{1,5},{3,7},{12,8},{14,10},{8,... | collective-permute-start | bytes 6152 | tf_op jit(solution)/shard_map/ppermute | solution.py:626
  20.9 1.4 collective-permute-start.4
  22.2 1.1 collective-permute-done.4
  23.4 0.8 collective-permute-start.9
  24.1 1.8 %collective-permute-start.8 = (bf16[4,160,640]{2,1,0:T(8,128)(2,1)S(1)}, bf16[4,160,640]{2,1,0:T(8,128)(2,1)S(1)}, u32[]{:S(2)}, u32[]{:S(2)}) collective-permute-start(bf16[4,160,640]{2,1,0:T(8,128)(2,1)S(1)} %pad_maximum_fusion), channel_id=1, source_target_pairs={{24,0},{0,8},{8,16},{16,24},{25,1},{1,9},{9,17},{17,25},{26,2},{2,... | collective-permute-start | bytes 2457608 | tf_op jit(solution)/shard_map/ppermute | solution.py:577
  25.9 0.9 collective-permute-start.7
  26.8 2.7 %collective-permute-start.10 = (bf16[480,320]{1,0:T(8,128)(2,1)}, bf16[480,320]{1,0:T(8,128)(2,1)}, u32[]{:S(2)}, u32[]{:S(2)}) collective-permute-start(bf16[480,320]{1,0:T(8,128)(2,1)} %collective-permute-done.p0), channel_id=1, source_target_pairs={{0,1},{1,0},{2,3},{3,2},{4,5},{5,4},{6,7},{7,6},{8,9},{9,8},{10,11... | collective-permute-start | bytes 921608 | tf_op jit(solution)/shard_map/ppermute | solution.py:573
  33.1 0.8 add_convert_fusion
  34.5 0.8 broadcast_in_dim.91.emb
  35.3 27.1 %down_forward.1 = (bf16[5,320,1024]{2,1,0:T(8,128)(2,1)}, f32[4,320,128]{2,1,0:T(8,128)}, f32[4,320,128]{2,1,0:T(8,128)}, bf16[80,1024]{1,0:T(8,128)(2,1)}, bf16...) custom-call(s32[3]{0:T(128)} %pad_add_fusion.ids, ...), custom_call_target="tpu_custom_call" | custom-call | flops 1000000000 | tf_op jit(solution)/shard_map/down_forward/pallas_call | solution.py:477
  63.7 0.8 copy.38.out_wide
  65.6 0.8 collective-permute-done.14.q1
  66.4 1.2 collective-permute-done.15.q2
  67.6 44.7 %up_both.1 = (f32[80,1280]{1,0:T(8,128)}, f32[80,1280]{1,0:T(8,128)}, bf16[4,320,1024]{2,1,0:T(8,128)(2,1)}, bf16[320,1024]{1,0:T(8,128)(2,1)}) custom-call(s32[3]{0:T(128)} %pad_add_fusion.ids, bf16[5,320,1024]{2,1,0:T(8,128)(2,1)} %get-tuple-element.38.xs, f32[4,320,128]{2,1,0:T(8,128)} %get-tuple-element.43.dmean, ...), custom_call_target="tpu_custom_call" | custom-call | flops 49999998976 | tf_op jit(solution)/shard_map/up_both/pallas_call | solution.py:505
  112.3 0.8 collective-permute-start.17
  113.1 14.8 %down_backward.1 = (f32[40,960]{1,0:T(8,128)}, f32[40,960]{1,0:T(8,128)}) custom-call(s32[3]{0:T(128)} %pad_add_fusion.ids, bf16[5,320,1024]{2,1,0:T(8,128)(2,1)} %get-tuple-element.38.xs, f32[4,320,128]{2,1,0:T(8,128)} %get-tuple-element.39.mean, f32[4,320,128]{2,1,0:T(8,128)} %get-tuple-element.40.rstd, bf16[80,1024]{1,0:T(8,128)(2,1)} %get-tuple-element.41.asel, ...), custom_call_target="tpu_custom_call" | custom-call | flops 15000000512 | tf_op jit(solution)/shard_map/down_backward/pallas_call | solution.py:540
  128.0 1.5 collective-permute-done.16
  129.5 0.9 add.71
  131.3 26.3 %all_to_all.9 = f32[8,1,17600]{2,1,0:T(1,128)S(1)} all-to-all(f32[8,1,17600]{2,1,0:T(1,128)S(1)} %all_to_all.6), channel_id=1, replica_groups=mesh['dp'=8,'segment'=4,'x'=4,'core'=2] {'dp'}, dimensions={0} | all-to-all | bytes 1126400 | tf_op jit(solution)/shard_map/all_to_all | solution.py:675
  158.5 0.6 copy.42
  159.1 0.6 broadcast_in_dim.94
  159.8 0.7 copy.43
  (88 shorter events, 7.9 us)
Async XLA Ops:
  1.7 21.7 %collective-permute-start.2 = (bf16[480,320]{1,0:T(8,128)(2,1)S(1)}, bf16[480,320]{1,0:T(8,128)(2,1)S(1)}, u32[]{:S(2)}, u32[]{:S(2)}) collective-permute-start(bf16[480,320]{1,0:T(8,128)(2,1)S(1)} %constant_dynamic-slice_fusion), channel_id=1, source_target_pairs={{16,0},{24,8},{0,16},{8,24},{17,1},{25,9},{1,17},{9,25},{18,2},{26... | collective-permute-start | bytes 921608 | tf_op jit(solution)/shard_map/ppermute | solution.py:577
  5.5 17.8 %collective-permute-start.1 = (bf16[480,320]{1,0:T(8,128)(2,1)S(1)}, bf16[480,320]{1,0:T(8,128)(2,1)S(1)}, u32[]{:S(2)}, u32[]{:S(2)}) collective-permute-start(bf16[480,320]{1,0:T(8,128)(2,1)S(1)} %constant_dynamic-slice_fusion), channel_id=1, source_target_pairs={{24,0},{0,8},{8,16},{16,24},{25,1},{1,9},{9,17},{17,25},{26,2},{2,... | collective-permute-start | bytes 921608 | tf_op jit(solution)/shard_map/ppermute | solution.py:577
  5.9 17.4 %collective-permute-start = (bf16[480,320]{1,0:T(8,128)(2,1)S(1)}, bf16[480,320]{1,0:T(8,128)(2,1)}, u32[]{:S(2)}, u32[]{:S(2)}) collective-permute-start(bf16[480,320]{1,0:T(8,128)(2,1)S(1)} %constant_dynamic-slice_fusion), channel_id=1, source_target_pairs={{8,0},{16,8},{24,16},{0,24},{9,1},{17,9},{25,17},{1,25},{10,2},{18... | collective-permute-start | bytes 921608 | tf_op jit(solution)/shard_map/ppermute | solution.py:577
  8.9 7.9 %collective-permute-start.3 = (bf16[2,4,64]{2,1,0:T(4,128)(2,1)S(1)}, bf16[2,4,64]{2,1,0:T(4,128)(2,1)S(1)}, u32[]{:S(2)}, u32[]{:S(2)}) collective-permute-start(bf16[2,4,64]{2,1,0:T(4,128)(2,1)S(1)} %get-tuple-element.79), channel_id=1, source_target_pairs={{0,1},{1,0},{2,3},{3,2},{4,5},{5,4},{6,7},{7,6},{8,9},{9,8},{10,11... | collective-permute-start | bytes 3080 | tf_op jit(solution)/shard_map/ppermute | solution.py:573
  16.6 47.0 %copy-start.1 = (bf16[320,4]{0,1:T(4,128)(2,1)S(1)}, bf16[320,4]{0,1:T(4,128)(2,1)}, u32[]{:S(2)}) copy-start(bf16[320,4]{0,1:T(4,128)(2,1)} %param.15) | copy-start | bytes 7684
  16.9 4.0 %collective-permute-start.6 = (bf16[2,2,4,64]{3,1,0,2:T(2,128)(2,1)S(1)}, bf16[2,2,4,64]{3,1,0,2:T(2,128)(2,1)S(1)}, u32[]{:S(2)}, u32[]{:S(2)}) collective-permute-start(bf16[2,2,4,64]{3,1,0,2:T(2,128)(2,1)S(1)} %broadcast_select_fusion), channel_id=1, source_target_pairs={{6,0},{0,2},{2,4},{4,6},{7,1},{1,3},{3,5},{5,7},{14,8},{8,10},{10,... | collective-permute-start | bytes 6152 | tf_op jit(solution)/shard_map/ppermute | solution.py:626
  18.1 4.1 %collective-permute-start.5 = (bf16[2,2,4,64]{3,1,0,2:T(2,128)(2,1)S(1)}, bf16[2,2,4,64]{3,1,0,2:T(2,128)(2,1)S(1)}, u32[]{:S(2)}, u32[]{:S(2)}) collective-permute-start(bf16[2,2,4,64]{3,1,0,2:T(2,128)(2,1)S(1)} %broadcast_select_fusion), channel_id=1, source_target_pairs={{4,0},{6,2},{0,4},{2,6},{5,1},{7,3},{1,5},{3,7},{12,8},{14,10},{8,... | collective-permute-start | bytes 6152 | tf_op jit(solution)/shard_map/ppermute | solution.py:626
  20.9 2.5 %collective-permute-start.4 = (bf16[2,2,4,64]{3,1,0,2:T(2,128)(2,1)S(1)}, bf16[2,2,4,64]{3,1,0,2:T(2,128)(2,1)S(1)}, u32[]{:S(2)}, u32[]{:S(2)}) collective-permute-start(bf16[2,2,4,64]{3,1,0,2:T(2,128)(2,1)S(1)} %broadcast_select_fusion), channel_id=1, source_target_pairs={{2,0},{4,2},{6,4},{0,6},{3,1},{5,3},{7,5},{1,7},{10,8},{12,10},{14... | collective-permute-start | bytes 6152 | tf_op jit(solution)/shard_map/ppermute | solution.py:626
  23.3 12.0 %copy-start.5 = (bf16[480,320]{1,0:T(8,128)(2,1)}, bf16[480,320]{1,0:T(8,128)(2,1)S(1)}, u32[]{:S(2)}) copy-start(bf16[480,320]{1,0:T(8,128)(2,1)S(1)} %collective-permute-done.2.p2) | copy-start | bytes 921604
  23.3 12.0 %copy-start.6 = (bf16[480,320]{1,0:T(8,128)(2,1)}, bf16[480,320]{1,0:T(8,128)(2,1)S(1)}, u32[]{:S(2)}) copy-start(bf16[480,320]{1,0:T(8,128)(2,1)S(1)} %collective-permute-done.1.p1) | copy-start | bytes 921604
  23.4 39.0 %collective-permute-start.9 = (bf16[4,160,640]{2,1,0:T(8,128)(2,1)S(1)}, bf16[4,160,640]{2,1,0:T(8,128)(2,1)S(1)}, u32[]{:S(2)}, u32[]{:S(2)}) collective-permute-start(bf16[4,160,640]{2,1,0:T(8,128)(2,1)S(1)} %pad_maximum_fusion), channel_id=1, source_target_pairs={{16,0},{24,8},{0,16},{8,24},{17,1},{25,9},{1,17},{9,25},{18,2},{26... | collective-permute-start | bytes 2457608 | tf_op jit(solution)/shard_map/ppermute | solution.py:577
  24.1 38.5 %collective-permute-start.8 = (bf16[4,160,640]{2,1,0:T(8,128)(2,1)S(1)}, bf16[4,160,640]{2,1,0:T(8,128)(2,1)S(1)}, u32[]{:S(2)}, u32[]{:S(2)}) collective-permute-start(bf16[4,160,640]{2,1,0:T(8,128)(2,1)S(1)} %pad_maximum_fusion), channel_id=1, source_target_pairs={{24,0},{0,8},{8,16},{16,24},{25,1},{1,9},{9,17},{17,25},{26,2},{2,... | collective-permute-start | bytes 2457608 | tf_op jit(solution)/shard_map/ppermute | solution.py:577
  25.9 36.8 %collective-permute-start.7 = (bf16[4,160,640]{2,1,0:T(8,128)(2,1)S(1)}, bf16[4,160,640]{2,1,0:T(8,128)(2,1)}, u32[]{:S(2)}, u32[]{:S(2)}) collective-permute-start(bf16[4,160,640]{2,1,0:T(8,128)(2,1)S(1)} %pad_maximum_fusion), channel_id=1, source_target_pairs={{8,0},{16,8},{24,16},{0,24},{9,1},{17,9},{25,17},{1,25},{10,2},{18... | collective-permute-start | bytes 2457608 | tf_op jit(solution)/shard_map/ppermute | solution.py:577
  26.8 5.4 %collective-permute-start.10 = (bf16[480,320]{1,0:T(8,128)(2,1)}, bf16[480,320]{1,0:T(8,128)(2,1)}, u32[]{:S(2)}, u32[]{:S(2)}) collective-permute-start(bf16[480,320]{1,0:T(8,128)(2,1)} %collective-permute-done.p0), channel_id=1, source_target_pairs={{0,1},{1,0},{2,3},{3,2},{4,5},{5,4},{6,7},{7,6},{8,9},{9,8},{10,11... | collective-permute-start | bytes 921608 | tf_op jit(solution)/shard_map/ppermute | solution.py:573
  32.1 1.9 %collective-permute-start.11 = (bf16[480,320]{1,0:T(8,128)(2,1)S(1)}, bf16[480,320]{1,0:T(8,128)(2,1)}, u32[]{:S(2)}, u32[]{:S(2)}) collective-permute-start(bf16[480,320]{1,0:T(8,128)(2,1)S(1)} %collective-permute-done.1.p1), channel_id=1, source_target_pairs={{0,1},{1,0},{2,3},{3,2},{4,5},{5,4},{6,7},{7,6},{8,9},{9,8},{10,11... | collective-permute-start | bytes 921608 | tf_op jit(solution)/shard_map/ppermute | solution.py:573
  32.2 2.3 %collective-permute-start.12 = (bf16[480,320]{1,0:T(8,128)(2,1)S(1)}, bf16[480,320]{1,0:T(8,128)(2,1)}, u32[]{:S(2)}, u32[]{:S(2)}) collective-permute-start(bf16[480,320]{1,0:T(8,128)(2,1)S(1)} %collective-permute-done.2.p2), channel_id=1, source_target_pairs={{0,1},{1,0},{2,3},{3,2},{4,5},{5,4},{6,7},{7,6},{8,9},{9,8},{10,11... | collective-permute-start | bytes 921608 | tf_op jit(solution)/shard_map/ppermute | solution.py:573
  62.4 5.2 %copy-start.2 = (bf16[4,160,640]{2,1,0:T(8,128)(2,1)}, bf16[4,160,640]{2,1,0:T(8,128)(2,1)S(1)}, u32[]{:S(2)}) copy-start(bf16[4,160,640]{2,1,0:T(8,128)(2,1)S(1)} %collective-permute-done.9.p2) | copy-start | bytes 2457604
  62.7 4.9 %copy-start.3 = (bf16[4,160,640]{2,1,0:T(8,128)(2,1)}, bf16[4,160,640]{2,1,0:T(8,128)(2,1)S(1)}, u32[]{:S(2)}) copy-start(bf16[4,160,640]{2,1,0:T(8,128)(2,1)S(1)} %collective-permute-done.8.p1) | copy-start | bytes 2457604
  62.7 2.9 %collective-permute-start.13 = (bf16[4,160,640]{2,1,0:T(8,128)(2,1)}, bf16[4,160,640]{2,1,0:T(8,128)(2,1)S(1)}, u32[]{:S(2)}, u32[]{:S(2)}) collective-permute-start(bf16[4,160,640]{2,1,0:T(8,128)(2,1)} %collective-permute-done.7.p0), channel_id=1, source_target_pairs={{0,1},{1,0},{2,3},{3,2},{4,5},{5,4},{6,7},{7,6},{8,9},{9,8},{10,11... | collective-permute-start | bytes 2457608 | tf_op jit(solution)/shard_map/ppermute | solution.py:573
  63.2 3.3 %collective-permute-start.14 = (bf16[4,160,640]{2,1,0:T(8,128)(2,1)S(1)}, bf16[4,160,640]{2,1,0:T(8,128)(2,1)}, u32[]{:S(2)}, u32[]{:S(2)}) collective-permute-start(bf16[4,160,640]{2,1,0:T(8,128)(2,1)S(1)} %collective-permute-done.8.p1), channel_id=1, source_target_pairs={{0,1},{1,0},{2,3},{3,2},{4,5},{5,4},{6,7},{7,6},{8,9},{9,8},{10,11... | collective-permute-start | bytes 2457608 | tf_op jit(solution)/shard_map/ppermute | solution.py:573
  63.3 4.3 %collective-permute-start.15 = (bf16[4,160,640]{2,1,0:T(8,128)(2,1)S(1)}, bf16[4,160,640]{2,1,0:T(8,128)(2,1)}, u32[]{:S(2)}, u32[]{:S(2)}) collective-permute-start(bf16[4,160,640]{2,1,0:T(8,128)(2,1)S(1)} %collective-permute-done.9.p2), channel_id=1, source_target_pairs={{0,1},{1,0},{2,3},{3,2},{4,5},{5,4},{6,7},{7,6},{8,9},{9,8},{10,11... | collective-permute-start | bytes 2457608 | tf_op jit(solution)/shard_map/ppermute | solution.py:573
  65.6 2.0 %copy-start.4 = (bf16[4,160,640]{2,1,0:T(8,128)(2,1)}, bf16[4,160,640]{2,1,0:T(8,128)(2,1)S(1)}, u32[]{:S(2)}) copy-start(bf16[4,160,640]{2,1,0:T(8,128)(2,1)S(1)} %collective-permute-done.13.q0) | copy-start | bytes 2457604
  112.3 18.2 %collective-permute-start.17 = (f32[80,1280]{1,0:T(8,128)}, f32[80,1280]{1,0:T(8,128)S(1)}, u32[]{:S(2)}, u32[]{:S(2)}) collective-permute-start(f32[80,1280]{1,0:T(8,128)} %get-tuple-element.54), channel_id=1, source_target_pairs={{0,1},{1,0},{2,3},{3,2},{4,5},{5,4},{6,7},{7,6},{8,9},{9,8},{10,11... | collective-permute-start | bytes 1228808 | tf_op jit(solution)/shard_map/ppermute | solution.py:573
  113.1 17.4 %copy-start = (f32[80,1280]{1,0:T(8,128)S(1)}, f32[80,1280]{1,0:T(8,128)}, u32[]{:S(2)}) copy-start(f32[80,1280]{1,0:T(8,128)} %get-tuple-element.53) | copy-start | bytes 1228804
  127.9 1.6 %collective-permute-start.16 = (f32[40,960]{1,0:T(8,128)}, f32[40,960]{1,0:T(8,128)S(1)}, u32[]{:S(2)}, u32[]{:S(2)}) collective-permute-start(f32[40,960]{1,0:T(8,128)} %get-tuple-element.52), channel_id=1, source_target_pairs={{0,1},{1,0},{2,3},{3,2},{4,5},{5,4},{6,7},{7,6},{8,9},{9,8},{10,11... | collective-permute-start | bytes 460808 | tf_op jit(solution)/shard_map/ppermute | solution.py:573
